TPU v7x, 32 devices: a whole 2x2x4 slice. The times are simulated.
32 devices in a mesh: row: 8 (over z, x), col: 4 (over y, core).
Axes of the slice: x: 2, y: 2, z: 4, core: 2. Of those that a mesh axis runs over, the one named last changes fastest.
Arguments:
- inputs: bfloat16 [768, 8192], P(None, 'row'), may hold values from -6 to 6
- out_grad: bfloat16 [768, 8192], P(None, 'col'), may hold values from -6 to 6
- gate_weight: bfloat16 [8192, 14336], P('row', 'col'), may hold values from -0.09375 to 0.09375
- up_weight: bfloat16 [8192, 14336], P('row', 'col'), may hold values from -0.09375 to 0.09375
- down_weight: bfloat16 [14336, 8192], P('row', 'col'), may hold values from -0.0625 to 0.0625
- gate_mask: int32 [64, 112], P('row', 'col'), may hold values 0 or 1
- up_mask: int32 [64, 112], P('row', 'col'), may hold values 0 or 1
- down_mask: int32 [112, 64], P('row', 'col'), may hold values 0 or 1
Outputs:
- input_grad: bfloat16 [768, 8192], P(None, 'row')
- gate_grad: bfloat16 [8192, 14336], P('row', 'col')
- up_grad: bfloat16 [8192, 14336], P('row', 'col')
- down_grad: bfloat16 [14336, 8192], P('row', 'col')
All inputs are finite; a program needn't handle non-finite values. No bound on the sum of `gate_mask` or of `up_mask` or of `down_mask` on one device may be relied on, other than what follows from the above.
Results may differ from a plain program's by a relative error of at most 0.0068.
Values may be sent and summed in bfloat16 or wider, within the bound.
No kernel may reach another device: no remote copies, remote signals or barrier semaphores. Data moves between devices by JAX's collectives and lax.ppermute only.
A program may use at most 256 MiB of HBM per device.

v0:
```python
import jax
import jax.numpy as jnp
from jax import lax
from jax.sharding import PartitionSpec as P

BLOCK = 128


def spread(block, axis, source):
    block = jnp.where(lax.axis_index(axis) == source, block, jnp.zeros_like(block))
    return lax.psum(block, axis)


def expand(mask):
    return jnp.repeat(jnp.repeat(mask, BLOCK, axis=0), BLOCK, axis=1).astype(jnp.bfloat16)


def contract_first(left, right):
    return lax.dot_general(
        left, right, (((0,), (0,)), ((), ())), preferred_element_type=jnp.float32
    )


def contract_last(left, right):
    return lax.dot_general(
        left, right, (((1,), (1,)), ((), ())), preferred_element_type=jnp.float32
    )


def on_device(inputs, out_grad, gate_weight, up_weight, down_weight, gate_mask, up_mask, down_mask):
    gate_keep = expand(gate_mask)
    up_keep = expand(up_mask)
    down_keep = expand(down_mask)
    gate_eff = gate_weight * gate_keep
    up_eff = up_weight * up_keep
    down_eff = down_weight * down_keep
    width = gate_weight.shape[1]
    joined = jnp.concatenate([gate_eff, up_eff], axis=1)
    share = lax.psum_scatter(
        jnp.dot(inputs, joined, preferred_element_type=jnp.float32),
        "row",
        scatter_dimension=0,
        tiled=True,
    )
    both = lax.all_gather(share.astype(jnp.bfloat16), "row", axis=0, tiled=True)
    gate_f = both[:, :width].astype(jnp.float32)
    up_f = both[:, width:].astype(jnp.float32)
    sig = jax.nn.sigmoid(gate_f)
    hidden = (gate_f * sig * up_f).astype(jnp.bfloat16)
    half = down_weight.shape[0]
    row_index = lax.axis_index("row")
    col_index = lax.axis_index("col")
    offset = row_index % 2 * half
    own_part = lax.dynamic_slice_in_dim(hidden, offset, half, 1)
    hidden_rows = spread(own_part, "col", row_index // 2)
    partial_value = contract_last(out_grad, down_eff)
    hidden_grad = lax.psum(partial_value, "col")
    down_grad = (contract_first(hidden_rows, out_grad) * down_keep.astype(jnp.float32)).astype(
        jnp.bfloat16
    )
    pieces = []
    for which in range(2):
        pieces.append(spread(hidden_grad, "row", 2 * col_index + which))
    grad_cols = jnp.concatenate(pieces, axis=1)
    gate_delta = (grad_cols * up_f * sig * (1.0 + gate_f * (1.0 - sig))).astype(jnp.bfloat16)
    up_delta = (grad_cols * gate_f * sig).astype(jnp.bfloat16)
    gate_grad = (contract_first(inputs, gate_delta) * gate_keep.astype(jnp.float32)).astype(
        jnp.bfloat16
    )
    up_grad = (contract_first(inputs, up_delta) * up_keep.astype(jnp.float32)).astype(jnp.bfloat16)
    deltas = jnp.concatenate([gate_delta, up_delta], axis=1)
    local_grad = contract_last(deltas, joined)
    input_grad = lax.psum(local_grad, "col").astype(jnp.bfloat16)
    return (input_grad, gate_grad, up_grad, down_grad)


def solution(mesh):
    placed = (
        P(None, "row"),
        P(None, "col"),
        P("row", "col"),
        P("row", "col"),
        P("row", "col"),
        P("row", "col"),
        P("row", "col"),
        P("row", "col"),
    )
    return jax.shard_map(
        on_device,
        mesh=mesh,
        in_specs=placed,
        out_specs=(P(None, "row"), P("row", "col"), P("row", "col"), P("row", "col")),
        check_vma=False,
    )
```

profile of v0, /device:TPU:9, one launch (start us, length us, event | category | flops | bytes accessed | tf_op | source)
XLA Modules:
  0.0 1214.9 jit_solution(13989796834139604809)
XLA Ops:
  8.1 0.9 convert_element_type.72
  9.0 11.2 broadcast_in_dim.22
  20.2 3.0 copy-done.3
  23.2 7.9 fusion.9
  31.9 10.3 copy.28
  42.2 10.4 copy.30
  52.7 8.7 bitcast_multiply_fusion.2
  61.4 3.0 copy-done.2
  64.4 22.7 %convolution_bitcast_fusion = f32[768,7168]{0,1:T(8,128)} fusion(bf16[768,1024]{1,0:T(8,128)(2,1)S(1)} %copy-done.7, bf16[1024,3584]{0,1:T(8,128)(2,1)S(1)} %get-tuple-element.25, bf16[1024,3584]{0,1:T(8,128)(2,1)} %get-tuple-element.26), kind=kOutput, calls=%fused_computation.6 | convolution fusion | flops 11303649280 | bytes 38273024 | tf_op jit(solution)/shard_map/dot_general | solution.py:40
  87.1 22.1 %copy.36 = f32[768,7168]{1,0:T(8,128)} copy(f32[768,7168]{0,1:T(8,128)} %convolution_bitcast_fusion) | data formatting | bytes 44040192
  109.3 29.8 %all-reduce.6.cloned.1.call-done = f32[768,1792]{0,1:T(8,128)} async-done(((f32[768,1792]{0,1:T(8,128)}), f32[768,1792]{0,1:T(8,128)}) %all-reduce.6.cloned.1.call-update) | async-done | bytes 5505040 | tf_op jit(solution)/shard_map/psum | solution.py:57
  139.1 7.6 broadcast_select_fusion
  146.8 319.5 %reduce-scatter.4.cloned.1.call-done = f32[96,7168]{1,0:T(8,128)} async-done(((f32[768,7168]{1,0:T(8,128)}), f32[96,7168]{1,0:T(8,128)}) %reduce-scatter.4.cloned.1.call-update) | async-done | bytes 2752528 | tf_op jit(solution)/shard_map/reduce_scatter | solution.py:39
  466.3 3.0 convert_element_type.81
  469.6 341.6 %all-reduce.10.cloned.1.call-done = (f32[768,1792]{0,1:T(8,128)}, f32[768,1792]{0,1:T(8,128)}) async-done(((f32[768,1792]{0,1:T(8,128)}, f32[768,1792]{0,1:T(8,128)}), (f32[768,1792]{0,1:T(8,128)}, f32[768,1792]{0,1:T(8,128)})) %all-reduce.10.cloned.1.call-update) | async-done | bytes 11010064 | tf_op jit(solution)/shard_map/psum | solution.py:11
  811.2 5.5 constant_dynamic-update-slice_fusion.1
  816.7 2.8 constant_dynamic-update-slice_fusion
  819.5 150.2 %all-gather.2.cloned.1.call-done = bf16[768,7168]{1,0:T(8,128)(2,1)} async-done(((bf16[96,7168]{1,0:T(8,128)(2,1)}), bf16[768,7168]{1,0:T(8,128)(2,1)}) %all-gather.2.cloned.1.call-update) | async-done | bytes 11010064 | tf_op jit(solution)/shard_map/all_gather | solution.py:45
  969.7 9.1 fusion.13
  978.8 8.3 copy.38
  987.1 8.3 copy.39
  995.3 8.2 convert_element_type.83
  1003.6 4.9 convert_element_type.82
  1008.5 15.1 %multiply_convert_fusion.2 = (bf16[768,3584]{0,1:T(8,128)(2,1)}, bf16[768,3584]{0,1:T(8,128)(2,1)}, f32[768,3584]{0,1:T(8,128)}) fusion(f32[768,3584]{0,1:T(8,128)} %constant_dynamic-update-slice_fusion, bf16[768,3584]{0,1:T(8,128)(2,1)S(1)} %bitcast.48, bf16[768,3584]{0,1:T(8,128)(2,1)S(1)} %copy-done.1), kind=kLoop, calls=%fused_computation.14 | loop fusion | flops 41287680 | bytes 44040192 | tf_op jit(solution)/shard_map/convert_element_type | solution.py:65
  1023.6 19.4 %fusion.2 = f32[768,1024]{1,0:T(8,128)} fusion(bf16[768,3584]{0,1:T(8,128)(2,1)} %get-tuple-element.19, bf16[768,3584]{0,1:T(8,128)(2,1)} %get-tuple-element.18, bf16[1024,3584]{0,1:T(8,128)(2,1)} %copy-done.2, bf16[1024,3584]{0,1:T(8,128)(2,1)} %get-tuple-element.26), kind=kOutput, calls=%fused_computation.7 | convolution fusion | flops 11325669376 | bytes 28835840 | tf_op jit(solution)/shard_map/dot_general | solution.py:25
  1043.0 8.4 fusion.10
  1051.4 102.3 %all-reduce.11 = bf16[768,1024]{1,0:T(8,128)(2,1)} all-reduce(f32[768,1024]{1,0:T(8,128)} %fusion.2), channel_id=1, replica_groups=mesh['row'=8,'col'=4] {'col'}, use_global_device_ids=true, to_apply=%region_4.5 | all-reduce | flops 786432 | bytes 4718592 | tf_op jit(solution)/shard_map/psum | solution.py:73
  1153.7 10.8 fusion.1
  1164.5 10.6 fusion
  1175.1 9.9 copy.34
  1185.0 9.9 copy.35
  1194.9 11.9 multiply_convert_fusion
  (48 shorter events, 1.2 us)
Async XLA Ops:
  8.0 15.2 %copy-start = (bf16[768,2048]{1,0:T(8,128)(2,1)S(1)}, bf16[768,2048]{1,0:T(8,128)(2,1)}, u32[]{:S(2)}) copy-start(bf16[768,2048]{1,0:T(8,128)(2,1)} %param.9) | copy-start | bytes 9437188
  8.0 131.1 %all-reduce.6.cloned.1.call-start = ((), (), s32[]{:S(2)}) async-start(), calls=%async_computation.1 | async-start | bytes 11010048 | tf_op jit(solution)/shard_map/psum | solution.py:57
  8.1 15.1 %copy-start.6 = (bf16[1792,2048]{1,0:T(8,128)(2,1)S(1)}, bf16[1792,2048]{1,0:T(8,128)(2,1)}, u32[]{:S(2)}) copy-start(bf16[1792,2048]{1,0:T(8,128)(2,1)} %param.12) | copy-start | bytes 22020100
  20.2 3.0 copy-start.3
  23.2 8.2 copy-start.4
  23.2 8.2 copy-start.5
  31.2 435.1 %reduce-scatter.4.cloned.1.call-start = ((), (), s32[]{:S(2)}) async-start(), calls=%async_computation.4 | async-start | bytes 24772608 | tf_op jit(solution)/shard_map/reduce_scatter | solution.py:39
  52.6 11.8 copy-start.7
  61.4 3.0 copy-start.2
  109.2 702.0 %all-reduce.10.cloned.1.call-start = ((), (), s32[]{:S(2)}) async-start(), calls=%async_computation.5 | async-start | bytes 22020096 | tf_op jit(solution)/shard_map/psum | solution.py:11
  146.7 823.0 %all-gather.2.cloned.1.call-start = ((), (), s32[]{:S(2)}) async-start(), calls=%async_computation.2 | async-start | bytes 12386304 | tf_op jit(solution)/shard_map/all_gather | solution.py:45
  469.3 725.6 %all-reduce.8.cloned.1.call-start = ((), (), s32[]{:S(2)}) async-start(), calls=%async_computation.3 | async-start | bytes 5505024 | tf_op jit(solution)/shard_map/psum | solution.py:11
  811.2 5.5 slice-start.2
  811.2 5.5 slice-start.3
  995.3 8.3 copy-start.1
  995.3 13.1 %slice-start = ((s8[5505024]{0:T(1024)(128)(4,1)}), s8[4194304]{0:T(1024)(128)(4,1)S(1)}, s32[]{:S(2)}) async-start(s8[5505024]{0:T(1024)(128)(4,1)} %bitcast.47), calls=%async_computation.6 | async-start | bytes 8388608
  1003.6 4.9 slice-start.1
  1153.7 10.8 copy-start.8
Sparse Core Ops, SparseCore 0:
  31.3 107.7 all-reduce.5
  1051.6 103.4 all-reduce.7
Sparse Core Ops, SparseCore 1:
  109.3 356.9 reduce-scatter.3
  471.3 339.9 all-reduce.9
  814.1 155.6 all-gather.1
where the time goes:
time: 1220 us; the launch traced here: 1210 us
  waiting for transfers between devices  841 us (69%)
  local copies, waits for them, and re-layouts  114 us (9%)
  blocking collectives  102 us (8%)
  matrix products  83.4 us (7%)
  other arithmetic  56.8 us (5%)
  between operations  16.3 us (1%)
    psum x2, waiting for transfers between devices, spread(): return lax.psum(block, axis)  342 us
    reduce_scatter x1, waiting for transfers between devices, on_device(): lax.psum_scatter(jnp.dot(inputs, joined, preferred_element_type=jnp.float...  320 us
    all_gather x1, waiting for transfers between devices, on_device(): both = lax.all_gather(share.astype(jnp.bfloat16), 'row', axis=0, tiled=True)  150 us
    psum x1, blocking collectives, on_device(): input_grad = lax.psum(local_grad, 'col').astype(jnp.bfloat16)  102 us
    unnamed x40, local copies, waits for them, and re-layouts  91.1 us
    dot_general x3, matrix products, contract_first(): lax.dot_general(left, right, (((0,), (0,)), ((), ())), preferred_element_...  33.3 us
    psum x1, waiting for transfers between devices, on_device(): hidden_grad = lax.psum(partial_value, 'col')  29.8 us
    dot_general x2, matrix products, contract_last(): lax.dot_general(left, right, (((1,), (1,)), ((), ())), preferred_element_...  27.4 us
  transfers between devices with their start and end apart: 5, of which 4 were waited for; matrix products, arithmetic and copies ran while one was open for 11% of the time, Pallas kernels for 0%

commit v1 on v0

v1 whole, which is shorter than its diff:
```python
import functools

import jax
import jax.numpy as jnp
from jax import lax
from jax.experimental import pallas as pl
from jax.experimental.pallas import tpu as pltpu
from jax.sharding import PartitionSpec as P

BLOCK = 128
ROWS = 16
BF16 = jnp.bfloat16
F32 = jnp.float32


def params(**more):
    return pltpu.CompilerParams(vmem_limit_bytes=50 * 1024 * 1024, **more)


def cost(flops, bytes_accessed):
    return pl.CostEstimate(flops=int(flops), bytes_accessed=int(bytes_accessed), transcendentals=0)


def widen(mask):
    return jnp.repeat(jnp.repeat(mask.astype(BF16), BLOCK, axis=1), ROWS, axis=0)


def masked(value, wide):
    rows, columns = value.shape
    blocks = rows // BLOCK
    spread = jnp.broadcast_to(
        wide.reshape(blocks, 1, ROWS, columns), (blocks, BLOCK // ROWS, ROWS, columns)
    )
    return value * spread.reshape(rows, columns)


def dot_nt(left, right):
    return lax.dot_general(left, right, (((1,), (1,)), ((), ())), preferred_element_type=F32)


def tile_of(size, most):
    best = BLOCK
    for tile in range(BLOCK, most + 1, BLOCK):
        if size % tile == 0:
            best = tile
    return best


def piece_kernel(at, x_ref, w_ref, m_ref, *rest):
    *came, out_ref, total_ref = rest
    term = jnp.dot(x_ref[...], masked(w_ref[...], m_ref[...]), preferred_element_type=F32)

    @pl.when(pl.program_id(0) == 0)
    def _():
        start = term
        for ref in came:
            start = start + ref[...].astype(F32)
        total_ref[...] = start

    @pl.when(pl.program_id(0) > 0)
    def _():
        total_ref[...] += term

    @pl.when(pl.program_id(0) == pl.num_programs(0) - 1)
    def _():
        out_ref[...] = total_ref[...].astype(out_ref.dtype)


def piece(at, inputs, weight, wide, came, tokens, columns, kind):
    depth = inputs.shape[1]
    tile = tile_of(depth, 256)
    whole = pl.BlockSpec((tokens, columns), lambda k, at: (0, 0))
    return pl.pallas_call(
        piece_kernel,
        out_shape=jax.ShapeDtypeStruct((tokens, columns), kind),
        grid_spec=pltpu.PrefetchScalarGridSpec(
            num_scalar_prefetch=1,
            grid=(depth // tile,),
            in_specs=[
                pl.BlockSpec((tokens, tile), lambda k, at: (at[0], k)),
                pl.BlockSpec((tile, columns), lambda k, at: (k, at[1])),
                pl.BlockSpec((tile // BLOCK * ROWS, columns), lambda k, at: (k, at[1])),
            ]
            + [whole] * len(came),
            out_specs=whole,
            scratch_shapes=[pltpu.VMEM((tokens, columns), F32)],
        ),
        compiler_params=params(),
        cost_estimate=cost(2 * tokens * depth * columns, 2 * depth * columns + 6 * tokens * columns),
    )(at, inputs, weight, wide, *came)


def hidden_grad_kernel(g_ref, w_ref, m_ref, out_ref):
    weight = masked(w_ref[...], m_ref[...])
    parts, tokens, _ = out_ref.shape
    first = pl.program_id(1) == 0
    for t in range(parts):
        term = dot_nt(g_ref[t * tokens : (t + 1) * tokens, :], weight)

        @pl.when(first)
        def _():
            out_ref[t] = term

        @pl.when(jnp.logical_not(first))
        def _():
            out_ref[t] += term


def hidden_grad_partial(out_grad, weight, wide, parts, columns):
    count, depth = out_grad.shape
    cuts = weight.shape[0] // columns
    tokens = count // parts
    tile = tile_of(depth, 512)
    return pl.pallas_call(
        hidden_grad_kernel,
        out_shape=jax.ShapeDtypeStruct((cuts * parts, tokens, columns), F32),
        grid=(cuts, depth // tile),
        in_specs=[
            pl.BlockSpec((count, tile), lambda i, k: (0, k)),
            pl.BlockSpec((columns, tile), lambda i, k: (i, k)),
            pl.BlockSpec((columns // BLOCK * ROWS, tile), lambda i, k: (i, k)),
        ],
        out_specs=pl.BlockSpec((parts, tokens, columns), lambda i, k: (i, 0, 0)),
        compiler_params=params(),
        cost_estimate=cost(2 * count * depth * weight.shape[0], 2 * weight.size + 2 * out_grad.size + 4 * count * weight.shape[0]),
    )(out_grad, weight, wide)


def input_grad_kernel(at, sum_ref, gd_ref, ud_ref, gw_ref, uw_ref, gm_ref, um_ref, out_ref):
    term = dot_nt(gd_ref[...], masked(gw_ref[...], gm_ref[...]))
    term = term + dot_nt(ud_ref[...], masked(uw_ref[...], um_ref[...]))
    out_ref[0] = sum_ref[0] + term


def add_input_grad(at, total, gate_delta, up_delta, gate_weight, up_weight, gate_wide, up_wide):
    tokens, columns = gate_delta.shape
    depth = gate_weight.shape[0]
    tile = tile_of(depth, 256)
    delta = pl.BlockSpec((tokens, columns), lambda n, at: (0, 0))
    weight = pl.BlockSpec((tile, columns), lambda n, at: (n, at[1]))
    wide = pl.BlockSpec((tile // BLOCK * ROWS, columns), lambda n, at: (n, at[1]))
    sums = pl.BlockSpec((1, tokens, tile), lambda n, at: (at[0], 0, n))
    return pl.pallas_call(
        input_grad_kernel,
        out_shape=jax.ShapeDtypeStruct(total.shape, F32),
        grid_spec=pltpu.PrefetchScalarGridSpec(
            num_scalar_prefetch=1,
            grid=(depth // tile,),
            in_specs=[sums, delta, delta, weight, weight, wide, wide],
            out_specs=sums,
        ),
        input_output_aliases={1: 0},
        compiler_params=params(),
        cost_estimate=cost(4 * tokens * depth * columns, 4 * depth * columns + 8 * tokens * depth),
    )(at, total, gate_delta, up_delta, gate_weight, up_weight, gate_wide, up_wide)


def weight_grads_kernel(parts, at, *refs):
    lefts, gates, ups = refs[:parts], refs[parts : 2 * parts], refs[2 * parts : 3 * parts]
    gm_ref, um_ref, gate_ref, up_ref = refs[3 * parts], refs[3 * parts + 1], refs[-2], refs[-1]
    for deltas, m_ref, out_ref in ((gates, gm_ref, gate_ref), (ups, um_ref, up_ref)):
        total = None
        for left, delta in zip(lefts, deltas):
            term = jnp.dot(left[0], delta[...], preferred_element_type=F32)
            total = term if total is None else total + term
        out_ref[...] = masked(total.astype(BF16), m_ref[...])


def weight_grads(at, inputs_t, gates, ups, gate_wide, up_wide, width, before):
    _, depth, tokens = inputs_t.shape
    parts, columns = len(gates), gates[0].shape[1]
    tile = tile_of(depth, 256)
    lefts = [
        pl.BlockSpec((1, tile, tokens), lambda m, at, i=i: (at[1 + i], m, 0)) for i in range(parts)
    ]
    delta = pl.BlockSpec((tokens, columns), lambda m, at: (0, 0))
    wide = pl.BlockSpec((tile // BLOCK * ROWS, columns), lambda m, at: (m, at[0]))
    out = pl.BlockSpec((tile, columns), lambda m, at: (m, at[0]))
    shape = jax.ShapeDtypeStruct((depth, width), BF16)
    operands = [inputs_t] * parts + gates + ups + [gate_wide, up_wide]
    specs = lefts + [delta] * (2 * parts) + [wide, wide]
    aliases = {}
    if before is not None:
        aliases = {1 + len(operands): 0, 2 + len(operands): 1}
        operands = operands + list(before)
        specs = specs + [pl.BlockSpec(memory_space=pl.ANY)] * 2
    return pl.pallas_call(
        functools.partial(weight_grads_kernel, parts),
        out_shape=(shape, shape),
        grid_spec=pltpu.PrefetchScalarGridSpec(
            num_scalar_prefetch=1,
            grid=(depth // tile,),
            in_specs=specs,
            out_specs=(out, out),
        ),
        input_output_aliases=aliases,
        compiler_params=params(),
        cost_estimate=cost(4 * parts * tokens * depth * columns, 4 * depth * columns + 4 * parts * tokens * columns),
    )(at, *operands)


def down_grad_kernel(h_ref, g_ref, m_ref, out_ref):
    parts, _, tokens = h_ref.shape
    total = None
    for t in range(parts):
        term = jnp.dot(h_ref[t], g_ref[t * tokens : (t + 1) * tokens, :], preferred_element_type=F32)
        total = term if total is None else total + term
    out_ref[...] = masked(total.astype(BF16), m_ref[...])


def down_grad_of(hidden_t, out_grad, wide, parts):
    pieces, columns, tokens = hidden_t.shape
    cuts = pieces // parts
    count, width = out_grad.shape
    tile = tile_of(width, 512)
    return pl.pallas_call(
        down_grad_kernel,
        out_shape=jax.ShapeDtypeStruct((cuts * columns, width), BF16),
        grid=(cuts, width // tile),
        in_specs=[
            pl.BlockSpec((parts, columns, tokens), lambda i, j: (i, 0, 0)),
            pl.BlockSpec((count, tile), lambda i, j: (0, j)),
            pl.BlockSpec((columns // BLOCK * ROWS, tile), lambda i, j: (i, j)),
        ],
        out_specs=pl.BlockSpec((columns, tile), lambda i, j: (i, j)),
        compiler_params=params(),
        cost_estimate=cost(2 * count * cuts * columns * width, 2 * cuts * columns * width + 2 * out_grad.size),
    )(hidden_t, out_grad, wide)


def on_device(rows, cols, inputs, out_grad, gate_weight, up_weight, down_weight, gate_mask, up_mask, down_mask):
    count, depth = inputs.shape
    width = gate_weight.shape[1]
    ratio = rows // cols

    lines = rows // 4 if rows % 4 == 0 else 1
    length = rows // lines
    ring = []
    for line in range(lines):
        steps = range(length) if line % 2 == 0 else range(length - 1, -1, -1)
        ring += [step * lines + line for step in steps]
    place = [ring.index(r) for r in range(rows)]
    ahead = [(ring[p], ring[(p + 1) % rows]) for p in range(rows)]
    back = [(b, a) for a, b in ahead]
    me = jnp.array(place, jnp.int32)[lax.axis_index("row")]

    cuts = max(
        q for q in range(ratio, rows // 2 + 1, ratio) if rows % q == 0 and width // BLOCK % q == 0
    )
    parts = rows // cuts
    tokens, columns = count // parts, width // cuts
    far, near = rows // 2, rows - 1 - rows // 2

    def where_is(shard):
        shard = lax.rem(shard + 2 * rows, rows)
        return jnp.stack([shard // cuts, lax.rem(shard, cuts)])

    meet = []
    for r in range(rows):
        for c in range(cols):
            shard = (c % parts) * cuts + r % ratio * (cuts // ratio) + c // parts
            meet.append((r * cols + c, ring[shard] * cols + r // ratio))
    meet_back = [(b, a) for a, b in meet]

    gate_wide, up_wide, down_wide = widen(gate_mask), widen(up_mask), widen(down_mask)
    gate_set, up_set = (gate_weight, gate_wide), (up_weight, up_wide)

    def part(which, shard, came, kind=BF16):
        return piece(where_is(shard), inputs, *which, came, tokens, columns, kind)

    def onward(value):
        return lax.ppermute(value, "row", ahead)

    def backward(value):
        return lax.ppermute(value, "row", back)

    gate_on, up_back = part(gate_set, me + far, []), part(up_set, me - far, [])
    up_on, gate_back = part(up_set, me + near, []), part(gate_set, me - near, [])
    out_grad, gate_on, up_back, up_on, gate_back = lax.optimization_barrier(
        (out_grad, gate_on, up_back, up_on, gate_back)
    )
    hidden_grad = hidden_grad_partial(out_grad, down_weight, down_wide, parts, columns)
    hidden_grad = lax.psum_scatter(hidden_grad, "col", scatter_dimension=0, tiled=False)
    hidden_grad = lax.ppermute(hidden_grad.astype(BF16), ("row", "col"), meet)
    for step in range(1, far + 1):
        gate_on, up_back = onward(gate_on), backward(up_back)
        if step <= near:
            up_on, gate_back = onward(up_on), backward(gate_back)
        if step < far:
            gate_on = part(gate_set, me + far - step, [gate_on])
            up_back = part(up_set, me - far + step, [up_back])
        if step < near:
            up_on = part(up_set, me + near - step, [up_on])
            gate_back = part(gate_set, me - near + step, [gate_back])
        if step == near:
            gate_on, hidden_grad = lax.optimization_barrier((gate_on, hidden_grad))
    gate = part(gate_set, me, [gate_back, gate_on], F32)
    up = part(up_set, me, [up_on, up_back], F32)

    hidden_grad = hidden_grad.astype(F32)
    sig = jax.nn.sigmoid(gate)
    hidden = (gate * sig * up).astype(BF16)
    gate_delta = (hidden_grad * up * sig * (1.0 + gate * (1.0 - sig))).astype(BF16)
    up_delta = (hidden_grad * gate * sig).astype(BF16)

    hidden_t = lax.ppermute(hidden.T, ("row", "col"), meet_back)
    hidden_t = lax.all_gather(hidden_t, "col", axis=0, tiled=False)
    down_grad = down_grad_of(hidden_t, out_grad, down_wide, parts)

    gates, ups = {0: gate_delta}, {0: up_delta}
    gate_on = gate_back = gate_delta
    up_on = up_back = up_delta
    total = jnp.zeros((parts, tokens, depth), F32)
    inputs_t = jnp.swapaxes(inputs.reshape(parts, tokens, depth), 1, 2)

    def add(total, offset):
        return add_input_grad(
            where_is(me + offset), total, gates[offset % rows], ups[offset % rows],
            gate_weight, up_weight, gate_wide, up_wide,
        )

    total = add(total, 0)
    grads = None
    done = set()

    def column_cuts(grads):
        for j in range(cuts):
            offsets = [(j + cuts * i) % rows for i in range(parts)]
            if j not in done and all(o in gates and o in ups for o in offsets):
                done.add(j)
                at = jnp.stack([where_is(me + j)[1]] + [where_is(me + o)[0] for o in offsets])
                grads = weight_grads(
                    at, inputs_t, [gates[o] for o in offsets], [ups[o] for o in offsets],
                    gate_wide, up_wide, width, grads,
                )
        return grads

    for step in range(1, far + 1):
        gate_on, up_back = onward(gate_on), backward(up_back)
        gates[-step % rows], ups[step % rows] = gate_on, up_back
        if step <= near:
            up_on, gate_back = onward(up_on), backward(gate_back)
            ups[-step % rows], gates[step % rows] = up_on, gate_back
            total = add(total, -step)
            total = add(total, step)
            grads = column_cuts(grads)

    late = where_is(me - far)[0]
    others = [lax.rem(late + 1 + i, parts) for i in range(parts - 1)]
    early = [lax.dynamic_index_in_dim(total, o, 0, keepdims=False) for o in others]
    early = [sum_over_col(value, cols) for value in early]
    total = add(total, -far)
    grads = column_cuts(grads)
    last = sum_over_col(lax.dynamic_index_in_dim(total, late, 0, keepdims=False), cols)
    input_grad = jnp.zeros((parts, tokens, depth), BF16)
    for place_of, value in zip(others + [late], early + [last]):
        input_grad = lax.dynamic_update_index_in_dim(input_grad, value, place_of, 0)
    return (input_grad.reshape(count, depth), *grads, down_grad)


def sum_over_col(value, cols):
    half = value.shape[0] // 2
    mine = lax.axis_index("col") % 2

    def across(array, bit):
        return lax.ppermute(array, "col", [(c, c ^ bit) for c in range(cols)])

    other = lax.dynamic_slice_in_dim(value, (1 - mine) * half, half, 0)
    total = lax.dynamic_slice_in_dim(value, mine * half, half, 0) + across(other, 1)
    bit = 2
    while bit < cols:
        rounded = total.astype(BF16)
        total = rounded.astype(F32) + across(rounded, bit).astype(F32)
        bit *= 2
    own = total.astype(BF16)
    theirs = across(own, 1)
    first = mine == 0
    return jnp.concatenate([jnp.where(first, own, theirs), jnp.where(first, theirs, own)], axis=0)


def solution(mesh):
    placed = (P(None, "row"), P(None, "col")) + (P("row", "col"),) * 6
    return jax.shard_map(
        functools.partial(on_device, mesh.shape["row"], mesh.shape["col"]),
        mesh=mesh,
        in_specs=placed,
        out_specs=(P(None, "row"), P("row", "col"), P("row", "col"), P("row", "col")),
        check_vma=False,
    )
```

time: 1220 us -> 434 us (0.36)
  waiting for transfers between devices: 841 us -> 76.9 us
  Pallas kernels: 0 us -> 192 us
  blocking collectives: 102 us -> 0 us
  starting transfers between devices: 0.6 us -> 100 us
  local copies, waits for them, and re-layouts: 114 us -> 22.3 us
  matrix products: 83.4 us -> 0 us
  other arithmetic: 56.8 us -> 12.5 us
    psum x3 -> x0, waiting for transfers between devices: 371 us -> none  [the longest x2 342 us: spread(): return lax.psum(block, axis)]
    reduce_scatter x1, waiting for transfers between devices: 320 us -> 0.01 us  [on_device(): lax.psum_scatter(hidden_grad, 'col', scatter_dimension=0, tiled=False)]
    pallas_call x0 -> x30, Pallas kernels: none -> 192 us  [the longest x16 81.9 us: piece(): pl.pallas_call(piece_kernel, out_shape=jax.ShapeDtypeStruct((tokens, colu...]
    all_gather x1, waiting for transfers between devices: 150 us -> 0.01 us  [on_device(): hidden_t = lax.all_gather(hidden_t, 'col', axis=0, tiled=False)]
    psum x1 -> x0, blocking collectives: 102 us -> none  [on_device(): input_grad = lax.psum(local_grad, 'col').astype(jnp.bfloat16)]
    ppermute x0 -> x36, starting transfers between devices: none -> 100 us  [the longest x14 71.9 us: onward(): return lax.ppermute(value, 'row', ahead)]
    dot_general x6 -> x0, matrix products: 83.4 us -> none  [the longest x3 33.3 us: contract_first(): lax.dot_general(left, right, (((0,), (0,)), ((), ())), preferred_element_...]
    unnamed x40 -> x46, local copies, waits for them, and re-layouts: 91.1 us -> 8.57 us
  transfers between devices with their start and end apart: 5 -> 38, of which waited for: 4 -> 14; matrix products, arithmetic and copies ran while one was open for 11% -> 4% of each run, Pallas kernels for 0% -> 33%
where the time goes in v1:
time: 434 us; the launch traced here: 426 us
  Pallas kernels  192 us (44%)
  starting transfers between devices  100 us (23%)
  waiting for transfers between devices  76.9 us (18%)
  local copies, waits for them, and re-layouts  22.3 us (5%)
  between operations  21.6 us (5%)
  other arithmetic  12.5 us (3%)
    pallas_call x16, Pallas kernels, piece(): pl.pallas_call(piece_kernel, out_shape=jax.ShapeDtypeStruct((tokens, colu...  81.9 us
    ppermute x14, starting transfers between devices, onward(): return lax.ppermute(value, 'row', ahead)  71.9 us
    pallas_call x8, Pallas kernels, add_input_grad(): pl.pallas_call(input_grad_kernel, out_shape=jax.ShapeDtypeStruct(total.sh...  50.5 us
    ppermute x14, waiting for transfers between devices, backward(): return lax.ppermute(value, 'row', back)  49.1 us
    pallas_call x4, Pallas kernels, weight_grads(): pl.pallas_call(functools.partial(weight_grads_kernel, parts), out_shape=(...  32.1 us
    ppermute x14, waiting for transfers between devices, onward(): return lax.ppermute(value, 'row', ahead)  24.3 us
    pallas_call x1, Pallas kernels, hidden_grad_partial(): pl.pallas_call(hidden_grad_kernel, out_shape=jax.ShapeDtypeStruct((cuts *...  15.4 us
    pallas_call x1, Pallas kernels, down_grad_of(): pl.pallas_call(down_grad_kernel, out_shape=jax.ShapeDtypeStruct((cuts * c...  12.3 us
  transfers between devices with their start and end apart: 38, of which 14 were waited for; matrix products, arithmetic and copies ran while one was open for 4% of the time, Pallas kernels for 33%

profile of v1, /device:TPU:9, one launch (start us, length us, event | category | flops | bytes accessed | tf_op | source)
XLA Modules:
  0.0 425.5 jit_solution(12167333763879739290)
XLA Ops:
  33.6 15.4 %shard_map.127 = f32[4,384,896]{2,1,0:T(8,128)} custom-call(bf16[768,2048]{1,0:T(8,128)(2,1)S(1)} %copy-done.20, bf16[1792,2048]{1,0:T(8,128)(2,1)} %w_ref.24, bf16[224,2048]{1,0:T(8,128)(2,1)S(1)} %bitcast.113), custom_call_target="tpu_custom_call" | custom-call | flops 5637144576 | bytes 15990784 | tf_op jit(solution)/shard_map/pallas_call | solution.py:114
  53.0 13.6 %collective-permute-done.7.rest_0_ = bf16[384,896]{1,0:T(8,128)(2,1)S(1)} collective-permute-done((bf16[384,896]{1,0:T(8,128)(2,1)}, bf16[384,896]{1,0:T(8,128)(2,1)S(1)}, u32[]{:S(2)}, u32[]{:S(2)}) %collective-permute-start.7) | collective-permute-done | bytes 688160 | tf_op jit(solution)/shard_map/ppermute | solution.py:275
  81.5 5.4 %shard_map.128 = bf16[384,896]{1,0:T(8,128)(2,1)} custom-call(s32[2]{0:T(128)S(1)} %pad_add_fusion.2.at, bf16[768,1024]{1,0:T(8,128)(2,1)S(1)} %copy-done.1, bf16[1024,3584]{1,0:T(8,128)(2,1)} %uw_ref.15, bf16[128,3584]{1,0:T(8,128)(2,1)S(1)} %bitcast.75, bf16[384,896]{1,0:T(8,128)(2,1)} %collective-permute-done.4.rest_0_), custom_call_target="tpu_custom_call" | custom-call | flops 704643072 | bytes 3899392 | tf_op jit(solution)/shard_map/pallas_call | solution.py:73
  88.1 5.5 %shard_map.134 = bf16[384,896]{1,0:T(8,128)(2,1)} custom-call(s32[2]{0:T(128)S(1)} %pad_add_fusion.3.at, bf16[768,1024]{1,0:T(8,128)(2,1)S(1)} %copy-done.1, bf16[1024,3584]{1,0:T(8,128)(2,1)} %gw_ref.15, bf16[128,3584]{1,0:T(8,128)(2,1)S(1)} %bitcast.95, bf16[384,896]{1,0:T(8,128)(2,1)} %collective-permute-done.11.rest_0_), custom_call_target="tpu_custom_call" | custom-call | flops 704643072 | bytes 3899392 | tf_op jit(solution)/shard_map/pallas_call | solution.py:73
  96.2 5.5 %shard_map.131 = bf16[384,896]{1,0:T(8,128)(2,1)} custom-call(s32[2]{0:T(128)S(1)} %pad_add_fusion.3.at, bf16[768,1024]{1,0:T(8,128)(2,1)S(1)} %copy-done.1, bf16[1024,3584]{1,0:T(8,128)(2,1)} %uw_ref.15, bf16[128,3584]{1,0:T(8,128)(2,1)S(1)} %bitcast.76, bf16[384,896]{1,0:T(8,128)(2,1)} %collective-permute-done.8.rest_0_), custom_call_target="tpu_custom_call" | custom-call | flops 704643072 | bytes 3899392 | tf_op jit(solution)/shard_map/pallas_call | solution.py:73
  102.0 5.5 %shard_map.125 = bf16[384,896]{1,0:T(8,128)(2,1)} custom-call(s32[2]{0:T(128)S(1)} %pad_add_fusion.2.at, bf16[768,1024]{1,0:T(8,128)(2,1)S(1)} %copy-done.1, bf16[1024,3584]{1,0:T(8,128)(2,1)} %gw_ref.15, bf16[128,3584]{1,0:T(8,128)(2,1)S(1)} %bitcast.96, bf16[384,896]{1,0:T(8,128)(2,1)} %collective-permute-done.1.rest_0_), custom_call_target="tpu_custom_call" | custom-call | flops 704643072 | bytes 3899392 | tf_op jit(solution)/shard_map/pallas_call | solution.py:73
  117.4 5.4 %shard_map.129 = bf16[384,896]{1,0:T(8,128)(2,1)} custom-call(s32[2]{0:T(128)S(1)} %pad_add_fusion.4.at, bf16[768,1024]{1,0:T(8,128)(2,1)S(1)} %copy-done.1, bf16[1024,3584]{1,0:T(8,128)(2,1)} %uw_ref.15, bf16[128,3584]{1,0:T(8,128)(2,1)S(1)} %bitcast.77, bf16[384,896]{1,0:T(8,128)(2,1)} %collective-permute-done.5.rest_0_), custom_call_target="tpu_custom_call" | custom-call | flops 704643072 | bytes 3899392 | tf_op jit(solution)/shard_map/pallas_call | solution.py:73
  126.8 5.4 %shard_map.135 = bf16[384,896]{1,0:T(8,128)(2,1)} custom-call(s32[2]{0:T(128)S(1)} %pad_add_fusion.5.at, bf16[768,1024]{1,0:T(8,128)(2,1)S(1)} %copy-done.1, bf16[1024,3584]{1,0:T(8,128)(2,1)} %gw_ref.15, bf16[128,3584]{1,0:T(8,128)(2,1)S(1)} %bitcast.97, bf16[384,896]{1,0:T(8,128)(2,1)} %collective-permute-done.12.rest_0_), custom_call_target="tpu_custom_call" | custom-call | flops 704643072 | bytes 3899392 | tf_op jit(solution)/shard_map/pallas_call | solution.py:73
  132.2 5.4 %shard_map.132 = bf16[384,896]{1,0:T(8,128)(2,1)} custom-call(s32[2]{0:T(128)S(1)} %pad_add_fusion.5.at, bf16[768,1024]{1,0:T(8,128)(2,1)S(1)} %copy-done.1, bf16[1024,3584]{1,0:T(8,128)(2,1)} %uw_ref.15, bf16[128,3584]{1,0:T(8,128)(2,1)S(1)} %bitcast.78, bf16[384,896]{1,0:T(8,128)(2,1)} %collective-permute-done.9.rest_0_), custom_call_target="tpu_custom_call" | custom-call | flops 704643072 | bytes 3899392 | tf_op jit(solution)/shard_map/pallas_call | solution.py:73
  139.0 5.4 %shard_map.126 = bf16[384,896]{1,0:T(8,128)(2,1)} custom-call(s32[2]{0:T(128)S(1)} %pad_add_fusion.4.at, bf16[768,1024]{1,0:T(8,128)(2,1)S(1)} %copy-done.1, bf16[1024,3584]{1,0:T(8,128)(2,1)} %gw_ref.15, bf16[128,3584]{1,0:T(8,128)(2,1)S(1)} %bitcast.98, bf16[384,896]{1,0:T(8,128)(2,1)} %collective-permute-done.2.rest_0_), custom_call_target="tpu_custom_call" | custom-call | flops 704643072 | bytes 3899392 | tf_op jit(solution)/shard_map/pallas_call | solution.py:73
  146.8 8.7 %collective-permute-start.14 = (bf16[384,896]{1,0:T(8,128)(2,1)}, bf16[384,896]{1,0:T(8,128)(2,1)S(1)}, u32[]{:S(2)}, u32[]{:S(2)}) collective-permute-start(bf16[384,896]{1,0:T(8,128)(2,1)} %shard_map.126), channel_id=1, source_target_pairs={{0,8},{8,16},{16,24},{24,28},{28,20},{20,12},{12,4},{4,0},{1,9},{9... | collective-permute-start | bytes 2064392 | tf_op jit(solution)/shard_map/ppermute | solution.py:272
  156.9 13.3 %collective-permute-done.10.rest_1_ = bf16[384,896]{1,0:T(8,128)(2,1)} collective-permute-done((bf16[384,896]{1,0:T(8,128)(2,1)}, bf16[384,896]{1,0:T(8,128)(2,1)}, u32[]{:S(2)}, u32[]{:S(2)}) %collective-permute-start.10) | collective-permute-done | bytes 688160 | tf_op jit(solution)/shard_map/ppermute | solution.py:275
  186.7 8.7 %collective-permute-start.16 = (bf16[384,896]{1,0:T(8,128)(2,1)S(1)}, bf16[384,896]{1,0:T(8,128)(2,1)S(1)}, u32[]{:S(2)}, u32[]{:S(2)}) collective-permute-start(bf16[384,896]{1,0:T(8,128)(2,1)S(1)} %get-tuple-element.36.ud_ref.refs_4_), channel_id=1, source_target_pairs={{0,8},{8,16},{16,24},{24,28},{28,20},{20,12},{12,4},{4,0},{1,9},{9... | collective-permute-start | bytes 2064392 | tf_op jit(solution)/shard_map/ppermute | solution.py:272
  198.9 11.7 %collective-permute-start.19 = (bf16[384,896]{1,0:T(8,128)(2,1)S(1)}, bf16[384,896]{1,0:T(8,128)(2,1)}, u32[]{:S(2)}, u32[]{:S(2)}) collective-permute-start(bf16[384,896]{1,0:T(8,128)(2,1)S(1)} %collective-permute-done.15.gd_ref.refs_3_), channel_id=1, source_target_pairs={{0,8},{8,16},{16,24},{24,28},{28,20},{20,12},{12,4},{4,0},{1,9},{9... | collective-permute-start | bytes 2064392 | tf_op jit(solution)/shard_map/ppermute | solution.py:272
  213.7 11.7 %collective-permute-start.20 = (bf16[384,896]{1,0:T(8,128)(2,1)S(1)}, bf16[384,896]{1,0:T(8,128)(2,1)}, u32[]{:S(2)}, u32[]{:S(2)}) collective-permute-start(bf16[384,896]{1,0:T(8,128)(2,1)S(1)} %collective-permute-done.16.ud_ref.refs_5_), channel_id=1, source_target_pairs={{0,8},{8,16},{16,24},{24,28},{28,20},{20,12},{12,4},{4,0},{1,9},{9... | collective-permute-start | bytes 2064392 | tf_op jit(solution)/shard_map/ppermute | solution.py:272
  226.3 10.4 %collective-permute-start.35 = (bf16[896,384]{0,1:T(8,128)(2,1)}, bf16[896,384]{0,1:T(8,128)(2,1)}, u32[]{:S(2)}, u32[]{:S(2)}) collective-permute-start(bf16[896,384]{0,1:T(8,128)(2,1)} %get-tuple-element.34), channel_id=1, source_target_pairs={{0,0},{28,1},{8,2},{20,3},{16,4},{12,5},{24,6},{4,7},{1,8},{29,9},... | collective-permute-start | bytes 2064392 | tf_op jit(solution)/shard_map/ppermute | solution.py:306
  243.2 11.7 %collective-permute-start.24 = (bf16[384,896]{1,0:T(8,128)(2,1)}, bf16[384,896]{1,0:T(8,128)(2,1)}, u32[]{:S(2)}, u32[]{:S(2)}) collective-permute-start(bf16[384,896]{1,0:T(8,128)(2,1)} %collective-permute-done.20.ud_ref.refs_5_), channel_id=1, source_target_pairs={{0,8},{8,16},{16,24},{24,28},{28,20},{20,12},{12,4},{4,0},{1,9},{9... | collective-permute-start | bytes 2064392 | tf_op jit(solution)/shard_map/ppermute | solution.py:272
  254.9 18.0 %collective-permute-done.22.ud_ref.refs_4_ = bf16[384,896]{1,0:T(8,128)(2,1)} collective-permute-done((bf16[384,896]{1,0:T(8,128)(2,1)}, bf16[384,896]{1,0:T(8,128)(2,1)}, u32[]{:S(2)}, u32[]{:S(2)}) %collective-permute-start.22) | collective-permute-done | bytes 688160 | tf_op jit(solution)/shard_map/ppermute | solution.py:275
  274.9 6.0 %shard_map.137.sum_ref = f32[2,384,1024]{2,1,0:T(8,128)} custom-call(s32[2]{0:T(128)S(1)} %pad_add_fusion.6.at, f32[2,384,1024]{2,1,0:T(8,128)} %broadcast_in_dim.32.sum_ref, bf16[384,896]{1,0:T(8,128)(2,1)S(1)} %get-tuple-element.35.gd_ref.refs_2_, bf16[384,896]{1,0:T(8,128)(2,1)S(1)} %get-tuple-element.36.ud_ref.refs_4_, ...), custom_call_target="tpu_custom_call", output_to_operand_aliasing={{}: (1, {})} | custom-call | flops 1409286144 | bytes 6815744 | tf_op jit(solution)/shard_map/pallas_call | solution.py:143
  283.2 6.0 %shard_map.138.sum_ref = f32[2,384,1024]{2,1,0:T(8,128)} custom-call(s32[2]{0:T(128)S(1)} %pad_add_fusion.5.at, f32[2,384,1024]{2,1,0:T(8,128)} %shard_map.137.sum_ref, bf16[384,896]{1,0:T(8,128)(2,1)S(1)} %copy-done.9, bf16[384,896]{1,0:T(8,128)(2,1)S(1)} %copy-done.12, bf16[1024,3584]{1,0:T(8,128)(2,1)} %gw_ref.15, ...), custom_call_target="tpu_custom_call", output_to_operand_aliasing={{}: (1, {})} | custom-call | flops 1409286144 | bytes 6815744 | tf_op jit(solution)/shard_map/pallas_call | solution.py:143
  289.2 6.5 %shard_map.139.sum_ref = f32[2,384,1024]{2,1,0:T(8,128)} custom-call(s32[2]{0:T(128)S(1)} %pad_add_fusion.4.at, f32[2,384,1024]{2,1,0:T(8,128)} %shard_map.138.sum_ref, bf16[384,896]{1,0:T(8,128)(2,1)} %collective-permute-done.17.gd_ref.refs_2_, bf16[384,896]{1,0:T(8,128)(2,1)} %collective-permute-done.18.ud_ref.refs_4_, ...), custom_call_target="tpu_custom_call", output_to_operand_aliasing={{}: (1, {})} | custom-call | flops 1409286144 | bytes 6815744 | tf_op jit(solution)/shard_map/pallas_call | solution.py:143
  295.6 6.6 %shard_map.140.sum_ref = f32[2,384,1024]{2,1,0:T(8,128)} custom-call(s32[2]{0:T(128)S(1)} %pad_add_fusion.3.at, f32[2,384,1024]{2,1,0:T(8,128)} %shard_map.139.sum_ref, bf16[384,896]{1,0:T(8,128)(2,1)} %collective-permute-done.19.gd_ref.refs_3_, bf16[384,896]{1,0:T(8,128)(2,1)} %collective-permute-done.20.ud_ref.refs_5_, ...), custom_call_target="tpu_custom_call", output_to_operand_aliasing={{}: (1, {})} | custom-call | flops 1409286144 | bytes 6815744 | tf_op jit(solution)/shard_map/pallas_call | solution.py:143
  302.2 6.5 %shard_map.141.sum_ref = f32[2,384,1024]{2,1,0:T(8,128)} custom-call(s32[2]{0:T(128)S(1)} %pad_add_fusion.2.at, f32[2,384,1024]{2,1,0:T(8,128)} %shard_map.140.sum_ref, bf16[384,896]{1,0:T(8,128)(2,1)} %collective-permute-done.21.gd_ref.refs_2_, bf16[384,896]{1,0:T(8,128)(2,1)} %collective-permute-done.22.ud_ref.refs_4_, ...), custom_call_target="tpu_custom_call", output_to_operand_aliasing={{}: (1, {})} | custom-call | flops 1409286144 | bytes 6815744 | tf_op jit(solution)/shard_map/pallas_call | solution.py:143
  308.7 6.5 %shard_map.142.sum_ref = f32[2,384,1024]{2,1,0:T(8,128)} custom-call(s32[2]{0:T(128)S(1)} %get-tuple-element.42.at, f32[2,384,1024]{2,1,0:T(8,128)} %shard_map.141.sum_ref, bf16[384,896]{1,0:T(8,128)(2,1)} %collective-permute-done.23.gd_ref.refs_3_, bf16[384,896]{1,0:T(8,128)(2,1)} %collective-permute-done.24.ud_ref.refs_5_, ...), custom_call_target="tpu_custom_call", output_to_operand_aliasing={{}: (1, {})} | custom-call | flops 1409286144 | bytes 6815744 | tf_op jit(solution)/shard_map/pallas_call | solution.py:143
  315.8 6.5 %shard_map.143.sum_ref = f32[2,384,1024]{2,1,0:T(8,128)} custom-call(s32[2]{0:T(128)S(1)} %get-tuple-element.41.at, f32[2,384,1024]{2,1,0:T(8,128)} %shard_map.142.sum_ref, bf16[384,896]{1,0:T(8,128)(2,1)} %collective-permute-done.25.gd_ref.refs_2_, bf16[384,896]{1,0:T(8,128)(2,1)} %collective-permute-done.26.ud_ref.refs_4_, ...), custom_call_target="tpu_custom_call", output_to_operand_aliasing={{}: (1, {})} | custom-call | flops 1409286144 | bytes 6815744 | tf_op jit(solution)/shard_map/pallas_call | solution.py:143
  336.6 13.2 %collective-permute-done.30.gd_ref.refs_3_ = bf16[384,896]{1,0:T(8,128)(2,1)S(1)} collective-permute-done((bf16[384,896]{1,0:T(8,128)(2,1)}, bf16[384,896]{1,0:T(8,128)(2,1)S(1)}, u32[]{:S(2)}, u32[]{:S(2)}) %collective-permute-start.30) | collective-permute-done | bytes 688160 | tf_op jit(solution)/shard_map/ppermute | solution.py:272
  351.2 6.0 %shard_map.144 = f32[2,384,1024]{2,1,0:T(8,128)} custom-call(s32[2]{0:T(128)S(1)} %get-tuple-element.44.at, f32[2,384,1024]{2,1,0:T(8,128)} %shard_map.143.sum_ref, bf16[384,896]{1,0:T(8,128)(2,1)S(1)} %collective-permute-done.30.gd_ref.refs_3_, bf16[384,896]{1,0:T(8,128)(2,1)S(1)} %collective-permute-done.31.ud_ref.refs_5_, ...), custom_call_target="tpu_custom_call", output_to_operand_aliasing={{}: (1, {})} | custom-call | flops 1409286144 | bytes 6815744 | tf_op jit(solution)/shard_map/pallas_call | solution.py:143
  360.2 8.4 %shard_map.145 = (bf16[1024,3584]{1,0:T(8,128)(2,1)}, bf16[1024,3584]{1,0:T(8,128)(2,1)}) custom-call(s32[3]{0:T(128)S(1)} %pad_add_fusion.12.at, bf16[2,1024,384]{2,1,0:T(8,128)(2,1)} %bitcast.115, bf16[2,1024,384]{2,1,0:T(8,128)(2,1)} %bitcast.116, bf16[384,896]{1,0:T(8,128)(2,1)} %collective-permute-done.21.gd_ref.refs_2_, ...), custom_call_target="tpu_custom_call" | custom-call | flops 2818572288 | bytes 6422528 | tf_op jit(solution)/shard_map/pallas_call | solution.py:187
  368.5 8.4 %shard_map.146 = (bf16[1024,3584]{1,0:T(8,128)(2,1)}, bf16[1024,3584]{1,0:T(8,128)(2,1)}) custom-call(s32[3]{0:T(128)S(1)} %pad_add_fusion.11.at, bf16[2,1024,384]{2,1,0:T(8,128)(2,1)} %bitcast.117, bf16[2,1024,384]{2,1,0:T(8,128)(2,1)} %bitcast.118, ...), custom_call_target="tpu_custom_call", output_to_operand_aliasing={{0}: (9, {}), {1}: (10, {})} | custom-call | flops 2818572288 | bytes 6422528 | tf_op jit(solution)/shard_map/pallas_call | solution.py:187
  377.4 8.0 %shard_map.147 = (bf16[1024,3584]{1,0:T(8,128)(2,1)}, bf16[1024,3584]{1,0:T(8,128)(2,1)}) custom-call(s32[3]{0:T(128)S(1)} %pad_add_fusion.10.at, bf16[2,1024,384]{2,1,0:T(8,128)(2,1)} %bitcast.119, bf16[2,1024,384]{2,1,0:T(8,128)(2,1)} %bitcast.120, ...), custom_call_target="tpu_custom_call", output_to_operand_aliasing={{0}: (9, {}), {1}: (10, {})} | custom-call | flops 2818572288 | bytes 6422528 | tf_op jit(solution)/shard_map/pallas_call | solution.py:187
  388.7 7.4 %shard_map.148 = (bf16[1024,3584]{1,0:T(8,128)(2,1)}, bf16[1024,3584]{1,0:T(8,128)(2,1)}) custom-call(s32[3]{0:T(128)S(1)} %pad_add_fusion.9.at, bf16[2,1024,384]{2,1,0:T(8,128)(2,1)} %bitcast.121, bf16[2,1024,384]{2,1,0:T(8,128)(2,1)} %bitcast.122, bf16[384,896]{1,0:T(8,128)(2,1)S(1)} %copy-done.5, ...), custom_call_target="tpu_custom_call", output_to_operand_aliasing={{0}: (9, {}), {1}: (10, {})} | custom-call | flops 2818572288 | bytes 6422528 | tf_op jit(solution)/shard_map/pallas_call | solution.py:187
  406.4 12.3 %shard_map.149 = bf16[1792,2048]{1,0:T(8,128)(2,1)} custom-call(bf16[4,896,384]{2,1,0:T(8,128)(2,1)S(1)} %bitcast.112, bf16[768,2048]{1,0:T(8,128)(2,1)} %g_ref.1, bf16[224,2048]{1,0:T(8,128)(2,1)S(1)} %bitcast.114), custom_call_target="tpu_custom_call" | custom-call | flops 5637144576 | bytes 10485760 | tf_op jit(solution)/shard_map/pallas_call | solution.py:216
  (161 shorter events, 129.1 us)
Async XLA Ops:
  7.2 101.4 %reduce-scatter.2.cloned.1.call-start = ((), (), s32[]{:S(2)}) async-start(), calls=%async_computation.1 | async-start | bytes 6881280 | tf_op jit(solution)/shard_map/reduce_scatter | solution.py:283
  50.0 351.9 %all-gather.3.cloned.1.call-start = ((), (), s32[]{:S(2)}) async-start(), calls=%async_computation.2 | async-start | bytes 3440640 | tf_op jit(solution)/shard_map/all_gather | solution.py:307
  50.0 16.6 %collective-permute-start.7 = (bf16[384,896]{1,0:T(8,128)(2,1)}, bf16[384,896]{1,0:T(8,128)(2,1)S(1)}, u32[]{:S(2)}, u32[]{:S(2)}) collective-permute-start(bf16[384,896]{1,0:T(8,128)(2,1)} %copy-done.19), channel_id=1, source_target_pairs={{8,0},{16,8},{24,16},{28,24},{20,28},{12,20},{4,12},{0,4},{9,1},{1... | collective-permute-start | bytes 2064392 | tf_op jit(solution)/shard_map/ppermute | solution.py:275
  50.1 22.1 %collective-permute-start = (bf16[384,896]{1,0:T(8,128)(2,1)}, bf16[384,896]{1,0:T(8,128)(2,1)S(1)}, u32[]{:S(2)}, u32[]{:S(2)}) collective-permute-start(bf16[384,896]{1,0:T(8,128)(2,1)} %copy-done.18), channel_id=1, source_target_pairs={{0,8},{8,16},{16,24},{24,28},{28,20},{20,12},{12,4},{4,0},{1,9},{9... | collective-permute-start | bytes 2064392 | tf_op jit(solution)/shard_map/ppermute | solution.py:272
  51.5 30.0 %collective-permute-start.4 = (bf16[384,896]{1,0:T(8,128)(2,1)}, bf16[384,896]{1,0:T(8,128)(2,1)}, u32[]{:S(2)}, u32[]{:S(2)}) collective-permute-start(bf16[384,896]{1,0:T(8,128)(2,1)} %copy-done.17), channel_id=1, source_target_pairs={{0,8},{8,16},{16,24},{24,28},{28,20},{20,12},{12,4},{4,0},{1,9},{9... | collective-permute-start | bytes 2064392 | tf_op jit(solution)/shard_map/ppermute | solution.py:272
  52.8 35.2 %collective-permute-start.11 = (bf16[384,896]{1,0:T(8,128)(2,1)}, bf16[384,896]{1,0:T(8,128)(2,1)}, u32[]{:S(2)}, u32[]{:S(2)}) collective-permute-start(bf16[384,896]{1,0:T(8,128)(2,1)} %copy-done.16), channel_id=1, source_target_pairs={{8,0},{16,8},{24,16},{28,24},{20,28},{12,20},{4,12},{0,4},{9,1},{1... | collective-permute-start | bytes 2064392 | tf_op jit(solution)/shard_map/ppermute | solution.py:275
  71.8 24.4 %collective-permute-start.8 = (bf16[384,896]{1,0:T(8,128)(2,1)}, bf16[384,896]{1,0:T(8,128)(2,1)}, u32[]{:S(2)}, u32[]{:S(2)}) collective-permute-start(bf16[384,896]{1,0:T(8,128)(2,1)} %shard_map.130), channel_id=1, source_target_pairs={{8,0},{16,8},{24,16},{28,24},{20,28},{12,20},{4,12},{0,4},{9,1},{1... | collective-permute-start | bytes 2064392 | tf_op jit(solution)/shard_map/ppermute | solution.py:275
  77.5 24.5 %collective-permute-start.1 = (bf16[384,896]{1,0:T(8,128)(2,1)}, bf16[384,896]{1,0:T(8,128)(2,1)}, u32[]{:S(2)}, u32[]{:S(2)}) collective-permute-start(bf16[384,896]{1,0:T(8,128)(2,1)} %shard_map.124), channel_id=1, source_target_pairs={{0,8},{8,16},{16,24},{24,28},{28,20},{20,12},{12,4},{4,0},{1,9},{9... | collective-permute-start | bytes 2064392 | tf_op jit(solution)/shard_map/ppermute | solution.py:272
  87.0 30.5 %collective-permute-start.5 = (bf16[384,896]{1,0:T(8,128)(2,1)}, bf16[384,896]{1,0:T(8,128)(2,1)}, u32[]{:S(2)}, u32[]{:S(2)}) collective-permute-start(bf16[384,896]{1,0:T(8,128)(2,1)} %shard_map.128), channel_id=1, source_target_pairs={{0,8},{8,16},{16,24},{24,28},{28,20},{20,12},{12,4},{4,0},{1,9},{9... | collective-permute-start | bytes 2064392 | tf_op jit(solution)/shard_map/ppermute | solution.py:272
  93.6 33.2 %collective-permute-start.12 = (bf16[384,896]{1,0:T(8,128)(2,1)}, bf16[384,896]{1,0:T(8,128)(2,1)}, u32[]{:S(2)}, u32[]{:S(2)}) collective-permute-start(bf16[384,896]{1,0:T(8,128)(2,1)} %shard_map.134), channel_id=1, source_target_pairs={{8,0},{16,8},{24,16},{28,24},{20,28},{12,20},{4,12},{0,4},{9,1},{1... | collective-permute-start | bytes 2064392 | tf_op jit(solution)/shard_map/ppermute | solution.py:275
  101.6 30.6 %collective-permute-start.9 = (bf16[384,896]{1,0:T(8,128)(2,1)}, bf16[384,896]{1,0:T(8,128)(2,1)}, u32[]{:S(2)}, u32[]{:S(2)}) collective-permute-start(bf16[384,896]{1,0:T(8,128)(2,1)} %shard_map.131), channel_id=1, source_target_pairs={{8,0},{16,8},{24,16},{28,24},{20,28},{12,20},{4,12},{0,4},{9,1},{1... | collective-permute-start | bytes 2064392 | tf_op jit(solution)/shard_map/ppermute | solution.py:275
  107.4 31.6 %collective-permute-start.2 = (bf16[384,896]{1,0:T(8,128)(2,1)}, bf16[384,896]{1,0:T(8,128)(2,1)}, u32[]{:S(2)}, u32[]{:S(2)}) collective-permute-start(bf16[384,896]{1,0:T(8,128)(2,1)} %shard_map.125), channel_id=1, source_target_pairs={{0,8},{8,16},{16,24},{24,28},{28,20},{20,12},{12,4},{4,0},{1,9},{9... | collective-permute-start | bytes 2064392 | tf_op jit(solution)/shard_map/ppermute | solution.py:272
  110.9 35.9 %collective-permute-start.3 = (bf16[384,896]{1,0:T(8,128)(2,1)}, bf16[384,896]{1,0:T(8,128)(2,1)}, u32[]{:S(2)}, u32[]{:S(2)}) collective-permute-start(bf16[384,896]{1,0:T(8,128)(2,1)} %convert_bitcast_fusion), channel_id=1, source_target_pairs={{0,0},{1,28},{2,8},{3,20},{4,16},{5,12},{6,24},{7,4},{8,1},{9,29},... | collective-permute-start | bytes 2064392 | tf_op jit(solution)/shard_map/ppermute | solution.py:284
  122.9 34.1 %collective-permute-start.6 = (bf16[384,896]{1,0:T(8,128)(2,1)}, bf16[384,896]{1,0:T(8,128)(2,1)}, u32[]{:S(2)}, u32[]{:S(2)}) collective-permute-start(bf16[384,896]{1,0:T(8,128)(2,1)} %shard_map.129), channel_id=1, source_target_pairs={{0,8},{8,16},{16,24},{24,28},{28,20},{20,12},{12,4},{4,0},{1,9},{9... | collective-permute-start | bytes 2064392 | tf_op jit(solution)/shard_map/ppermute | solution.py:272
  132.2 43.1 %collective-permute-start.13 = (bf16[384,896]{1,0:T(8,128)(2,1)}, bf16[384,896]{1,0:T(8,128)(2,1)}, u32[]{:S(2)}, u32[]{:S(2)}) collective-permute-start(bf16[384,896]{1,0:T(8,128)(2,1)} %shard_map.135), channel_id=1, source_target_pairs={{8,0},{16,8},{24,16},{28,24},{20,28},{12,20},{4,12},{0,4},{9,1},{1... | collective-permute-start | bytes 2064392 | tf_op jit(solution)/shard_map/ppermute | solution.py:275
  137.7 32.5 %collective-permute-start.10 = (bf16[384,896]{1,0:T(8,128)(2,1)}, bf16[384,896]{1,0:T(8,128)(2,1)}, u32[]{:S(2)}, u32[]{:S(2)}) collective-permute-start(bf16[384,896]{1,0:T(8,128)(2,1)} %shard_map.132), channel_id=1, source_target_pairs={{8,0},{16,8},{24,16},{28,24},{20,28},{12,20},{4,12},{0,4},{9,1},{1... | collective-permute-start | bytes 2064392 | tf_op jit(solution)/shard_map/ppermute | solution.py:275
  146.8 28.5 %collective-permute-start.14 = (bf16[384,896]{1,0:T(8,128)(2,1)}, bf16[384,896]{1,0:T(8,128)(2,1)S(1)}, u32[]{:S(2)}, u32[]{:S(2)}) collective-permute-start(bf16[384,896]{1,0:T(8,128)(2,1)} %shard_map.126), channel_id=1, source_target_pairs={{0,8},{8,16},{16,24},{24,28},{28,20},{20,12},{12,4},{4,0},{1,9},{9... | collective-permute-start | bytes 2064392 | tf_op jit(solution)/shard_map/ppermute | solution.py:272
  186.7 27.0 %collective-permute-start.16 = (bf16[384,896]{1,0:T(8,128)(2,1)S(1)}, bf16[384,896]{1,0:T(8,128)(2,1)S(1)}, u32[]{:S(2)}, u32[]{:S(2)}) collective-permute-start(bf16[384,896]{1,0:T(8,128)(2,1)S(1)} %get-tuple-element.36.ud_ref.refs_4_), channel_id=1, source_target_pairs={{0,8},{8,16},{16,24},{24,28},{28,20},{20,12},{12,4},{4,0},{1,9},{9... | collective-permute-start | bytes 2064392 | tf_op jit(solution)/shard_map/ppermute | solution.py:272
  195.3 30.9 %collective-permute-start.17 = (bf16[384,896]{1,0:T(8,128)(2,1)S(1)}, bf16[384,896]{1,0:T(8,128)(2,1)}, u32[]{:S(2)}, u32[]{:S(2)}) collective-permute-start(bf16[384,896]{1,0:T(8,128)(2,1)S(1)} %get-tuple-element.35.gd_ref.refs_2_), channel_id=1, source_target_pairs={{8,0},{16,8},{24,16},{28,24},{20,28},{12,20},{4,12},{0,4},{9,1},{1... | collective-permute-start | bytes 2064392 | tf_op jit(solution)/shard_map/ppermute | solution.py:275
  195.3 30.9 %collective-permute-start.18 = (bf16[384,896]{1,0:T(8,128)(2,1)S(1)}, bf16[384,896]{1,0:T(8,128)(2,1)}, u32[]{:S(2)}, u32[]{:S(2)}) collective-permute-start(bf16[384,896]{1,0:T(8,128)(2,1)S(1)} %get-tuple-element.36.ud_ref.refs_4_), channel_id=1, source_target_pairs={{8,0},{16,8},{24,16},{28,24},{20,28},{12,20},{4,12},{0,4},{9,1},{1... | collective-permute-start | bytes 2064392 | tf_op jit(solution)/shard_map/ppermute | solution.py:275
  198.9 37.8 %collective-permute-start.19 = (bf16[384,896]{1,0:T(8,128)(2,1)S(1)}, bf16[384,896]{1,0:T(8,128)(2,1)}, u32[]{:S(2)}, u32[]{:S(2)}) collective-permute-start(bf16[384,896]{1,0:T(8,128)(2,1)S(1)} %collective-permute-done.15.gd_ref.refs_3_), channel_id=1, source_target_pairs={{0,8},{8,16},{16,24},{24,28},{28,20},{20,12},{12,4},{4,0},{1,9},{9... | collective-permute-start | bytes 2064392 | tf_op jit(solution)/shard_map/ppermute | solution.py:272
  213.7 29.5 %collective-permute-start.20 = (bf16[384,896]{1,0:T(8,128)(2,1)S(1)}, bf16[384,896]{1,0:T(8,128)(2,1)}, u32[]{:S(2)}, u32[]{:S(2)}) collective-permute-start(bf16[384,896]{1,0:T(8,128)(2,1)S(1)} %collective-permute-done.16.ud_ref.refs_5_), channel_id=1, source_target_pairs={{0,8},{8,16},{16,24},{24,28},{28,20},{20,12},{12,4},{4,0},{1,9},{9... | collective-permute-start | bytes 2064392 | tf_op jit(solution)/shard_map/ppermute | solution.py:272
  226.3 28.6 %collective-permute-start.21 = (bf16[384,896]{1,0:T(8,128)(2,1)}, bf16[384,896]{1,0:T(8,128)(2,1)}, u32[]{:S(2)}, u32[]{:S(2)}) collective-permute-start(bf16[384,896]{1,0:T(8,128)(2,1)} %collective-permute-done.17.gd_ref.refs_2_), channel_id=1, source_target_pairs={{8,0},{16,8},{24,16},{28,24},{20,28},{12,20},{4,12},{0,4},{9,1},{1... | collective-permute-start | bytes 2064392 | tf_op jit(solution)/shard_map/ppermute | solution.py:275
  226.3 46.6 %collective-permute-start.22 = (bf16[384,896]{1,0:T(8,128)(2,1)}, bf16[384,896]{1,0:T(8,128)(2,1)}, u32[]{:S(2)}, u32[]{:S(2)}) collective-permute-start(bf16[384,896]{1,0:T(8,128)(2,1)} %collective-permute-done.18.ud_ref.refs_4_), channel_id=1, source_target_pairs={{8,0},{16,8},{24,16},{28,24},{20,28},{12,20},{4,12},{0,4},{9,1},{1... | collective-permute-start | bytes 2064392 | tf_op jit(solution)/shard_map/ppermute | solution.py:275
  226.3 54.6 %collective-permute-start.35 = (bf16[896,384]{0,1:T(8,128)(2,1)}, bf16[896,384]{0,1:T(8,128)(2,1)}, u32[]{:S(2)}, u32[]{:S(2)}) collective-permute-start(bf16[896,384]{0,1:T(8,128)(2,1)} %get-tuple-element.34), channel_id=1, source_target_pairs={{0,0},{28,1},{8,2},{20,3},{16,4},{12,5},{24,6},{4,7},{1,8},{29,9},... | collective-permute-start | bytes 2064392 | tf_op jit(solution)/shard_map/ppermute | solution.py:306
  236.7 71.9 %collective-permute-start.23 = (bf16[384,896]{1,0:T(8,128)(2,1)}, bf16[384,896]{1,0:T(8,128)(2,1)}, u32[]{:S(2)}, u32[]{:S(2)}) collective-permute-start(bf16[384,896]{1,0:T(8,128)(2,1)} %collective-permute-done.19.gd_ref.refs_3_), channel_id=1, source_target_pairs={{0,8},{8,16},{16,24},{24,28},{28,20},{20,12},{12,4},{4,0},{1,9},{9... | collective-permute-start | bytes 2064392 | tf_op jit(solution)/shard_map/ppermute | solution.py:272
  243.2 65.5 %collective-permute-start.24 = (bf16[384,896]{1,0:T(8,128)(2,1)}, bf16[384,896]{1,0:T(8,128)(2,1)}, u32[]{:S(2)}, u32[]{:S(2)}) collective-permute-start(bf16[384,896]{1,0:T(8,128)(2,1)} %collective-permute-done.20.ud_ref.refs_5_), channel_id=1, source_target_pairs={{0,8},{8,16},{16,24},{24,28},{28,20},{20,12},{12,4},{4,0},{1,9},{9... | collective-permute-start | bytes 2064392 | tf_op jit(solution)/shard_map/ppermute | solution.py:272
  254.9 60.3 %collective-permute-start.25 = (bf16[384,896]{1,0:T(8,128)(2,1)}, bf16[384,896]{1,0:T(8,128)(2,1)}, u32[]{:S(2)}, u32[]{:S(2)}) collective-permute-start(bf16[384,896]{1,0:T(8,128)(2,1)} %collective-permute-done.21.gd_ref.refs_2_), channel_id=1, source_target_pairs={{8,0},{16,8},{24,16},{28,24},{20,28},{12,20},{4,12},{0,4},{9,1},{1... | collective-permute-start | bytes 2064392 | tf_op jit(solution)/shard_map/ppermute | solution.py:275
  272.9 42.9 %collective-permute-start.26 = (bf16[384,896]{1,0:T(8,128)(2,1)}, bf16[384,896]{1,0:T(8,128)(2,1)}, u32[]{:S(2)}, u32[]{:S(2)}) collective-permute-start(bf16[384,896]{1,0:T(8,128)(2,1)} %collective-permute-done.22.ud_ref.refs_4_), channel_id=1, source_target_pairs={{8,0},{16,8},{24,16},{28,24},{20,28},{12,20},{4,12},{0,4},{9,1},{1... | collective-permute-start | bytes 2064392 | tf_op jit(solution)/shard_map/ppermute | solution.py:275
  332.5 17.3 %collective-permute-start.30 = (bf16[384,896]{1,0:T(8,128)(2,1)}, bf16[384,896]{1,0:T(8,128)(2,1)S(1)}, u32[]{:S(2)}, u32[]{:S(2)}) collective-permute-start(bf16[384,896]{1,0:T(8,128)(2,1)} %collective-permute-done.23.gd_ref.refs_3_), channel_id=1, source_target_pairs={{0,8},{8,16},{16,24},{24,28},{28,20},{20,12},{12,4},{4,0},{1,9},{9... | collective-permute-start | bytes 2064392 | tf_op jit(solution)/shard_map/ppermute | solution.py:272
  334.8 16.4 %collective-permute-start.31 = (bf16[384,896]{1,0:T(8,128)(2,1)}, bf16[384,896]{1,0:T(8,128)(2,1)S(1)}, u32[]{:S(2)}, u32[]{:S(2)}) collective-permute-start(bf16[384,896]{1,0:T(8,128)(2,1)} %collective-permute-done.26.ud_ref.refs_4_), channel_id=1, source_target_pairs={{8,0},{16,8},{24,16},{28,24},{20,28},{12,20},{4,12},{0,4},{9,1},{1... | collective-permute-start | bytes 2064392 | tf_op jit(solution)/shard_map/ppermute | solution.py:275
  358.4 26.9 %collective-permute-start.32 = (f32[192,1024]{1,0:T(8,128)S(1)}, f32[192,1024]{1,0:T(8,128)S(1)}, u32[]{:S(2)}, u32[]{:S(2)}) collective-permute-start(f32[192,1024]{1,0:T(8,128)S(1)} %dynamic-slice_bitcast_fusion), channel_id=1, source_target_pairs={{0,1},{1,0},{2,3},{3,2},{4,5},{5,4},{6,7},{7,6},{8,9},{9,8},{10,11... | collective-permute-start | bytes 2359304 | tf_op jit(solution)/shard_map/ppermute | solution.py:366
  (28 other events, 654.7 us)
Sparse Core Ops, SparseCore 0:
  50.1 54.2 reduce-scatter.1
  281.1 38.1 all-gather.2

commit v2 on v1

--- a/solution.py
+++ b/solution.py
@@ -46,84 +46,109 @@
     return best
 
 
-def piece_kernel(at, x_ref, w_ref, m_ref, *rest):
-    *came, out_ref, total_ref = rest
-    term = jnp.dot(x_ref[...], masked(w_ref[...], m_ref[...]), preferred_element_type=F32)
-
-    @pl.when(pl.program_id(0) == 0)
-    def _():
-        start = term
-        for ref in came:
-            start = start + ref[...].astype(F32)
-        total_ref[...] = start
-
-    @pl.when(pl.program_id(0) > 0)
-    def _():
-        total_ref[...] += term
-
-    @pl.when(pl.program_id(0) == pl.num_programs(0) - 1)
-    def _():
-        out_ref[...] = total_ref[...].astype(out_ref.dtype)
-
-
-def piece(at, inputs, weight, wide, came, tokens, columns, kind):
-    depth = inputs.shape[1]
-    tile = tile_of(depth, 256)
+def product_kernel(parts, at, x_ref, w_ref, m_ref, *outs):
+    weight = masked(w_ref[...], m_ref[...])
+    tokens = outs[0].shape[0]
+    for i in range(parts):
+        start = pl.multiple_of(at[1 + i] * tokens, tokens)
+        term = jnp.dot(x_ref[pl.ds(start, tokens), :], weight, preferred_element_type=F32)
+        outs[i][...] = term.astype(outs[i].dtype)
+
+
+def products(at, inputs, weight, wide, columns, kinds):
+    count, depth = inputs.shape
+    parts = len(kinds)
+    tokens = count // parts
     whole = pl.BlockSpec((tokens, columns), lambda k, at: (0, 0))
     return pl.pallas_call(
-        piece_kernel,
-        out_shape=jax.ShapeDtypeStruct((tokens, columns), kind),
+        functools.partial(product_kernel, parts),
+        name="products",
+        out_shape=tuple(jax.ShapeDtypeStruct((tokens, columns), kind) for kind in kinds),
         grid_spec=pltpu.PrefetchScalarGridSpec(
             num_scalar_prefetch=1,
-            grid=(depth // tile,),
+            grid=(1,),
             in_specs=[
-                pl.BlockSpec((tokens, tile), lambda k, at: (at[0], k)),
-                pl.BlockSpec((tile, columns), lambda k, at: (k, at[1])),
-                pl.BlockSpec((tile // BLOCK * ROWS, columns), lambda k, at: (k, at[1])),
-            ]
-            + [whole] * len(came),
-            out_specs=whole,
-            scratch_shapes=[pltpu.VMEM((tokens, columns), F32)],
+                pl.BlockSpec((count, depth), lambda k, at: (0, 0)),
+                pl.BlockSpec((depth, columns), lambda k, at: (0, at[0])),
+                pl.BlockSpec((wide.shape[0], columns), lambda k, at: (0, at[0])),
+            ],
+            out_specs=(whole,) * parts,
         ),
         compiler_params=params(),
-        cost_estimate=cost(2 * tokens * depth * columns, 2 * depth * columns + 6 * tokens * columns),
-    )(at, inputs, weight, wide, *came)
-
-
-def hidden_grad_kernel(g_ref, w_ref, m_ref, out_ref):
+        cost_estimate=cost(2 * count * depth * columns, 2 * depth * columns + 6 * count * columns),
+    )(at, inputs, weight, wide)
+
+
+def owner_kernel(gate_ref, gate_on, gate_back, up_ref, up_on, up_back, hg_ref, gd_ref, ud_ref, h_ref):
+    gate = gate_ref[...] + gate_on[...].astype(F32) + gate_back[...].astype(F32)
+    up = up_ref[...] + up_on[...].astype(F32) + up_back[...].astype(F32)
+    hidden_grad = hg_ref[...].astype(F32)
+    sig = jax.nn.sigmoid(gate)
+    gated = gate * sig
+    gd_ref[...] = (hidden_grad * up * sig * (1.0 + gate * (1.0 - sig))).astype(BF16)
+    ud_ref[...] = (hidden_grad * gated).astype(BF16)
+    h_ref[...] = (gated * up).T.astype(BF16)
+
+
+def owner(*operands):
+    tokens, columns = operands[0].shape
+    tile = BLOCK
+    block = pl.BlockSpec((tokens, tile), lambda i: (0, i))
+    shape = jax.ShapeDtypeStruct((tokens, columns), BF16)
+    return pl.pallas_call(
+        owner_kernel,
+        name="owner",
+        out_shape=(shape, shape, jax.ShapeDtypeStruct((columns, tokens), BF16)),
+        grid=(columns // tile,),
+        in_specs=[block] * len(operands),
+        out_specs=(block, block, pl.BlockSpec((tile, tokens), lambda i: (i, 0))),
+        compiler_params=params(),
+        cost_estimate=cost(0, 24 * tokens * columns),
+    )(*operands)
+
+
+def hidden_grad_kernel(at, g_ref, w_ref, m_ref, keep_ref, *send_refs):
     weight = masked(w_ref[...], m_ref[...])
-    parts, tokens, _ = out_ref.shape
-    first = pl.program_id(1) == 0
-    for t in range(parts):
-        term = dot_nt(g_ref[t * tokens : (t + 1) * tokens, :], weight)
-
-        @pl.when(first)
+    _, half, tokens, _ = keep_ref.shape
+
+    def product(t):
+        start = pl.multiple_of(t * tokens, tokens)
+        return dot_nt(g_ref[pl.ds(start, tokens), :], weight)
+
+    for t in range(half):
+        keep_ref[0, t] = product(2 * t + at[0])
+    for i, send_ref in enumerate(send_refs):
+
+        @pl.when(pl.program_id(0) == i)
         def _():
-            out_ref[t] = term
-
-        @pl.when(jnp.logical_not(first))
-        def _():
-            out_ref[t] += term
-
-
-def hidden_grad_partial(out_grad, weight, wide, parts, columns):
+            for t in range(half):
+                send_ref[t] = product(2 * t + 1 - at[0]).astype(BF16)
+
+
+def hidden_grad_partial(at, out_grad, weight, wide, parts, columns):
     count, depth = out_grad.shape
     cuts = weight.shape[0] // columns
     tokens = count // parts
-    tile = tile_of(depth, 512)
+    shape = (cuts, parts // 2, tokens, columns)
+    keep = pl.BlockSpec((1,) + shape[1:], lambda i, at: (i, 0, 0, 0))
+    send = pl.BlockSpec(shape[1:], lambda i, at: (0, 0, 0))
     return pl.pallas_call(
         hidden_grad_kernel,
-        out_shape=jax.ShapeDtypeStruct((cuts * parts, tokens, columns), F32),
-        grid=(cuts, depth // tile),
-        in_specs=[
-            pl.BlockSpec((count, tile), lambda i, k: (0, k)),
-            pl.BlockSpec((columns, tile), lambda i, k: (i, k)),
-            pl.BlockSpec((columns // BLOCK * ROWS, tile), lambda i, k: (i, k)),
-        ],
-        out_specs=pl.BlockSpec((parts, tokens, columns), lambda i, k: (i, 0, 0)),
+        name="hidden_grad",
+        out_shape=(jax.ShapeDtypeStruct(shape, F32),) + (jax.ShapeDtypeStruct(shape[1:], BF16),) * cuts,
+        grid_spec=pltpu.PrefetchScalarGridSpec(
+            num_scalar_prefetch=1,
+            grid=(cuts,),
+            in_specs=[
+                pl.BlockSpec((count, depth), lambda i, at: (0, 0)),
+                pl.BlockSpec((columns, depth), lambda i, at: (i, 0)),
+                pl.BlockSpec((columns // BLOCK * ROWS, depth), lambda i, at: (i, 0)),
+            ],
+            out_specs=(keep,) + (send,) * cuts,
+        ),
         compiler_params=params(),
         cost_estimate=cost(2 * count * depth * weight.shape[0], 2 * weight.size + 2 * out_grad.size + 4 * count * weight.shape[0]),
-    )(out_grad, weight, wide)
+    )(at, out_grad, weight, wide)
 
 
 def input_grad_kernel(at, sum_ref, gd_ref, ud_ref, gw_ref, uw_ref, gm_ref, um_ref, out_ref):
@@ -135,13 +160,14 @@
 def add_input_grad(at, total, gate_delta, up_delta, gate_weight, up_weight, gate_wide, up_wide):
     tokens, columns = gate_delta.shape
     depth = gate_weight.shape[0]
-    tile = tile_of(depth, 256)
+    tile = tile_of(depth, 512)
     delta = pl.BlockSpec((tokens, columns), lambda n, at: (0, 0))
     weight = pl.BlockSpec((tile, columns), lambda n, at: (n, at[1]))
     wide = pl.BlockSpec((tile // BLOCK * ROWS, columns), lambda n, at: (n, at[1]))
     sums = pl.BlockSpec((1, tokens, tile), lambda n, at: (at[0], 0, n))
     return pl.pallas_call(
         input_grad_kernel,
+        name="input_grad",
         out_shape=jax.ShapeDtypeStruct(total.shape, F32),
         grid_spec=pltpu.PrefetchScalarGridSpec(
             num_scalar_prefetch=1,
@@ -186,6 +212,7 @@
         specs = specs + [pl.BlockSpec(memory_space=pl.ANY)] * 2
     return pl.pallas_call(
         functools.partial(weight_grads_kernel, parts),
+        name="weight_grads",
         out_shape=(shape, shape),
         grid_spec=pltpu.PrefetchScalarGridSpec(
             num_scalar_prefetch=1,
@@ -199,33 +226,45 @@
     )(at, *operands)
 
 
-def down_grad_kernel(h_ref, g_ref, m_ref, out_ref):
-    parts, _, tokens = h_ref.shape
+def down_grad_kernel(parts, at, *refs):
+    hiddens, grads, m_ref, out_ref = refs[:parts], refs[parts : 2 * parts], refs[2 * parts], refs[-1]
     total = None
-    for t in range(parts):
-        term = jnp.dot(h_ref[t], g_ref[t * tokens : (t + 1) * tokens, :], preferred_element_type=F32)
+    for hidden, grad in zip(hiddens, grads):
+        term = jnp.dot(hidden[...], grad[0], preferred_element_type=F32)
         total = term if total is None else total + term
     out_ref[...] = masked(total.astype(BF16), m_ref[...])
 
 
-def down_grad_of(hidden_t, out_grad, wide, parts):
-    pieces, columns, tokens = hidden_t.shape
-    cuts = pieces // parts
-    count, width = out_grad.shape
+def down_grad_cut(at, hiddens, out_grad, wide, before):
+    parts = len(hiddens)
+    columns, tokens = hiddens[0].shape
+    width = out_grad.shape[2]
     tile = tile_of(width, 512)
-    return pl.pallas_call(
-        down_grad_kernel,
-        out_shape=jax.ShapeDtypeStruct((cuts * columns, width), BF16),
-        grid=(cuts, width // tile),
-        in_specs=[
-            pl.BlockSpec((parts, columns, tokens), lambda i, j: (i, 0, 0)),
-            pl.BlockSpec((count, tile), lambda i, j: (0, j)),
-            pl.BlockSpec((columns // BLOCK * ROWS, tile), lambda i, j: (i, j)),
-        ],
-        out_specs=pl.BlockSpec((columns, tile), lambda i, j: (i, j)),
-        compiler_params=params(),
-        cost_estimate=cost(2 * count * cuts * columns * width, 2 * cuts * columns * width + 2 * out_grad.size),
-    )(hidden_t, out_grad, wide)
+    operands = list(hiddens) + [out_grad] * parts + [wide]
+    specs = [pl.BlockSpec((columns, tokens), lambda j, at: (0, 0))] * parts
+    specs += [
+        pl.BlockSpec((1, tokens, tile), lambda j, at, i=i: (at[1 + i], 0, j)) for i in range(parts)
+    ]
+    specs += [pl.BlockSpec((columns // BLOCK * ROWS, tile), lambda j, at: (at[0], j))]
+    aliases = {}
+    if before is not None:
+        aliases = {1 + len(operands): 0}
+        operands.append(before)
+        specs.append(pl.BlockSpec(memory_space=pl.ANY))
+    return pl.pallas_call(
+        functools.partial(down_grad_kernel, parts),
+        name="down_grad",
+        out_shape=jax.ShapeDtypeStruct((wide.shape[0] // ROWS * BLOCK, width), BF16),
+        grid_spec=pltpu.PrefetchScalarGridSpec(
+            num_scalar_prefetch=1,
+            grid=(width // tile,),
+            in_specs=specs,
+            out_specs=pl.BlockSpec((columns, tile), lambda j, at: (at[0], j)),
+        ),
+        input_output_aliases=aliases,
+        compiler_params=params(),
+        cost_estimate=cost(2 * parts * tokens * columns * width, 2 * columns * width + 2 * out_grad.size),
+    )(at, *operands)
 
 
 def on_device(rows, cols, inputs, out_grad, gate_weight, up_weight, down_weight, gate_mask, up_mask, down_mask):
@@ -263,49 +302,76 @@
     meet_back = [(b, a) for a, b in meet]
 
     gate_wide, up_wide, down_wide = widen(gate_mask), widen(up_mask), widen(down_mask)
-    gate_set, up_set = (gate_weight, gate_wide), (up_weight, up_wide)
-
-    def part(which, shard, came, kind=BF16):
-        return piece(where_is(shard), inputs, *which, came, tokens, columns, kind)
-
     def onward(value):
         return lax.ppermute(value, "row", ahead)
 
     def backward(value):
         return lax.ppermute(value, "row", back)
 
-    gate_on, up_back = part(gate_set, me + far, []), part(up_set, me - far, [])
-    up_on, gate_back = part(up_set, me + near, []), part(gate_set, me - near, [])
-    out_grad, gate_on, up_back, up_on, gate_back = lax.optimization_barrier(
-        (out_grad, gate_on, up_back, up_on, gate_back)
-    )
-    hidden_grad = hidden_grad_partial(out_grad, down_weight, down_wide, parts, columns)
-    hidden_grad = lax.psum_scatter(hidden_grad, "col", scatter_dimension=0, tiled=False)
-    hidden_grad = lax.ppermute(hidden_grad.astype(BF16), ("row", "col"), meet)
+    col = lax.axis_index("col")
+
+    def across(array, bit):
+        return lax.ppermute(array, "col", [(c, c ^ bit) for c in range(cols)])
+
+    terms = {}
+
+    def term(which, offset, kind=F32):
+        offset %= rows
+        if (which, offset) not in terms:
+            weight, wide = {"gate": (gate_weight, gate_wide), "up": (up_weight, up_wide)}[which]
+            offsets = [(offset + cuts * i) % rows for i in range(parts)]
+            at = jnp.stack([where_is(me + offset)[1]] + [where_is(me + o)[0] for o in offsets])
+            kinds = [kind] + [F32] * (parts - 1)
+            values = products(at, inputs, weight, wide, columns, kinds)
+            terms.update({(which, o): value for o, value in zip(offsets, values)})
+        return terms[which, offset]
+
+    def plus(which, offset, came):
+        return (term(which, offset) + came.astype(F32)).astype(BF16)
+
+    gate_on, up_back = term("gate", far, BF16), term("up", -far, BF16)
+    up_on, gate_back = term("up", near, BF16), term("gate", -near, BF16)
+
+    def hidden_grad_of(out_grad):
+        held, *sent = hidden_grad_partial((col % 2)[None], out_grad, down_weight, down_wide, parts, columns)
+        held = held + jnp.stack([across(value, 1) for value in sent]).astype(F32)
+        bit = 2
+        while bit < cols:
+            held = held.reshape(-1, 2, tokens, columns)
+            mine = col // bit % 2
+            sent = lax.dynamic_index_in_dim(held, 1 - mine, 1, keepdims=False).astype(BF16)
+            held = lax.dynamic_index_in_dim(held, mine, 1, keepdims=False) + across(sent, bit).astype(F32)
+            bit *= 2
+        return lax.ppermute(held.reshape(tokens, columns).astype(BF16), ("row", "col"), meet)
+
     for step in range(1, far + 1):
         gate_on, up_back = onward(gate_on), backward(up_back)
         if step <= near:
             up_on, gate_back = onward(up_on), backward(gate_back)
+        if step == 1:
+            out_grad, gate_on, up_back = lax.optimization_barrier((out_grad, gate_on, up_back))
+            hidden_grad = hidden_grad_of(out_grad)
         if step < far:
-            gate_on = part(gate_set, me + far - step, [gate_on])
-            up_back = part(up_set, me - far + step, [up_back])
+            gate_on = plus("gate", far - step, gate_on)
+            up_back = plus("up", step - far, up_back)
         if step < near:
-            up_on = part(up_set, me + near - step, [up_on])
-            gate_back = part(gate_set, me - near + step, [gate_back])
-        if step == near:
-            gate_on, hidden_grad = lax.optimization_barrier((gate_on, hidden_grad))
-    gate = part(gate_set, me, [gate_back, gate_on], F32)
-    up = part(up_set, me, [up_on, up_back], F32)
-
-    hidden_grad = hidden_grad.astype(F32)
-    sig = jax.nn.sigmoid(gate)
-    hidden = (gate * sig * up).astype(BF16)
-    gate_delta = (hidden_grad * up * sig * (1.0 + gate * (1.0 - sig))).astype(BF16)
-    up_delta = (hidden_grad * gate * sig).astype(BF16)
-
-    hidden_t = lax.ppermute(hidden.T, ("row", "col"), meet_back)
-    hidden_t = lax.all_gather(hidden_t, "col", axis=0, tiled=False)
-    down_grad = down_grad_of(hidden_t, out_grad, down_wide, parts)
+            up_on = plus("up", near - step, up_on)
+            gate_back = plus("gate", step - near, gate_back)
+    gate_delta, up_delta, hidden_t = owner(
+        term("gate", 0), gate_on, gate_back, term("up", 0), up_on, up_back, hidden_grad
+    )
+
+    hiddens = {0: lax.ppermute(hidden_t, ("row", "col"), meet_back)}
+    bit = cols // 2
+    while bit:
+        hiddens.update({r ^ bit: across(value, bit) for r, value in list(hiddens.items())})
+        bit //= 2
+    grad_parts = out_grad.reshape(parts, tokens, -1)
+    down_grad = None
+    for cut in range(cols // parts):
+        at = jnp.stack([(col // parts) ^ cut] + [(col % parts) ^ i for i in range(parts)])
+        pieces = [hiddens[cut * parts + i] for i in range(parts)]
+        down_grad = down_grad_cut(at, pieces, grad_parts, down_wide, down_grad)
 
     gates, ups = {0: gate_delta}, {0: up_delta}
     gate_on = gate_back = gate_delta
@@ -336,15 +402,20 @@
         return grads
 
     for step in range(1, far + 1):
+        if step == far:
+            gate_on, total, grads = lax.optimization_barrier((gate_on, total, grads))
+        elif step > 1:
+            up_on, total = lax.optimization_barrier((up_on, total))
+        if step > 1:
+            total = add(add(total, 1 - step), step - 1)
+            grads = column_cuts(grads)
         gate_on, up_back = onward(gate_on), backward(up_back)
         gates[-step % rows], ups[step % rows] = gate_on, up_back
         if step <= near:
             up_on, gate_back = onward(up_on), backward(gate_back)
             ups[-step % rows], gates[step % rows] = up_on, gate_back
-            total = add(total, -step)
-            total = add(total, step)
-            grads = column_cuts(grads)
-
+
+    total, gates[-far % rows], ups[far] = lax.optimization_barrier((total, gates[-far % rows], ups[far]))
     late = where_is(me - far)[0]
     others = [lax.rem(late + 1 + i, parts) for i in range(parts - 1)]
     early = [lax.dynamic_index_in_dim(total, o, 0, keepdims=False) for o in others]

time: 434 us -> 359 us (0.83); the launches traced: 426 us -> 357 us
  Pallas kernels: 192 us -> 147 us
  starting transfers between devices: 100 us -> 62.9 us
  waiting for transfers between devices: 76.9 us -> 106 us
  between operations: 21.6 us -> 9.1 us
  local copies, waits for them, and re-layouts: 22.3 us -> 16.7 us
    pallas_call x30 -> x24, Pallas kernels: 192 us -> 147 us  [the longest x8 45.3 us: add_input_grad(): pl.pallas_call(input_grad_kernel, name='input_grad', out_shape=jax.ShapeD...]
    ppermute x14, starting transfers between devices: 71.9 us -> 46.3 us  [onward(): return lax.ppermute(value, 'row', ahead)]
    ppermute x14, waiting for transfers between devices: 49.1 us -> 62.7 us  [backward(): return lax.ppermute(value, 'row', back)]
    ppermute x2, waiting for transfers between devices: 2.27 us -> 15.4 us  [the longest x1 15.4 us: hidden_grad_of(): lax.ppermute(held.reshape(tokens, columns).astype(BF16), ('row', 'col'),...]
    ppermute x2, starting transfers between devices: 15.6 us -> 7.06 us  [the longest x1 5.15 us: hidden_grad_of(): lax.ppermute(held.reshape(tokens, columns).astype(BF16), ('row', 'col'),...]
    convert_element_type x1 -> x11, other arithmetic: 2.31 us -> 10 us  [the longest x10 9.88 us: plus(): return (term(which, offset) + came.astype(F32)).astype(BF16)]
    ppermute x6 -> x12, starting transfers between devices: 9.83 us -> 8.24 us  [across(): return lax.ppermute(array, 'col', [(c, c ^ bit) for c in range(cols)])]
  transfers between devices with their start and end apart: 38 -> 42, of which waited for: 14 -> 17; matrix products, arithmetic and copies ran while one was open for 4% -> 7% of each run, Pallas kernels for 33% -> 38%
where the time goes in v2:
time: 359 us; the launch traced here: 357 us
  Pallas kernels  147 us (41%)
  waiting for transfers between devices  106 us (30%)
  starting transfers between devices  62.9 us (18%)
  local copies, waits for them, and re-layouts  16.7 us (5%)
  other arithmetic  15.4 us (4%)
  between operations  9.1 us (3%)
    ppermute x14, waiting for transfers between devices, backward(): return lax.ppermute(value, 'row', back)  62.7 us
    ppermute x14, starting transfers between devices, onward(): return lax.ppermute(value, 'row', ahead)  46.3 us
    pallas_call x8, Pallas kernels, add_input_grad(): pl.pallas_call(input_grad_kernel, name='input_grad', out_shape=jax.ShapeD...  45.3 us
    pallas_call x8, Pallas kernels, products(): pl.pallas_call(functools.partial(product_kernel, parts), name='products',...  34.8 us
    pallas_call x4, Pallas kernels, weight_grads(): pl.pallas_call(functools.partial(weight_grads_kernel, parts), name='weigh...  32.8 us
    ppermute x14, waiting for transfers between devices, onward(): return lax.ppermute(value, 'row', ahead)  27.2 us
    pallas_call x2, Pallas kernels, down_grad_cut(): pl.pallas_call(functools.partial(down_grad_kernel, parts), name='down_gra...  15.8 us
    ppermute x1, waiting for transfers between devices, hidden_grad_of(): lax.ppermute(held.reshape(tokens, columns).astype(BF16), ('row', 'col'),...  15.4 us
  transfers between devices with their start and end apart: 42, of which 17 were waited for; matrix products, arithmetic and copies ran while one was open for 7% of the time, Pallas kernels for 38%

profile of v2, /device:TPU:9, one launch (start us, length us, event | category | flops | bytes accessed | tf_op | source)
XLA Modules:
  0.0 356.9 jit_solution(8592702108639093546)
XLA Ops:
  60.9 11.5 %hidden_grad.1 = (f32[2,1,384,896]{3,2,1,0:T(8,128)}, bf16[1,384,896]{2,1,0:T(8,128)(2,1)S(1)}, bf16[1,384,896]{2,1,0:T(8,128)(2,1)S(1)}) custom-call(s32[1]{0:T(128)} %bitcast.28.at, bf16[768,2048]{1,0:T(8,128)(2,1)} %g_ref, bf16[1792,2048]{1,0:T(8,128)(2,1)} %w_ref.17, bf16[224,2048]{1,0:T(8,128)(2,1)S(1)} %bitcast.117), custom_call_target="tpu_custom_call" | custom-call | flops 5637144576 | bytes 15990784 | tf_op jit(solution)/shard_map/hidden_grad/pallas_call | solution.py:135
  77.1 7.6 %collective-permute-done.11 = bf16[384,896]{1,0:T(8,128)(2,1)} collective-permute-done((bf16[384,896]{1,0:T(8,128)(2,1)}, bf16[384,896]{1,0:T(8,128)(2,1)}, u32[]{:S(2)}, u32[]{:S(2)}) %collective-permute-start.11) | collective-permute-done | bytes 688160 | tf_op jit(solution)/shard_map/ppermute | solution.py:309
  90.7 6.3 %collective-permute-done.3 = bf16[384,896]{1,0:T(8,128)(2,1)S(1)} collective-permute-done((bf16[384,896]{1,0:T(8,128)(2,1)S(1)}, bf16[384,896]{1,0:T(8,128)(2,1)S(1)}, u32[]{:S(2)}, u32[]{:S(2)}) %collective-permute-start.3) | collective-permute-done | bytes 688160 | tf_op jit(solution)/shard_map/ppermute | solution.py:306
  98.5 14.8 %collective-permute-done.12 = bf16[384,896]{1,0:T(8,128)(2,1)S(1)} collective-permute-done((bf16[384,896]{1,0:T(8,128)(2,1)S(1)}, bf16[384,896]{1,0:T(8,128)(2,1)S(1)}, u32[]{:S(2)}, u32[]{:S(2)}) %collective-permute-start.12) | collective-permute-done | bytes 688160 | tf_op jit(solution)/shard_map/ppermute | solution.py:309
  113.9 5.1 %collective-permute-start.17 = (bf16[384,896]{1,0:T(8,128)(2,1)S(1)}, bf16[384,896]{1,0:T(8,128)(2,1)S(1)}, u32[]{:S(2)}, u32[]{:S(2)}) collective-permute-start(bf16[384,896]{1,0:T(8,128)(2,1)S(1)} %fusion.6), channel_id=1, source_target_pairs={{0,0},{1,28},{2,8},{3,20},{4,16},{5,12},{6,24},{7,4},{8,1},{9,29},... | collective-permute-start | bytes 2064392 | tf_op jit(solution)/shard_map/ppermute | solution.py:345
  119.1 7.4 %collective-permute-done.4.gate_on = bf16[384,896]{1,0:T(8,128)(2,1)S(1)} collective-permute-done((bf16[384,896]{1,0:T(8,128)(2,1)S(1)}, bf16[384,896]{1,0:T(8,128)(2,1)S(1)}, u32[]{:S(2)}, u32[]{:S(2)}) %collective-permute-start.4) | collective-permute-done | bytes 688160 | tf_op jit(solution)/shard_map/ppermute | solution.py:306
  127.2 15.4 %collective-permute-done.17.hg_ref = bf16[384,896]{1,0:T(8,128)(2,1)S(1)} collective-permute-done((bf16[384,896]{1,0:T(8,128)(2,1)S(1)}, bf16[384,896]{1,0:T(8,128)(2,1)S(1)}, u32[]{:S(2)}, u32[]{:S(2)}) %collective-permute-start.17) | collective-permute-done | bytes 688160 | tf_op jit(solution)/shard_map/ppermute | solution.py:345
  143.5 6.4 %owner.1 = (bf16[384,896]{1,0:T(8,128)(2,1)S(1)}, bf16[384,896]{1,0:T(8,128)(2,1)}, bf16[896,384]{1,0:T(8,128)(2,1)}) custom-call(f32[384,896]{1,0:T(8,128)} %copy-done.2, bf16[384,896]{1,0:T(8,128)(2,1)S(1)} %collective-permute-done.4.gate_on, bf16[384,896]{1,0:T(8,128)(2,1)S(1)} %collective-permute-done.7.gate_back, f32[384,896]{1,0:T(8,128)} %copy-done.3, ...), custom_call_target="tpu_custom_call" | custom-call | bytes 8257536 | tf_op jit(solution)/shard_map/owner/pallas_call | solution.py:98
  149.9 12.0 %collective-permute-start.18 = (bf16[384,896]{1,0:T(8,128)(2,1)S(1)}, bf16[384,896]{1,0:T(8,128)(2,1)}, u32[]{:S(2)}, u32[]{:S(2)}) collective-permute-start(bf16[384,896]{1,0:T(8,128)(2,1)S(1)} %get-tuple-element.70.gd_ref.refs_2_), channel_id=1, source_target_pairs={{0,8},{8,16},{16,24},{24,28},{28,20},{20,12},{12,4},{4,0},{1,9},{9... | collective-permute-start | bytes 2064392 | tf_op jit(solution)/shard_map/ppermute | solution.py:306
  161.9 5.2 %collective-permute-start.21 = (bf16[384,896]{1,0:T(8,128)(2,1)}, bf16[384,896]{1,0:T(8,128)(2,1)}, u32[]{:S(2)}, u32[]{:S(2)}) collective-permute-start(bf16[384,896]{1,0:T(8,128)(2,1)} %get-tuple-element.71.ud_ref.refs_4_), channel_id=1, source_target_pairs={{0,8},{8,16},{16,24},{24,28},{28,20},{20,12},{12,4},{4,0},{1,9},{9... | collective-permute-start | bytes 2064392 | tf_op jit(solution)/shard_map/ppermute | solution.py:306
  171.0 6.2 %collective-permute-done.18.gd_ref.refs_3_ = bf16[384,896]{1,0:T(8,128)(2,1)} collective-permute-done((bf16[384,896]{1,0:T(8,128)(2,1)S(1)}, bf16[384,896]{1,0:T(8,128)(2,1)}, u32[]{:S(2)}, u32[]{:S(2)}) %collective-permute-start.18) | collective-permute-done | bytes 688160 | tf_op jit(solution)/shard_map/ppermute | solution.py:306
  177.2 5.2 %collective-permute-start.19 = (bf16[384,896]{1,0:T(8,128)(2,1)}, bf16[384,896]{1,0:T(8,128)(2,1)S(1)}, u32[]{:S(2)}, u32[]{:S(2)}) collective-permute-start(bf16[384,896]{1,0:T(8,128)(2,1)} %collective-permute-done.18.gd_ref.refs_3_), channel_id=1, source_target_pairs={{0,8},{8,16},{16,24},{24,28},{28,20},{20,12},{12,4},{4,0},{1,9},{9... | collective-permute-start | bytes 2064392 | tf_op jit(solution)/shard_map/ppermute | solution.py:306
  185.6 5.5 %input_grad.8.sum_ref = f32[2,384,1024]{2,1,0:T(8,128)} custom-call(s32[2]{0:T(128)S(1)} %pad_add_fusion.9.at, f32[2,384,1024]{2,1,0:T(8,128)} %broadcast_in_dim.42.sum_ref, bf16[384,896]{1,0:T(8,128)(2,1)S(1)} %get-tuple-element.70.gd_ref.refs_2_, bf16[384,896]{1,0:T(8,128)(2,1)} %get-tuple-element.71.ud_ref.refs_4_, ...), custom_call_target="tpu_custom_call", output_to_operand_aliasing={{}: (1, {})} | custom-call | flops 1409286144 | bytes 6815744 | tf_op jit(solution)/shard_map/input_grad/pallas_call | solution.py:168
  192.0 5.2 %collective-permute-start.22 = (bf16[384,896]{1,0:T(8,128)(2,1)}, bf16[384,896]{1,0:T(8,128)(2,1)}, u32[]{:S(2)}, u32[]{:S(2)}) collective-permute-start(bf16[384,896]{1,0:T(8,128)(2,1)} %collective-permute-done.21.ud_ref.refs_5_), channel_id=1, source_target_pairs={{0,8},{8,16},{16,24},{24,28},{28,20},{20,12},{12,4},{4,0},{1,9},{9... | collective-permute-start | bytes 2064392 | tf_op jit(solution)/shard_map/ppermute | solution.py:306
  200.3 6.4 %collective-permute-done.19.gd_ref.refs_3_ = bf16[384,896]{1,0:T(8,128)(2,1)S(1)} collective-permute-done((bf16[384,896]{1,0:T(8,128)(2,1)}, bf16[384,896]{1,0:T(8,128)(2,1)S(1)}, u32[]{:S(2)}, u32[]{:S(2)}) %collective-permute-start.19) | collective-permute-done | bytes 688160 | tf_op jit(solution)/shard_map/ppermute | solution.py:306
  206.8 5.2 %collective-permute-start.20 = (bf16[384,896]{1,0:T(8,128)(2,1)S(1)}, bf16[384,896]{1,0:T(8,128)(2,1)}, u32[]{:S(2)}, u32[]{:S(2)}) collective-permute-start(bf16[384,896]{1,0:T(8,128)(2,1)S(1)} %collective-permute-done.19.gd_ref.refs_3_), channel_id=1, source_target_pairs={{0,8},{8,16},{16,24},{24,28},{28,20},{20,12},{12,4},{4,0},{1,9},{9... | collective-permute-start | bytes 2064392 | tf_op jit(solution)/shard_map/ppermute | solution.py:306
  213.0 5.8 %input_grad.9.sum_ref = f32[2,384,1024]{2,1,0:T(8,128)} custom-call(s32[2]{0:T(128)S(1)} %pad_add_fusion.11.at, f32[2,384,1024]{2,1,0:T(8,128)} %input_grad.8.sum_ref, bf16[384,896]{1,0:T(8,128)(2,1)} %collective-permute-done.18.gd_ref.refs_3_, bf16[384,896]{1,0:T(8,128)(2,1)} %collective-permute-done.21.ud_ref.refs_5_, ...), custom_call_target="tpu_custom_call", output_to_operand_aliasing={{}: (1, {})} | custom-call | flops 1409286144 | bytes 6815744 | tf_op jit(solution)/shard_map/input_grad/pallas_call | solution.py:168
  218.8 5.7 %input_grad.10.sum_ref = f32[2,384,1024]{2,1,0:T(8,128)} custom-call(s32[2]{0:T(128)S(1)} %pad_add_fusion.10.at, f32[2,384,1024]{2,1,0:T(8,128)} %input_grad.9.sum_ref, bf16[384,896]{1,0:T(8,128)(2,1)} %collective-permute-done.23.gd_ref.refs_2_, bf16[384,896]{1,0:T(8,128)(2,1)} %collective-permute-done.24.ud_ref.refs_4_, ...), custom_call_target="tpu_custom_call", output_to_operand_aliasing={{}: (1, {})} | custom-call | flops 1409286144 | bytes 6815744 | tf_op jit(solution)/shard_map/input_grad/pallas_call | solution.py:168
  226.8 14.5 %collective-permute-done.25.gd_ref.refs_2_ = bf16[384,896]{1,0:T(8,128)(2,1)} collective-permute-done((bf16[384,896]{1,0:T(8,128)(2,1)}, bf16[384,896]{1,0:T(8,128)(2,1)}, u32[]{:S(2)}, u32[]{:S(2)}) %collective-permute-start.25) | collective-permute-done | bytes 688160 | tf_op jit(solution)/shard_map/ppermute | solution.py:309
  241.2 8.0 %weight_grads.4 = (bf16[1024,3584]{1,0:T(8,128)(2,1)}, bf16[1024,3584]{1,0:T(8,128)(2,1)}) custom-call(s32[3]{0:T(128)S(1)} %pad_add_fusion.6.at, bf16[2,1024,384]{2,1,0:T(8,128)(2,1)} %bitcast.121, bf16[2,1024,384]{2,1,0:T(8,128)(2,1)} %bitcast.122, bf16[384,896]{1,0:T(8,128)(2,1)} %collective-permute-done.25.gd_ref.refs_2_, ...), custom_call_target="tpu_custom_call" | custom-call | flops 2818572288 | bytes 6422528 | tf_op jit(solution)/shard_map/weight_grads/pallas_call | solution.py:213
  249.2 5.5 %input_grad.11.sum_ref = f32[2,384,1024]{2,1,0:T(8,128)} custom-call(s32[2]{0:T(128)S(1)} %pad_add_fusion.8.at, f32[2,384,1024]{2,1,0:T(8,128)} %input_grad.10.sum_ref, bf16[384,896]{1,0:T(8,128)(2,1)S(1)} %collective-permute-done.19.gd_ref.refs_3_, bf16[384,896]{1,0:T(8,128)(2,1)} %collective-permute-done.22.ud_ref.refs_5_, ...), custom_call_target="tpu_custom_call", output_to_operand_aliasing={{}: (1, {})} | custom-call | flops 1409286144 | bytes 6815744 | tf_op jit(solution)/shard_map/input_grad/pallas_call | solution.py:168
  254.8 5.6 %input_grad.12.sum_ref = f32[2,384,1024]{2,1,0:T(8,128)} custom-call(s32[2]{0:T(128)S(1)} %pad_add_fusion.7.at, f32[2,384,1024]{2,1,0:T(8,128)} %input_grad.11.sum_ref, bf16[384,896]{1,0:T(8,128)(2,1)} %collective-permute-done.25.gd_ref.refs_2_, bf16[384,896]{1,0:T(8,128)(2,1)S(1)} %collective-permute-done.26.ud_ref.refs_4_, ...), custom_call_target="tpu_custom_call", output_to_operand_aliasing={{}: (1, {})} | custom-call | flops 1409286144 | bytes 6815744 | tf_op jit(solution)/shard_map/input_grad/pallas_call | solution.py:168
  261.9 10.1 %collective-permute-done.29.ud_ref.refs_4_ = bf16[384,896]{1,0:T(8,128)(2,1)} collective-permute-done((bf16[384,896]{1,0:T(8,128)(2,1)S(1)}, bf16[384,896]{1,0:T(8,128)(2,1)}, u32[]{:S(2)}, u32[]{:S(2)}) %collective-permute-start.29) | collective-permute-done | bytes 688160 | tf_op jit(solution)/shard_map/ppermute | solution.py:309
  273.6 5.7 %input_grad.13.sum_ref = f32[2,384,1024]{2,1,0:T(8,128)} custom-call(s32[2]{0:T(128)S(1)} %pad_add_fusion.1.at, f32[2,384,1024]{2,1,0:T(8,128)} %input_grad.12.sum_ref, bf16[384,896]{1,0:T(8,128)(2,1)} %collective-permute-done.20.gd_ref.refs_3_, bf16[384,896]{1,0:T(8,128)(2,1)} %collective-permute-done.27.ud_ref.refs_5_, ...), custom_call_target="tpu_custom_call", output_to_operand_aliasing={{}: (1, {})} | custom-call | flops 1409286144 | bytes 6815744 | tf_op jit(solution)/shard_map/input_grad/pallas_call | solution.py:168
  279.3 7.4 %collective-permute-done.28.gd_ref.refs_2_ = bf16[384,896]{1,0:T(8,128)(2,1)} collective-permute-done((bf16[384,896]{1,0:T(8,128)(2,1)}, bf16[384,896]{1,0:T(8,128)(2,1)}, u32[]{:S(2)}, u32[]{:S(2)}) %collective-permute-start.28) | collective-permute-done | bytes 688160 | tf_op jit(solution)/shard_map/ppermute | solution.py:309
  286.7 5.7 %input_grad.14.sum_ref = f32[2,384,1024]{2,1,0:T(8,128)} custom-call(s32[2]{0:T(128)S(1)} %pad_add_fusion.at, f32[2,384,1024]{2,1,0:T(8,128)} %input_grad.13.sum_ref, bf16[384,896]{1,0:T(8,128)(2,1)} %collective-permute-done.28.gd_ref.refs_2_, bf16[384,896]{1,0:T(8,128)(2,1)} %collective-permute-done.29.ud_ref.refs_4_, ...), custom_call_target="tpu_custom_call", output_to_operand_aliasing={{}: (1, {})} | custom-call | flops 1409286144 | bytes 6815744 | tf_op jit(solution)/shard_map/input_grad/pallas_call | solution.py:168
  300.1 8.0 %down_grad.2.refs_5_ = bf16[1792,2048]{1,0:T(8,128)(2,1)} custom-call(s32[3]{0:T(128)S(1)} %get-tuple-element.101.at, bf16[896,384]{1,0:T(8,128)(2,1)} %collective-permute-done.38.refs_0_, bf16[896,384]{1,0:T(8,128)(2,1)} %collective-permute-done.41.refs_1_, bf16[2,384,2048]{2,1,0:T(8,128)(2,1)} %bitcast.129, bf16[2,384,2048]{2,1,0:T(8,128)(2,1)} %bitcast.130, ...), custom_call_target="tpu_custom_call" | custom-call | flops 2818572288 | bytes 6815744 | tf_op jit(solution)/shard_map/down_grad/pallas_call | solution.py:254
  309.6 5.7 %input_grad.15 = f32[2,384,1024]{2,1,0:T(8,128)} custom-call(s32[2]{0:T(128)S(1)} %pad_add_fusion.12.at, f32[2,384,1024]{2,1,0:T(8,128)} %input_grad.14.sum_ref, bf16[384,896]{1,0:T(8,128)(2,1)} %collective-permute-done.30.gd_ref.refs_3_, bf16[384,896]{1,0:T(8,128)(2,1)} %collective-permute-done.31.ud_ref.refs_5_, ...), custom_call_target="tpu_custom_call", output_to_operand_aliasing={{}: (1, {})} | custom-call | flops 1409286144 | bytes 6815744 | tf_op jit(solution)/shard_map/input_grad/pallas_call | solution.py:168
  316.7 8.4 %weight_grads.5 = (bf16[1024,3584]{1,0:T(8,128)(2,1)}, bf16[1024,3584]{1,0:T(8,128)(2,1)}) custom-call(s32[3]{0:T(128)S(1)} %pad_add_fusion.14.at, bf16[2,1024,384]{2,1,0:T(8,128)(2,1)} %bitcast.123, bf16[2,1024,384]{2,1,0:T(8,128)(2,1)} %bitcast.124, ...), custom_call_target="tpu_custom_call", output_to_operand_aliasing={{0}: (9, {}), {1}: (10, {})} | custom-call | flops 2818572288 | bytes 6422528 | tf_op jit(solution)/shard_map/weight_grads/pallas_call | solution.py:213
  325.0 8.4 %weight_grads.6 = (bf16[1024,3584]{1,0:T(8,128)(2,1)}, bf16[1024,3584]{1,0:T(8,128)(2,1)}) custom-call(s32[3]{0:T(128)S(1)} %get-tuple-element.99.at, bf16[2,1024,384]{2,1,0:T(8,128)(2,1)} %bitcast.125, bf16[2,1024,384]{2,1,0:T(8,128)(2,1)} %bitcast.126, ...), custom_call_target="tpu_custom_call", output_to_operand_aliasing={{0}: (9, {}), {1}: (10, {})} | custom-call | flops 2818572288 | bytes 6422528 | tf_op jit(solution)/shard_map/weight_grads/pallas_call | solution.py:213
  333.4 7.8 %down_grad.3 = bf16[1792,2048]{1,0:T(8,128)(2,1)} custom-call(s32[3]{0:T(128)S(1)} %get-tuple-element.100.at, bf16[896,384]{1,0:T(8,128)(2,1)} %collective-permute-done.39.refs_0_, bf16[896,384]{1,0:T(8,128)(2,1)S(1)} %collective-permute-done.40.refs_1_, bf16[2,384,2048]{2,1,0:T(8,128)(2,1)} %bitcast.131, ...), custom_call_target="tpu_custom_call", output_to_operand_aliasing={{}: (6, {})} | custom-call | flops 2818572288 | bytes 6815744 | tf_op jit(solution)/shard_map/down_grad/pallas_call | solution.py:254
  345.2 8.1 %weight_grads.7 = (bf16[1024,3584]{1,0:T(8,128)(2,1)}, bf16[1024,3584]{1,0:T(8,128)(2,1)}) custom-call(s32[3]{0:T(128)S(1)} %pad_add_fusion.13.at, bf16[2,1024,384]{2,1,0:T(8,128)(2,1)} %bitcast.127, bf16[2,1024,384]{2,1,0:T(8,128)(2,1)} %bitcast.128, ...), custom_call_target="tpu_custom_call", output_to_operand_aliasing={{0}: (9, {}), {1}: (10, {})} | custom-call | flops 2818572288 | bytes 6422528 | tf_op jit(solution)/shard_map/weight_grads/pallas_call | solution.py:213
  (158 shorter events, 101.8 us)
Async XLA Ops:
  11.1 39.9 %collective-permute-start = (bf16[384,896]{1,0:T(8,128)(2,1)}, bf16[384,896]{1,0:T(8,128)(2,1)}, u32[]{:S(2)}, u32[]{:S(2)}) collective-permute-start(bf16[384,896]{1,0:T(8,128)(2,1)} %get-tuple-element.52), channel_id=1, source_target_pairs={{0,8},{8,16},{16,24},{24,28},{28,20},{20,12},{12,4},{4,0},{1,9},{9... | collective-permute-start | bytes 2064392 | tf_op jit(solution)/shard_map/ppermute | solution.py:306
  18.1 32.9 %collective-permute-start.1 = (bf16[384,896]{1,0:T(8,128)(2,1)}, bf16[384,896]{1,0:T(8,128)(2,1)}, u32[]{:S(2)}, u32[]{:S(2)}) collective-permute-start(bf16[384,896]{1,0:T(8,128)(2,1)} %get-tuple-element.53), channel_id=1, source_target_pairs={{8,0},{16,8},{24,16},{28,24},{20,28},{12,20},{4,12},{0,4},{9,1},{1... | collective-permute-start | bytes 2064392 | tf_op jit(solution)/shard_map/ppermute | solution.py:309
  23.8 29.9 %collective-permute-start.5 = (bf16[384,896]{1,0:T(8,128)(2,1)}, bf16[384,896]{1,0:T(8,128)(2,1)}, u32[]{:S(2)}, u32[]{:S(2)}) collective-permute-start(bf16[384,896]{1,0:T(8,128)(2,1)} %get-tuple-element.57), channel_id=1, source_target_pairs={{8,0},{16,8},{24,16},{28,24},{20,28},{12,20},{4,12},{0,4},{9,1},{1... | collective-permute-start | bytes 2064392 | tf_op jit(solution)/shard_map/ppermute | solution.py:309
  32.0 23.1 %collective-permute-start.8 = (bf16[384,896]{1,0:T(8,128)(2,1)}, bf16[384,896]{1,0:T(8,128)(2,1)}, u32[]{:S(2)}, u32[]{:S(2)}) collective-permute-start(bf16[384,896]{1,0:T(8,128)(2,1)} %get-tuple-element.61), channel_id=1, source_target_pairs={{0,8},{8,16},{16,24},{24,28},{28,20},{20,12},{12,4},{4,0},{1,9},{9... | collective-permute-start | bytes 2064392 | tf_op jit(solution)/shard_map/ppermute | solution.py:306
  52.3 23.0 %collective-permute-start.2 = (bf16[384,896]{1,0:T(8,128)(2,1)S(1)}, bf16[384,896]{1,0:T(8,128)(2,1)S(1)}, u32[]{:S(2)}, u32[]{:S(2)}) collective-permute-start(bf16[384,896]{1,0:T(8,128)(2,1)S(1)} %add_convert_fusion.9), channel_id=1, source_target_pairs={{0,8},{8,16},{16,24},{24,28},{28,20},{20,12},{12,4},{4,0},{1,9},{9... | collective-permute-start | bytes 2064392 | tf_op jit(solution)/shard_map/ppermute | solution.py:306
  57.2 30.8 %collective-permute-start.9 = (bf16[384,896]{1,0:T(8,128)(2,1)}, bf16[384,896]{1,0:T(8,128)(2,1)}, u32[]{:S(2)}, u32[]{:S(2)}) collective-permute-start(bf16[384,896]{1,0:T(8,128)(2,1)} %add_convert_fusion.4), channel_id=1, source_target_pairs={{0,8},{8,16},{16,24},{24,28},{28,20},{20,12},{12,4},{4,0},{1,9},{9... | collective-permute-start | bytes 2064392 | tf_op jit(solution)/shard_map/ppermute | solution.py:306
  60.7 24.0 %collective-permute-start.11 = (bf16[384,896]{1,0:T(8,128)(2,1)}, bf16[384,896]{1,0:T(8,128)(2,1)}, u32[]{:S(2)}, u32[]{:S(2)}) collective-permute-start(bf16[384,896]{1,0:T(8,128)(2,1)} %add_convert_fusion.2), channel_id=1, source_target_pairs={{8,0},{16,8},{24,16},{28,24},{20,28},{12,20},{4,12},{0,4},{9,1},{1... | collective-permute-start | bytes 2064392 | tf_op jit(solution)/shard_map/ppermute | solution.py:309
  84.7 34.4 %collective-permute-start.7 = (bf16[384,896]{1,0:T(8,128)(2,1)S(1)}, bf16[384,896]{1,0:T(8,128)(2,1)S(1)}, u32[]{:S(2)}, u32[]{:S(2)}) collective-permute-start(bf16[384,896]{1,0:T(8,128)(2,1)S(1)} %add_convert_fusion.5), channel_id=1, source_target_pairs={{8,0},{16,8},{24,16},{28,24},{20,28},{12,20},{4,12},{0,4},{9,1},{1... | collective-permute-start | bytes 2064392 | tf_op jit(solution)/shard_map/ppermute | solution.py:309
  86.1 27.2 %collective-permute-start.12 = (bf16[384,896]{1,0:T(8,128)(2,1)S(1)}, bf16[384,896]{1,0:T(8,128)(2,1)S(1)}, u32[]{:S(2)}, u32[]{:S(2)}) collective-permute-start(bf16[384,896]{1,0:T(8,128)(2,1)S(1)} %add_convert_fusion.1), channel_id=1, source_target_pairs={{8,0},{16,8},{24,16},{28,24},{20,28},{12,20},{4,12},{0,4},{9,1},{1... | collective-permute-start | bytes 2064392 | tf_op jit(solution)/shard_map/ppermute | solution.py:309
  86.9 26.9 %collective-permute-start.16 = (bf16[1,384,896]{2,1,0:T(8,128)(2,1)S(1)}, bf16[1,384,896]{2,1,0:T(8,128)(2,1)S(1)}, u32[]{:S(2)}, u32[]{:S(2)}) collective-permute-start(bf16[1,384,896]{2,1,0:T(8,128)(2,1)S(1)} %fusion.5), channel_id=1, source_target_pairs={{0,2},{1,3},{2,0},{3,1},{4,6},{5,7},{6,4},{7,5},{8,10},{9,11},{10,... | collective-permute-start | bytes 2064392 | tf_op jit(solution)/shard_map/ppermute | solution.py:314
  89.3 29.7 %collective-permute-start.10 = (bf16[384,896]{1,0:T(8,128)(2,1)S(1)}, bf16[384,896]{1,0:T(8,128)(2,1)S(1)}, u32[]{:S(2)}, u32[]{:S(2)}) collective-permute-start(bf16[384,896]{1,0:T(8,128)(2,1)S(1)} %add_convert_fusion.3), channel_id=1, source_target_pairs={{0,8},{8,16},{16,24},{24,28},{28,20},{20,12},{12,4},{4,0},{1,9},{9... | collective-permute-start | bytes 2064392 | tf_op jit(solution)/shard_map/ppermute | solution.py:306
  97.2 29.3 %collective-permute-start.4 = (bf16[384,896]{1,0:T(8,128)(2,1)S(1)}, bf16[384,896]{1,0:T(8,128)(2,1)S(1)}, u32[]{:S(2)}, u32[]{:S(2)}) collective-permute-start(bf16[384,896]{1,0:T(8,128)(2,1)S(1)} %add_convert_fusion.7), channel_id=1, source_target_pairs={{0,8},{8,16},{16,24},{24,28},{28,20},{20,12},{12,4},{4,0},{1,9},{9... | collective-permute-start | bytes 2064392 | tf_op jit(solution)/shard_map/ppermute | solution.py:306
  113.9 28.7 %collective-permute-start.17 = (bf16[384,896]{1,0:T(8,128)(2,1)S(1)}, bf16[384,896]{1,0:T(8,128)(2,1)S(1)}, u32[]{:S(2)}, u32[]{:S(2)}) collective-permute-start(bf16[384,896]{1,0:T(8,128)(2,1)S(1)} %fusion.6), channel_id=1, source_target_pairs={{0,0},{1,28},{2,8},{3,20},{4,16},{5,12},{6,24},{7,4},{8,1},{9,29},... | collective-permute-start | bytes 2064392 | tf_op jit(solution)/shard_map/ppermute | solution.py:345
  149.9 27.3 %collective-permute-start.18 = (bf16[384,896]{1,0:T(8,128)(2,1)S(1)}, bf16[384,896]{1,0:T(8,128)(2,1)}, u32[]{:S(2)}, u32[]{:S(2)}) collective-permute-start(bf16[384,896]{1,0:T(8,128)(2,1)S(1)} %get-tuple-element.70.gd_ref.refs_2_), channel_id=1, source_target_pairs={{0,8},{8,16},{16,24},{24,28},{28,20},{20,12},{12,4},{4,0},{1,9},{9... | collective-permute-start | bytes 2064392 | tf_op jit(solution)/shard_map/ppermute | solution.py:306
  161.9 21.6 %collective-permute-start.24 = (bf16[384,896]{1,0:T(8,128)(2,1)}, bf16[384,896]{1,0:T(8,128)(2,1)}, u32[]{:S(2)}, u32[]{:S(2)}) collective-permute-start(bf16[384,896]{1,0:T(8,128)(2,1)} %get-tuple-element.71.ud_ref.refs_4_), channel_id=1, source_target_pairs={{8,0},{16,8},{24,16},{28,24},{20,28},{12,20},{4,12},{0,4},{9,1},{1... | collective-permute-start | bytes 2064392 | tf_op jit(solution)/shard_map/ppermute | solution.py:309
  161.9 30.2 %collective-permute-start.21 = (bf16[384,896]{1,0:T(8,128)(2,1)}, bf16[384,896]{1,0:T(8,128)(2,1)}, u32[]{:S(2)}, u32[]{:S(2)}) collective-permute-start(bf16[384,896]{1,0:T(8,128)(2,1)} %get-tuple-element.71.ud_ref.refs_4_), channel_id=1, source_target_pairs={{0,8},{8,16},{16,24},{24,28},{28,20},{20,12},{12,4},{4,0},{1,9},{9... | collective-permute-start | bytes 2064392 | tf_op jit(solution)/shard_map/ppermute | solution.py:306
  167.1 31.0 %collective-permute-start.23 = (bf16[384,896]{1,0:T(8,128)(2,1)S(1)}, bf16[384,896]{1,0:T(8,128)(2,1)}, u32[]{:S(2)}, u32[]{:S(2)}) collective-permute-start(bf16[384,896]{1,0:T(8,128)(2,1)S(1)} %get-tuple-element.70.gd_ref.refs_2_), channel_id=1, source_target_pairs={{8,0},{16,8},{24,16},{28,24},{20,28},{12,20},{4,12},{0,4},{9,1},{1... | collective-permute-start | bytes 2064392 | tf_op jit(solution)/shard_map/ppermute | solution.py:309
  177.2 29.6 %collective-permute-start.19 = (bf16[384,896]{1,0:T(8,128)(2,1)}, bf16[384,896]{1,0:T(8,128)(2,1)S(1)}, u32[]{:S(2)}, u32[]{:S(2)}) collective-permute-start(bf16[384,896]{1,0:T(8,128)(2,1)} %collective-permute-done.18.gd_ref.refs_3_), channel_id=1, source_target_pairs={{0,8},{8,16},{16,24},{24,28},{28,20},{20,12},{12,4},{4,0},{1,9},{9... | collective-permute-start | bytes 2064392 | tf_op jit(solution)/shard_map/ppermute | solution.py:306
  183.5 29.5 %collective-permute-start.26 = (bf16[384,896]{1,0:T(8,128)(2,1)}, bf16[384,896]{1,0:T(8,128)(2,1)S(1)}, u32[]{:S(2)}, u32[]{:S(2)}) collective-permute-start(bf16[384,896]{1,0:T(8,128)(2,1)} %collective-permute-done.24.ud_ref.refs_4_), channel_id=1, source_target_pairs={{8,0},{16,8},{24,16},{28,24},{20,28},{12,20},{4,12},{0,4},{9,1},{1... | collective-permute-start | bytes 2064392 | tf_op jit(solution)/shard_map/ppermute | solution.py:309
  192.0 32.5 %collective-permute-start.22 = (bf16[384,896]{1,0:T(8,128)(2,1)}, bf16[384,896]{1,0:T(8,128)(2,1)}, u32[]{:S(2)}, u32[]{:S(2)}) collective-permute-start(bf16[384,896]{1,0:T(8,128)(2,1)} %collective-permute-done.21.ud_ref.refs_5_), channel_id=1, source_target_pairs={{0,8},{8,16},{16,24},{24,28},{28,20},{20,12},{12,4},{4,0},{1,9},{9... | collective-permute-start | bytes 2064392 | tf_op jit(solution)/shard_map/ppermute | solution.py:306
  198.1 43.1 %collective-permute-start.25 = (bf16[384,896]{1,0:T(8,128)(2,1)}, bf16[384,896]{1,0:T(8,128)(2,1)}, u32[]{:S(2)}, u32[]{:S(2)}) collective-permute-start(bf16[384,896]{1,0:T(8,128)(2,1)} %collective-permute-done.23.gd_ref.refs_2_), channel_id=1, source_target_pairs={{8,0},{16,8},{24,16},{28,24},{20,28},{12,20},{4,12},{0,4},{9,1},{1... | collective-permute-start | bytes 2064392 | tf_op jit(solution)/shard_map/ppermute | solution.py:309
  198.4 75.1 %collective-permute-start.38 = (bf16[896,384]{1,0:T(8,128)(2,1)}, bf16[896,384]{1,0:T(8,128)(2,1)}, u32[]{:S(2)}, u32[]{:S(2)}) collective-permute-start(bf16[896,384]{1,0:T(8,128)(2,1)} %get-tuple-element.91), channel_id=1, source_target_pairs={{0,0},{28,1},{8,2},{20,3},{16,4},{12,5},{24,6},{4,7},{1,8},{29,9},... | collective-permute-start | bytes 2064392 | tf_op jit(solution)/shard_map/ppermute | solution.py:364
  206.8 53.5 %collective-permute-start.20 = (bf16[384,896]{1,0:T(8,128)(2,1)S(1)}, bf16[384,896]{1,0:T(8,128)(2,1)}, u32[]{:S(2)}, u32[]{:S(2)}) collective-permute-start(bf16[384,896]{1,0:T(8,128)(2,1)S(1)} %collective-permute-done.19.gd_ref.refs_3_), channel_id=1, source_target_pairs={{0,8},{8,16},{16,24},{24,28},{28,20},{20,12},{12,4},{4,0},{1,9},{9... | collective-permute-start | bytes 2064392 | tf_op jit(solution)/shard_map/ppermute | solution.py:306
  213.0 59.0 %collective-permute-start.29 = (bf16[384,896]{1,0:T(8,128)(2,1)S(1)}, bf16[384,896]{1,0:T(8,128)(2,1)}, u32[]{:S(2)}, u32[]{:S(2)}) collective-permute-start(bf16[384,896]{1,0:T(8,128)(2,1)S(1)} %collective-permute-done.26.ud_ref.refs_4_), channel_id=1, source_target_pairs={{8,0},{16,8},{24,16},{28,24},{20,28},{12,20},{4,12},{0,4},{9,1},{1... | collective-permute-start | bytes 2064392 | tf_op jit(solution)/shard_map/ppermute | solution.py:309
  224.5 49.0 %collective-permute-start.27 = (bf16[384,896]{1,0:T(8,128)(2,1)}, bf16[384,896]{1,0:T(8,128)(2,1)}, u32[]{:S(2)}, u32[]{:S(2)}) collective-permute-start(bf16[384,896]{1,0:T(8,128)(2,1)} %collective-permute-done.22.ud_ref.refs_5_), channel_id=1, source_target_pairs={{0,8},{8,16},{16,24},{24,28},{28,20},{20,12},{12,4},{4,0},{1,9},{9... | collective-permute-start | bytes 2064392 | tf_op jit(solution)/shard_map/ppermute | solution.py:306
  241.2 45.5 %collective-permute-start.28 = (bf16[384,896]{1,0:T(8,128)(2,1)}, bf16[384,896]{1,0:T(8,128)(2,1)}, u32[]{:S(2)}, u32[]{:S(2)}) collective-permute-start(bf16[384,896]{1,0:T(8,128)(2,1)} %collective-permute-done.25.gd_ref.refs_2_), channel_id=1, source_target_pairs={{8,0},{16,8},{24,16},{28,24},{20,28},{12,20},{4,12},{0,4},{9,1},{1... | collective-permute-start | bytes 2064392 | tf_op jit(solution)/shard_map/ppermute | solution.py:309
  260.3 32.1 %collective-permute-start.30 = (bf16[384,896]{1,0:T(8,128)(2,1)}, bf16[384,896]{1,0:T(8,128)(2,1)}, u32[]{:S(2)}, u32[]{:S(2)}) collective-permute-start(bf16[384,896]{1,0:T(8,128)(2,1)} %collective-permute-done.20.gd_ref.refs_3_), channel_id=1, source_target_pairs={{0,8},{8,16},{16,24},{24,28},{28,20},{20,12},{12,4},{4,0},{1,9},{9... | collective-permute-start | bytes 2064392 | tf_op jit(solution)/shard_map/ppermute | solution.py:306
  272.0 25.2 %collective-permute-start.31 = (bf16[384,896]{1,0:T(8,128)(2,1)}, bf16[384,896]{1,0:T(8,128)(2,1)}, u32[]{:S(2)}, u32[]{:S(2)}) collective-permute-start(bf16[384,896]{1,0:T(8,128)(2,1)} %collective-permute-done.29.ud_ref.refs_4_), channel_id=1, source_target_pairs={{8,0},{16,8},{24,16},{28,24},{20,28},{12,20},{4,12},{0,4},{9,1},{1... | collective-permute-start | bytes 2064392 | tf_op jit(solution)/shard_map/ppermute | solution.py:309
  273.5 26.1 %collective-permute-start.39 = (bf16[896,384]{1,0:T(8,128)(2,1)}, bf16[896,384]{1,0:T(8,128)(2,1)}, u32[]{:S(2)}, u32[]{:S(2)}) collective-permute-start(bf16[896,384]{1,0:T(8,128)(2,1)} %collective-permute-done.38.refs_0_), channel_id=1, source_target_pairs={{0,2},{1,3},{2,0},{3,1},{4,6},{5,7},{6,4},{7,5},{8,10},{9,11},{10,... | collective-permute-start | bytes 2064392 | tf_op jit(solution)/shard_map/ppermute | solution.py:314
  273.5 26.6 %collective-permute-start.41 = (bf16[896,384]{1,0:T(8,128)(2,1)}, bf16[896,384]{1,0:T(8,128)(2,1)}, u32[]{:S(2)}, u32[]{:S(2)}) collective-permute-start(bf16[896,384]{1,0:T(8,128)(2,1)} %collective-permute-done.38.refs_0_), channel_id=1, source_target_pairs={{0,1},{1,0},{2,3},{3,2},{4,5},{5,4},{6,7},{7,6},{8,9},{9,8},{10,11... | collective-permute-start | bytes 2064392 | tf_op jit(solution)/shard_map/ppermute | solution.py:314
  299.6 33.8 %collective-permute-start.40 = (bf16[896,384]{1,0:T(8,128)(2,1)}, bf16[896,384]{1,0:T(8,128)(2,1)S(1)}, u32[]{:S(2)}, u32[]{:S(2)}) collective-permute-start(bf16[896,384]{1,0:T(8,128)(2,1)} %collective-permute-done.39.refs_0_), channel_id=1, source_target_pairs={{0,1},{1,0},{2,3},{3,2},{4,5},{5,4},{6,7},{7,6},{8,9},{9,8},{10,11... | collective-permute-start | bytes 2064392 | tf_op jit(solution)/shard_map/ppermute | solution.py:314
  316.6 24.6 %collective-permute-start.35 = (f32[192,1024]{1,0:T(8,128)S(1)}, f32[192,1024]{1,0:T(8,128)S(1)}, u32[]{:S(2)}, u32[]{:S(2)}) collective-permute-start(f32[192,1024]{1,0:T(8,128)S(1)} %dynamic-slice_bitcast_fusion), channel_id=1, source_target_pairs={{0,1},{1,0},{2,3},{3,2},{4,5},{5,4},{6,7},{7,6},{8,9},{9,8},{10,11... | collective-permute-start | bytes 2359304 | tf_op jit(solution)/shard_map/ppermute | solution.py:437
  (24 other events, 416.2 us)

commit v3 on v2

--- a/solution.py
+++ b/solution.py
@@ -281,7 +281,9 @@
     place = [ring.index(r) for r in range(rows)]
     ahead = [(ring[p], ring[(p + 1) % rows]) for p in range(rows)]
     back = [(b, a) for a, b in ahead]
+    turn = [(0, 1, 2, 0)[c % 4] for c in range(cols)]
     me = jnp.array(place, jnp.int32)[lax.axis_index("row")]
+    me = lax.rem(me + jnp.array(turn, jnp.int32)[lax.axis_index("col")], rows)
 
     cuts = max(
         q for q in range(ratio, rows // 2 + 1, ratio) if rows % q == 0 and width // BLOCK % q == 0
@@ -298,7 +300,8 @@
     for r in range(rows):
         for c in range(cols):
             shard = (c % parts) * cuts + r % ratio * (cuts // ratio) + c // parts
-            meet.append((r * cols + c, ring[shard] * cols + r // ratio))
+            owner_row = ring[(shard - turn[r // ratio]) % rows]
+            meet.append((r * cols + c, owner_row * cols + r // ratio))
     meet_back = [(b, a) for a, b in meet]
 
     gate_wide, up_wide, down_wide = widen(gate_mask), widen(up_mask), widen(down_mask)
@@ -415,18 +418,10 @@
             up_on, gate_back = onward(up_on), backward(gate_back)
             ups[-step % rows], gates[step % rows] = up_on, gate_back
 
-    total, gates[-far % rows], ups[far] = lax.optimization_barrier((total, gates[-far % rows], ups[far]))
-    late = where_is(me - far)[0]
-    others = [lax.rem(late + 1 + i, parts) for i in range(parts - 1)]
-    early = [lax.dynamic_index_in_dim(total, o, 0, keepdims=False) for o in others]
-    early = [sum_over_col(value, cols) for value in early]
     total = add(total, -far)
     grads = column_cuts(grads)
-    last = sum_over_col(lax.dynamic_index_in_dim(total, late, 0, keepdims=False), cols)
-    input_grad = jnp.zeros((parts, tokens, depth), BF16)
-    for place_of, value in zip(others + [late], early + [last]):
-        input_grad = lax.dynamic_update_index_in_dim(input_grad, value, place_of, 0)
-    return (input_grad.reshape(count, depth), *grads, down_grad)
+    halves = [sum_over_col(value, cols) for value in jnp.split(total.reshape(count, depth), 2)]
+    return (jnp.concatenate(halves), *grads, down_grad)
 
 
 def sum_over_col(value, cols):

time: 359 us -> 355 us (0.989)
  between operations: 9.1 us -> 2.47 us
  Pallas kernels: 147 us -> 141 us
  starting transfers between devices: 62.9 us -> 68.7 us
    ppermute x12, starting transfers between devices: 8.24 us -> 36.1 us  [across(): return lax.ppermute(array, 'col', [(c, c ^ bit) for c in range(cols)])]
    ppermute x14, starting transfers between devices: 46.3 us -> 19.7 us  [onward(): return lax.ppermute(value, 'row', ahead)]
    ppermute x14, waiting for transfers between devices: 62.7 us -> 46.2 us  [backward(): return lax.ppermute(value, 'row', back)]
    ppermute x1, waiting for transfers between devices: 0.01 us -> 10.4 us  [on_device(): hiddens = {0: lax.ppermute(hidden_t, ('row', 'col'), meet_back)}]
    ppermute x12, waiting for transfers between devices: 1.05 us -> 6.91 us  [across(): return lax.ppermute(array, 'col', [(c, c ^ bit) for c in range(cols)])]
    ppermute x14, starting transfers between devices: 1.31 us -> 6.5 us  [backward(): return lax.ppermute(value, 'row', back)]
  transfers between devices with their start and end apart: 42 -> 42, of which waited for: 17 -> 14; matrix products, arithmetic and copies ran while one was open for 7% -> 6% of each run, Pallas kernels for 38% -> 37%
where the time goes in v3:
time: 355 us; the launch traced here: 354 us
  Pallas kernels  141 us (40%)
  waiting for transfers between devices  109 us (31%)
  starting transfers between devices  68.7 us (19%)
  local copies, waits for them, and re-layouts  18 us (5%)
  other arithmetic  13.8 us (4%)
    ppermute x14, waiting for transfers between devices, backward(): return lax.ppermute(value, 'row', back)  46.2 us
    pallas_call x8, Pallas kernels, add_input_grad(): pl.pallas_call(input_grad_kernel, name='input_grad', out_shape=jax.ShapeD...  43.1 us
    ppermute x12, starting transfers between devices, across(): return lax.ppermute(array, 'col', [(c, c ^ bit) for c in range(cols)])  36.1 us
    pallas_call x8, Pallas kernels, products(): pl.pallas_call(functools.partial(product_kernel, parts), name='products',...  34.7 us
    pallas_call x4, Pallas kernels, weight_grads(): pl.pallas_call(functools.partial(weight_grads_kernel, parts), name='weigh...  31 us
    ppermute x14, waiting for transfers between devices, onward(): return lax.ppermute(value, 'row', ahead)  30.1 us
    ppermute x14, starting transfers between devices, onward(): return lax.ppermute(value, 'row', ahead)  19.7 us
    ppermute x1, waiting for transfers between devices, hidden_grad_of(): lax.ppermute(held.reshape(tokens, columns).astype(BF16), ('row', 'col'),...  15.5 us
  transfers between devices with their start and end apart: 42, of which 14 were waited for; matrix products, arithmetic and copies ran while one was open for 6% of the time, Pallas kernels for 37%

profile of v3, /device:TPU:9, one launch (start us, length us, event | category | flops | bytes accessed | tf_op | source)
XLA Modules:
  0.0 353.5 jit_solution(10062554809145352496)
XLA Ops:
  12.6 4.4 %products.12 = (bf16[384,896]{1,0:T(8,128)(2,1)}, f32[384,896]{1,0:T(8,128)S(1)}) custom-call(s32[3]{0:T(128)S(1)} %get-tuple-element.92.at, bf16[768,1024]{1,0:T(8,128)(2,1)} %x_ref.15, bf16[1024,3584]{1,0:T(8,128)(2,1)} %uw_ref.15, bf16[128,3584]{1,0:T(8,128)(2,1)S(1)} %bitcast.81), custom_call_target="tpu_custom_call" | custom-call | flops 1409286144 | bytes 5963776 | tf_op jit(solution)/shard_map/products/pallas_call | solution.py:63
  18.2 4.4 %products.9 = (bf16[384,896]{1,0:T(8,128)(2,1)}, f32[384,896]{1,0:T(8,128)S(1)}) custom-call(s32[3]{0:T(128)S(1)} %get-tuple-element.93.at, bf16[768,1024]{1,0:T(8,128)(2,1)} %x_ref.15, bf16[1024,3584]{1,0:T(8,128)(2,1)} %gw_ref.15, bf16[128,3584]{1,0:T(8,128)(2,1)S(1)} %bitcast.66), custom_call_target="tpu_custom_call" | custom-call | flops 1409286144 | bytes 5963776 | tf_op jit(solution)/shard_map/products/pallas_call | solution.py:63
  57.8 11.5 %hidden_grad.1 = (f32[2,1,384,896]{3,2,1,0:T(8,128)}, bf16[1,384,896]{2,1,0:T(8,128)(2,1)S(1)}, bf16[1,384,896]{2,1,0:T(8,128)(2,1)S(1)}) custom-call(s32[1]{0:T(128)} %bitcast.22.at, bf16[768,2048]{1,0:T(8,128)(2,1)} %g_ref, bf16[1792,2048]{1,0:T(8,128)(2,1)} %w_ref.17, bf16[224,2048]{1,0:T(8,128)(2,1)S(1)} %bitcast.97), custom_call_target="tpu_custom_call" | custom-call | flops 5637144576 | bytes 15990784 | tf_op jit(solution)/shard_map/hidden_grad/pallas_call | solution.py:135
  74.0 8.7 %collective-permute-done.11 = bf16[384,896]{1,0:T(8,128)(2,1)S(1)} collective-permute-done((bf16[384,896]{1,0:T(8,128)(2,1)}, bf16[384,896]{1,0:T(8,128)(2,1)S(1)}, u32[]{:S(2)}, u32[]{:S(2)}) %collective-permute-start.11) | collective-permute-done | bytes 688160 | tf_op jit(solution)/shard_map/ppermute | solution.py:312
  87.6 7.6 %collective-permute-done.3 = bf16[384,896]{1,0:T(8,128)(2,1)S(1)} collective-permute-done((bf16[384,896]{1,0:T(8,128)(2,1)S(1)}, bf16[384,896]{1,0:T(8,128)(2,1)S(1)}, u32[]{:S(2)}, u32[]{:S(2)}) %collective-permute-start.3) | collective-permute-done | bytes 688160 | tf_op jit(solution)/shard_map/ppermute | solution.py:309
  96.7 14.7 %collective-permute-done.12 = bf16[384,896]{1,0:T(8,128)(2,1)S(1)} collective-permute-done((bf16[384,896]{1,0:T(8,128)(2,1)S(1)}, bf16[384,896]{1,0:T(8,128)(2,1)S(1)}, u32[]{:S(2)}, u32[]{:S(2)}) %collective-permute-start.12) | collective-permute-done | bytes 688160 | tf_op jit(solution)/shard_map/ppermute | solution.py:312
  116.2 8.4 %collective-permute-done.4.gate_on = bf16[384,896]{1,0:T(8,128)(2,1)S(1)} collective-permute-done((bf16[384,896]{1,0:T(8,128)(2,1)S(1)}, bf16[384,896]{1,0:T(8,128)(2,1)S(1)}, u32[]{:S(2)}, u32[]{:S(2)}) %collective-permute-start.4) | collective-permute-done | bytes 688160 | tf_op jit(solution)/shard_map/ppermute | solution.py:309
  125.3 15.5 %collective-permute-done.17.hg_ref = bf16[384,896]{1,0:T(8,128)(2,1)S(1)} collective-permute-done((bf16[384,896]{1,0:T(8,128)(2,1)S(1)}, bf16[384,896]{1,0:T(8,128)(2,1)S(1)}, u32[]{:S(2)}, u32[]{:S(2)}) %collective-permute-start.17) | collective-permute-done | bytes 688160 | tf_op jit(solution)/shard_map/ppermute | solution.py:348
  141.7 6.2 %owner.1 = (bf16[384,896]{1,0:T(8,128)(2,1)S(1)}, bf16[384,896]{1,0:T(8,128)(2,1)}, bf16[896,384]{1,0:T(8,128)(2,1)S(1)}) custom-call(f32[384,896]{1,0:T(8,128)} %copy-done.2, bf16[384,896]{1,0:T(8,128)(2,1)S(1)} %collective-permute-done.4.gate_on, bf16[384,896]{1,0:T(8,128)(2,1)S(1)} %collective-permute-done.7.gate_back, f32[384,896]{1,0:T(8,128)} %copy-done.3, ...), custom_call_target="tpu_custom_call" | custom-call | bytes 8257536 | tf_op jit(solution)/shard_map/owner/pallas_call | solution.py:98
  148.7 5.6 %collective-permute-start.18 = (bf16[384,896]{1,0:T(8,128)(2,1)S(1)}, bf16[384,896]{1,0:T(8,128)(2,1)}, u32[]{:S(2)}, u32[]{:S(2)}) collective-permute-start(bf16[384,896]{1,0:T(8,128)(2,1)S(1)} %get-tuple-element.67.gd_ref.refs_2_), channel_id=1, source_target_pairs={{0,8},{8,16},{16,24},{24,28},{28,20},{20,12},{12,4},{4,0},{1,9},{9... | collective-permute-start | bytes 2064392 | tf_op jit(solution)/shard_map/ppermute | solution.py:309
  160.7 8.4 %collective-permute-done.18.gd_ref.refs_3_ = bf16[384,896]{1,0:T(8,128)(2,1)} collective-permute-done((bf16[384,896]{1,0:T(8,128)(2,1)S(1)}, bf16[384,896]{1,0:T(8,128)(2,1)}, u32[]{:S(2)}, u32[]{:S(2)}) %collective-permute-start.18) | collective-permute-done | bytes 688160 | tf_op jit(solution)/shard_map/ppermute | solution.py:309
  172.8 5.5 %input_grad.8.sum_ref = f32[2,384,1024]{2,1,0:T(8,128)} custom-call(s32[2]{0:T(128)S(1)} %pad_add_fusion.10.at, f32[2,384,1024]{2,1,0:T(8,128)} %broadcast_in_dim.31.sum_ref, bf16[384,896]{1,0:T(8,128)(2,1)S(1)} %get-tuple-element.67.gd_ref.refs_2_, bf16[384,896]{1,0:T(8,128)(2,1)} %get-tuple-element.68.ud_ref.refs_4_, ...), custom_call_target="tpu_custom_call", output_to_operand_aliasing={{}: (1, {})} | custom-call | flops 1409286144 | bytes 6815744 | tf_op jit(solution)/shard_map/input_grad/pallas_call | solution.py:168
  178.2 5.7 %collective-permute-done.21.ud_ref.refs_5_ = bf16[384,896]{1,0:T(8,128)(2,1)} collective-permute-done((bf16[384,896]{1,0:T(8,128)(2,1)}, bf16[384,896]{1,0:T(8,128)(2,1)}, u32[]{:S(2)}, u32[]{:S(2)}) %collective-permute-start.21) | collective-permute-done | bytes 688160 | tf_op jit(solution)/shard_map/ppermute | solution.py:309
  188.3 10.4 %collective-permute-done.38.refs_0_ = bf16[896,384]{1,0:T(8,128)(2,1)S(1)} collective-permute-done((bf16[896,384]{1,0:T(8,128)(2,1)}, bf16[896,384]{1,0:T(8,128)(2,1)S(1)}, u32[]{:S(2)}, u32[]{:S(2)}) %collective-permute-start.38) | collective-permute-done | bytes 688160 | tf_op jit(solution)/shard_map/ppermute | solution.py:367
  198.7 16.7 %collective-permute-start.39 = (bf16[896,384]{1,0:T(8,128)(2,1)S(1)}, bf16[896,384]{1,0:T(8,128)(2,1)S(1)}, u32[]{:S(2)}, u32[]{:S(2)}) collective-permute-start(bf16[896,384]{1,0:T(8,128)(2,1)S(1)} %collective-permute-done.38.refs_0_), channel_id=1, source_target_pairs={{0,2},{1,3},{2,0},{3,1},{4,6},{5,7},{6,4},{7,5},{8,10},{9,11},{10,... | collective-permute-start | bytes 2064392 | tf_op jit(solution)/shard_map/ppermute | solution.py:317
  215.4 12.7 %collective-permute-done.26.ud_ref.refs_4_ = bf16[384,896]{1,0:T(8,128)(2,1)S(1)} collective-permute-done((bf16[384,896]{1,0:T(8,128)(2,1)}, bf16[384,896]{1,0:T(8,128)(2,1)S(1)}, u32[]{:S(2)}, u32[]{:S(2)}) %collective-permute-start.26) | collective-permute-done | bytes 688160 | tf_op jit(solution)/shard_map/ppermute | solution.py:312
  228.1 5.7 %input_grad.9.sum_ref = f32[2,384,1024]{2,1,0:T(8,128)} custom-call(s32[2]{0:T(128)S(1)} %pad_add_fusion.12.at, f32[2,384,1024]{2,1,0:T(8,128)} %input_grad.8.sum_ref, bf16[384,896]{1,0:T(8,128)(2,1)} %collective-permute-done.18.gd_ref.refs_3_, bf16[384,896]{1,0:T(8,128)(2,1)} %collective-permute-done.21.ud_ref.refs_5_, ...), custom_call_target="tpu_custom_call", output_to_operand_aliasing={{}: (1, {})} | custom-call | flops 1409286144 | bytes 6815744 | tf_op jit(solution)/shard_map/input_grad/pallas_call | solution.py:168
  233.8 5.7 %input_grad.10.sum_ref = f32[2,384,1024]{2,1,0:T(8,128)} custom-call(s32[2]{0:T(128)S(1)} %pad_add_fusion.11.at, f32[2,384,1024]{2,1,0:T(8,128)} %input_grad.9.sum_ref, bf16[384,896]{1,0:T(8,128)(2,1)} %collective-permute-done.23.gd_ref.refs_2_, bf16[384,896]{1,0:T(8,128)(2,1)} %collective-permute-done.24.ud_ref.refs_4_, ...), custom_call_target="tpu_custom_call", output_to_operand_aliasing={{}: (1, {})} | custom-call | flops 1409286144 | bytes 6815744 | tf_op jit(solution)/shard_map/input_grad/pallas_call | solution.py:168
  242.9 7.4 %weight_grads.4 = (bf16[1024,3584]{1,0:T(8,128)(2,1)}, bf16[1024,3584]{1,0:T(8,128)(2,1)}) custom-call(s32[3]{0:T(128)S(1)} %pad_add_fusion.7.at, bf16[2,1024,384]{2,1,0:T(8,128)(2,1)} %bitcast.101, bf16[2,1024,384]{2,1,0:T(8,128)(2,1)} %bitcast.102, bf16[384,896]{1,0:T(8,128)(2,1)S(1)} %collective-permute-done.25.gd_ref.refs_2_, ...), custom_call_target="tpu_custom_call" | custom-call | flops 2818572288 | bytes 6422528 | tf_op jit(solution)/shard_map/weight_grads/pallas_call | solution.py:213
  250.3 5.3 %input_grad.11.sum_ref = f32[2,384,1024]{2,1,0:T(8,128)} custom-call(s32[2]{0:T(128)S(1)} %pad_add_fusion.9.at, f32[2,384,1024]{2,1,0:T(8,128)} %input_grad.10.sum_ref, bf16[384,896]{1,0:T(8,128)(2,1)S(1)} %collective-permute-done.19.gd_ref.refs_3_, bf16[384,896]{1,0:T(8,128)(2,1)S(1)} %collective-permute-done.22.ud_ref.refs_5_, ...), custom_call_target="tpu_custom_call", output_to_operand_aliasing={{}: (1, {})} | custom-call | flops 1409286144 | bytes 6815744 | tf_op jit(solution)/shard_map/input_grad/pallas_call | solution.py:168
  255.5 5.3 %input_grad.12.sum_ref = f32[2,384,1024]{2,1,0:T(8,128)} custom-call(s32[2]{0:T(128)S(1)} %pad_add_fusion.8.at, f32[2,384,1024]{2,1,0:T(8,128)} %input_grad.11.sum_ref, bf16[384,896]{1,0:T(8,128)(2,1)S(1)} %collective-permute-done.25.gd_ref.refs_2_, bf16[384,896]{1,0:T(8,128)(2,1)S(1)} %collective-permute-done.26.ud_ref.refs_4_, ...), custom_call_target="tpu_custom_call", output_to_operand_aliasing={{}: (1, {})} | custom-call | flops 1409286144 | bytes 6815744 | tf_op jit(solution)/shard_map/input_grad/pallas_call | solution.py:168
  262.6 6.6 %collective-permute-start.41 = (bf16[896,384]{1,0:T(8,128)(2,1)S(1)}, bf16[896,384]{1,0:T(8,128)(2,1)S(1)}, u32[]{:S(2)}, u32[]{:S(2)}) collective-permute-start(bf16[896,384]{1,0:T(8,128)(2,1)S(1)} %collective-permute-done.38.refs_0_), channel_id=1, source_target_pairs={{0,1},{1,0},{2,3},{3,2},{4,5},{5,4},{6,7},{7,6},{8,9},{9,8},{10,11... | collective-permute-start | bytes 2064392 | tf_op jit(solution)/shard_map/ppermute | solution.py:317
  269.2 5.3 %input_grad.13.sum_ref = f32[2,384,1024]{2,1,0:T(8,128)} custom-call(s32[2]{0:T(128)S(1)} %pad_add_fusion.2.at, f32[2,384,1024]{2,1,0:T(8,128)} %input_grad.12.sum_ref, bf16[384,896]{1,0:T(8,128)(2,1)S(1)} %collective-permute-done.20.gd_ref.refs_3_, bf16[384,896]{1,0:T(8,128)(2,1)S(1)} %collective-permute-done.27.ud_ref.refs_5_, ...), custom_call_target="tpu_custom_call", output_to_operand_aliasing={{}: (1, {})} | custom-call | flops 1409286144 | bytes 6815744 | tf_op jit(solution)/shard_map/input_grad/pallas_call | solution.py:168
  274.5 5.2 %input_grad.14.sum_ref = f32[2,384,1024]{2,1,0:T(8,128)} custom-call(s32[2]{0:T(128)S(1)} %pad_add_fusion.1.at, f32[2,384,1024]{2,1,0:T(8,128)} %input_grad.13.sum_ref, bf16[384,896]{1,0:T(8,128)(2,1)S(1)} %collective-permute-done.28.gd_ref.refs_2_, bf16[384,896]{1,0:T(8,128)(2,1)S(1)} %collective-permute-done.29.ud_ref.refs_4_, ...), custom_call_target="tpu_custom_call", output_to_operand_aliasing={{}: (1, {})} | custom-call | flops 1409286144 | bytes 6815744 | tf_op jit(solution)/shard_map/input_grad/pallas_call | solution.py:168
  279.7 7.4 %collective-permute-done.31.ud_ref.refs_5_ = bf16[384,896]{1,0:T(8,128)(2,1)S(1)} collective-permute-done((bf16[384,896]{1,0:T(8,128)(2,1)S(1)}, bf16[384,896]{1,0:T(8,128)(2,1)S(1)}, u32[]{:S(2)}, u32[]{:S(2)}) %collective-permute-start.31) | collective-permute-done | bytes 688160 | tf_op jit(solution)/shard_map/ppermute | solution.py:312
  287.1 5.3 %input_grad.15 = f32[2,384,1024]{2,1,0:T(8,128)} custom-call(s32[2]{0:T(128)S(1)} %pad_add_fusion.at, f32[2,384,1024]{2,1,0:T(8,128)} %input_grad.14.sum_ref, bf16[384,896]{1,0:T(8,128)(2,1)S(1)} %collective-permute-done.30.gd_ref.refs_3_, bf16[384,896]{1,0:T(8,128)(2,1)S(1)} %collective-permute-done.31.ud_ref.refs_5_, ...), custom_call_target="tpu_custom_call", output_to_operand_aliasing={{}: (1, {})} | custom-call | flops 1409286144 | bytes 6815744 | tf_op jit(solution)/shard_map/input_grad/pallas_call | solution.py:168
  299.6 7.5 %down_grad.2.refs_5_ = bf16[1792,2048]{1,0:T(8,128)(2,1)} custom-call(s32[3]{0:T(128)S(1)} %add_add_fusion.1.at, bf16[896,384]{1,0:T(8,128)(2,1)S(1)} %collective-permute-done.38.refs_0_, bf16[896,384]{1,0:T(8,128)(2,1)S(1)} %collective-permute-done.41.refs_1_, bf16[2,384,2048]{2,1,0:T(8,128)(2,1)} %bitcast.109, bf16[2,384,2048]{2,1,0:T(8,128)(2,1)} %bitcast.110, ...), custom_call_target="tpu_custom_call" | custom-call | flops 2818572288 | bytes 6815744 | tf_op jit(solution)/shard_map/down_grad/pallas_call | solution.py:254
  307.1 7.9 %weight_grads.5 = (bf16[1024,3584]{1,0:T(8,128)(2,1)}, bf16[1024,3584]{1,0:T(8,128)(2,1)}) custom-call(s32[3]{0:T(128)S(1)} %pad_add_fusion.14.at, bf16[2,1024,384]{2,1,0:T(8,128)(2,1)} %bitcast.103, bf16[2,1024,384]{2,1,0:T(8,128)(2,1)} %bitcast.104, ...), custom_call_target="tpu_custom_call", output_to_operand_aliasing={{0}: (9, {}), {1}: (10, {})} | custom-call | flops 2818572288 | bytes 6422528 | tf_op jit(solution)/shard_map/weight_grads/pallas_call | solution.py:213
  315.0 7.9 %weight_grads.6 = (bf16[1024,3584]{1,0:T(8,128)(2,1)}, bf16[1024,3584]{1,0:T(8,128)(2,1)}) custom-call(s32[3]{0:T(128)S(1)} %get-tuple-element.95.at, bf16[2,1024,384]{2,1,0:T(8,128)(2,1)} %bitcast.105, bf16[2,1024,384]{2,1,0:T(8,128)(2,1)} %bitcast.106, ...), custom_call_target="tpu_custom_call", output_to_operand_aliasing={{0}: (9, {}), {1}: (10, {})} | custom-call | flops 2818572288 | bytes 6422528 | tf_op jit(solution)/shard_map/weight_grads/pallas_call | solution.py:213
  325.9 7.5 %down_grad.3 = bf16[1792,2048]{1,0:T(8,128)(2,1)} custom-call(s32[3]{0:T(128)S(1)} %add_add_fusion.at, bf16[896,384]{1,0:T(8,128)(2,1)S(1)} %collective-permute-done.39.refs_0_, bf16[896,384]{1,0:T(8,128)(2,1)S(1)} %collective-permute-done.40.refs_1_, bf16[2,384,2048]{2,1,0:T(8,128)(2,1)} %bitcast.111, ...), custom_call_target="tpu_custom_call", output_to_operand_aliasing={{}: (6, {})} | custom-call | flops 2818572288 | bytes 6815744 | tf_op jit(solution)/shard_map/down_grad/pallas_call | solution.py:254
  336.9 5.9 %collective-permute-done.33 = bf16[192,1024]{1,0:T(8,128)(2,1)S(1)} collective-permute-done((bf16[192,1024]{1,0:T(8,128)(2,1)S(1)}, bf16[192,1024]{1,0:T(8,128)(2,1)S(1)}, u32[]{:S(2)}, u32[]{:S(2)}) %collective-permute-start.33) | collective-permute-done | bytes 393248 | tf_op jit(solution)/shard_map/ppermute | solution.py:432
  344.4 7.7 %weight_grads.7 = (bf16[1024,3584]{1,0:T(8,128)(2,1)}, bf16[1024,3584]{1,0:T(8,128)(2,1)}) custom-call(s32[3]{0:T(128)S(1)} %pad_add_fusion.13.at, bf16[2,1024,384]{2,1,0:T(8,128)(2,1)} %bitcast.107, bf16[2,1024,384]{2,1,0:T(8,128)(2,1)} %bitcast.108, ...), custom_call_target="tpu_custom_call", output_to_operand_aliasing={{0}: (9, {}), {1}: (10, {})} | custom-call | flops 2818572288 | bytes 6422528 | tf_op jit(solution)/shard_map/weight_grads/pallas_call | solution.py:213
  (159 shorter events, 101.3 us)
Async XLA Ops:
  11.0 37.2 %collective-permute-start = (bf16[384,896]{1,0:T(8,128)(2,1)}, bf16[384,896]{1,0:T(8,128)(2,1)}, u32[]{:S(2)}, u32[]{:S(2)}) collective-permute-start(bf16[384,896]{1,0:T(8,128)(2,1)} %get-tuple-element.49), channel_id=1, source_target_pairs={{0,8},{8,16},{16,24},{24,28},{28,20},{20,12},{12,4},{4,0},{1,9},{9... | collective-permute-start | bytes 2064392 | tf_op jit(solution)/shard_map/ppermute | solution.py:309
  18.1 30.2 %collective-permute-start.1 = (bf16[384,896]{1,0:T(8,128)(2,1)}, bf16[384,896]{1,0:T(8,128)(2,1)S(1)}, u32[]{:S(2)}, u32[]{:S(2)}) collective-permute-start(bf16[384,896]{1,0:T(8,128)(2,1)} %get-tuple-element.50), channel_id=1, source_target_pairs={{8,0},{16,8},{24,16},{28,24},{20,28},{12,20},{4,12},{0,4},{9,1},{1... | collective-permute-start | bytes 2064392 | tf_op jit(solution)/shard_map/ppermute | solution.py:312
  23.7 28.0 %collective-permute-start.5 = (bf16[384,896]{1,0:T(8,128)(2,1)}, bf16[384,896]{1,0:T(8,128)(2,1)}, u32[]{:S(2)}, u32[]{:S(2)}) collective-permute-start(bf16[384,896]{1,0:T(8,128)(2,1)} %get-tuple-element.54), channel_id=1, source_target_pairs={{8,0},{16,8},{24,16},{28,24},{20,28},{12,20},{4,12},{0,4},{9,1},{1... | collective-permute-start | bytes 2064392 | tf_op jit(solution)/shard_map/ppermute | solution.py:312
  29.2 23.9 %collective-permute-start.8 = (bf16[384,896]{1,0:T(8,128)(2,1)S(1)}, bf16[384,896]{1,0:T(8,128)(2,1)}, u32[]{:S(2)}, u32[]{:S(2)}) collective-permute-start(bf16[384,896]{1,0:T(8,128)(2,1)S(1)} %get-tuple-element.58), channel_id=1, source_target_pairs={{0,8},{8,16},{16,24},{24,28},{28,20},{20,12},{12,4},{4,0},{1,9},{9... | collective-permute-start | bytes 2064392 | tf_op jit(solution)/shard_map/ppermute | solution.py:309
  50.3 21.9 %collective-permute-start.2 = (bf16[384,896]{1,0:T(8,128)(2,1)}, bf16[384,896]{1,0:T(8,128)(2,1)S(1)}, u32[]{:S(2)}, u32[]{:S(2)}) collective-permute-start(bf16[384,896]{1,0:T(8,128)(2,1)} %add_convert_fusion.9), channel_id=1, source_target_pairs={{0,8},{8,16},{16,24},{24,28},{28,20},{20,12},{12,4},{4,0},{1,9},{9... | collective-permute-start | bytes 2064392 | tf_op jit(solution)/shard_map/ppermute | solution.py:309
  55.3 29.7 %collective-permute-start.9 = (bf16[384,896]{1,0:T(8,128)(2,1)}, bf16[384,896]{1,0:T(8,128)(2,1)}, u32[]{:S(2)}, u32[]{:S(2)}) collective-permute-start(bf16[384,896]{1,0:T(8,128)(2,1)} %add_convert_fusion.4), channel_id=1, source_target_pairs={{0,8},{8,16},{16,24},{24,28},{28,20},{20,12},{12,4},{4,0},{1,9},{9... | collective-permute-start | bytes 2064392 | tf_op jit(solution)/shard_map/ppermute | solution.py:309
  57.6 25.1 %collective-permute-start.11 = (bf16[384,896]{1,0:T(8,128)(2,1)}, bf16[384,896]{1,0:T(8,128)(2,1)S(1)}, u32[]{:S(2)}, u32[]{:S(2)}) collective-permute-start(bf16[384,896]{1,0:T(8,128)(2,1)} %add_convert_fusion.2), channel_id=1, source_target_pairs={{8,0},{16,8},{24,16},{28,24},{20,28},{12,20},{4,12},{0,4},{9,1},{1... | collective-permute-start | bytes 2064392 | tf_op jit(solution)/shard_map/ppermute | solution.py:312
  72.5 22.7 %collective-permute-start.3 = (bf16[384,896]{1,0:T(8,128)(2,1)S(1)}, bf16[384,896]{1,0:T(8,128)(2,1)S(1)}, u32[]{:S(2)}, u32[]{:S(2)}) collective-permute-start(bf16[384,896]{1,0:T(8,128)(2,1)S(1)} %add_convert_fusion.8), channel_id=1, source_target_pairs={{0,8},{8,16},{16,24},{24,28},{28,20},{20,12},{12,4},{4,0},{1,9},{9... | collective-permute-start | bytes 2064392 | tf_op jit(solution)/shard_map/ppermute | solution.py:309
  82.7 33.6 %collective-permute-start.7 = (bf16[384,896]{1,0:T(8,128)(2,1)S(1)}, bf16[384,896]{1,0:T(8,128)(2,1)S(1)}, u32[]{:S(2)}, u32[]{:S(2)}) collective-permute-start(bf16[384,896]{1,0:T(8,128)(2,1)S(1)} %add_convert_fusion.5), channel_id=1, source_target_pairs={{8,0},{16,8},{24,16},{28,24},{20,28},{12,20},{4,12},{0,4},{9,1},{1... | collective-permute-start | bytes 2064392 | tf_op jit(solution)/shard_map/ppermute | solution.py:312
  83.0 28.4 %collective-permute-start.12 = (bf16[384,896]{1,0:T(8,128)(2,1)S(1)}, bf16[384,896]{1,0:T(8,128)(2,1)S(1)}, u32[]{:S(2)}, u32[]{:S(2)}) collective-permute-start(bf16[384,896]{1,0:T(8,128)(2,1)S(1)} %add_convert_fusion.1), channel_id=1, source_target_pairs={{8,0},{16,8},{24,16},{28,24},{20,28},{12,20},{4,12},{0,4},{9,1},{1... | collective-permute-start | bytes 2064392 | tf_op jit(solution)/shard_map/ppermute | solution.py:312
  83.8 28.1 %collective-permute-start.16 = (bf16[1,384,896]{2,1,0:T(8,128)(2,1)S(1)}, bf16[1,384,896]{2,1,0:T(8,128)(2,1)S(1)}, u32[]{:S(2)}, u32[]{:S(2)}) collective-permute-start(bf16[1,384,896]{2,1,0:T(8,128)(2,1)S(1)} %fusion.3), channel_id=1, source_target_pairs={{0,2},{1,3},{2,0},{3,1},{4,6},{5,7},{6,4},{7,5},{8,10},{9,11},{10,... | collective-permute-start | bytes 2064392 | tf_op jit(solution)/shard_map/ppermute | solution.py:317
  86.2 30.0 %collective-permute-start.10 = (bf16[384,896]{1,0:T(8,128)(2,1)S(1)}, bf16[384,896]{1,0:T(8,128)(2,1)S(1)}, u32[]{:S(2)}, u32[]{:S(2)}) collective-permute-start(bf16[384,896]{1,0:T(8,128)(2,1)S(1)} %add_convert_fusion.3), channel_id=1, source_target_pairs={{0,8},{8,16},{16,24},{24,28},{28,20},{20,12},{12,4},{4,0},{1,9},{9... | collective-permute-start | bytes 2064392 | tf_op jit(solution)/shard_map/ppermute | solution.py:309
  95.4 29.3 %collective-permute-start.4 = (bf16[384,896]{1,0:T(8,128)(2,1)S(1)}, bf16[384,896]{1,0:T(8,128)(2,1)S(1)}, u32[]{:S(2)}, u32[]{:S(2)}) collective-permute-start(bf16[384,896]{1,0:T(8,128)(2,1)S(1)} %add_convert_fusion.7), channel_id=1, source_target_pairs={{0,8},{8,16},{16,24},{24,28},{28,20},{20,12},{12,4},{4,0},{1,9},{9... | collective-permute-start | bytes 2064392 | tf_op jit(solution)/shard_map/ppermute | solution.py:309
  112.0 28.8 %collective-permute-start.17 = (bf16[384,896]{1,0:T(8,128)(2,1)S(1)}, bf16[384,896]{1,0:T(8,128)(2,1)S(1)}, u32[]{:S(2)}, u32[]{:S(2)}) collective-permute-start(bf16[384,896]{1,0:T(8,128)(2,1)S(1)} %fusion.4), channel_id=1, source_target_pairs={{0,0},{1,28},{2,8},{3,20},{4,16},{5,12},{6,24},{7,4},{8,5},{9,25},... | collective-permute-start | bytes 2064392 | tf_op jit(solution)/shard_map/ppermute | solution.py:348
  148.7 20.4 %collective-permute-start.18 = (bf16[384,896]{1,0:T(8,128)(2,1)S(1)}, bf16[384,896]{1,0:T(8,128)(2,1)}, u32[]{:S(2)}, u32[]{:S(2)}) collective-permute-start(bf16[384,896]{1,0:T(8,128)(2,1)S(1)} %get-tuple-element.67.gd_ref.refs_2_), channel_id=1, source_target_pairs={{0,8},{8,16},{16,24},{24,28},{28,20},{20,12},{12,4},{4,0},{1,9},{9... | collective-permute-start | bytes 2064392 | tf_op jit(solution)/shard_map/ppermute | solution.py:309
  154.3 29.6 %collective-permute-start.21 = (bf16[384,896]{1,0:T(8,128)(2,1)}, bf16[384,896]{1,0:T(8,128)(2,1)}, u32[]{:S(2)}, u32[]{:S(2)}) collective-permute-start(bf16[384,896]{1,0:T(8,128)(2,1)} %get-tuple-element.68.ud_ref.refs_4_), channel_id=1, source_target_pairs={{0,8},{8,16},{16,24},{24,28},{28,20},{20,12},{12,4},{4,0},{1,9},{9... | collective-permute-start | bytes 2064392 | tf_op jit(solution)/shard_map/ppermute | solution.py:309
  155.7 28.3 %collective-permute-start.23 = (bf16[384,896]{1,0:T(8,128)(2,1)S(1)}, bf16[384,896]{1,0:T(8,128)(2,1)}, u32[]{:S(2)}, u32[]{:S(2)}) collective-permute-start(bf16[384,896]{1,0:T(8,128)(2,1)S(1)} %get-tuple-element.67.gd_ref.refs_2_), channel_id=1, source_target_pairs={{8,0},{16,8},{24,16},{28,24},{20,28},{12,20},{4,12},{0,4},{9,1},{1... | collective-permute-start | bytes 2064392 | tf_op jit(solution)/shard_map/ppermute | solution.py:312
  158.5 40.1 %collective-permute-start.38 = (bf16[896,384]{1,0:T(8,128)(2,1)}, bf16[896,384]{1,0:T(8,128)(2,1)S(1)}, u32[]{:S(2)}, u32[]{:S(2)}) collective-permute-start(bf16[896,384]{1,0:T(8,128)(2,1)} %copy-done.8), channel_id=1, source_target_pairs={{0,0},{28,1},{8,2},{20,3},{16,4},{12,5},{24,6},{4,7},{5,8},{25,9},... | collective-permute-start | bytes 2064392 | tf_op jit(solution)/shard_map/ppermute | solution.py:367
  169.1 46.2 %collective-permute-start.19 = (bf16[384,896]{1,0:T(8,128)(2,1)}, bf16[384,896]{1,0:T(8,128)(2,1)S(1)}, u32[]{:S(2)}, u32[]{:S(2)}) collective-permute-start(bf16[384,896]{1,0:T(8,128)(2,1)} %collective-permute-done.18.gd_ref.refs_3_), channel_id=1, source_target_pairs={{0,8},{8,16},{16,24},{24,28},{28,20},{20,12},{12,4},{4,0},{1,9},{9... | collective-permute-start | bytes 2064392 | tf_op jit(solution)/shard_map/ppermute | solution.py:309
  169.3 58.8 %collective-permute-start.26 = (bf16[384,896]{1,0:T(8,128)(2,1)}, bf16[384,896]{1,0:T(8,128)(2,1)S(1)}, u32[]{:S(2)}, u32[]{:S(2)}) collective-permute-start(bf16[384,896]{1,0:T(8,128)(2,1)} %collective-permute-done.24.ud_ref.refs_4_), channel_id=1, source_target_pairs={{8,0},{16,8},{24,16},{28,24},{20,28},{12,20},{4,12},{0,4},{9,1},{1... | collective-permute-start | bytes 2064392 | tf_op jit(solution)/shard_map/ppermute | solution.py:312
  183.9 55.6 %collective-permute-start.22 = (bf16[384,896]{1,0:T(8,128)(2,1)}, bf16[384,896]{1,0:T(8,128)(2,1)S(1)}, u32[]{:S(2)}, u32[]{:S(2)}) collective-permute-start(bf16[384,896]{1,0:T(8,128)(2,1)} %collective-permute-done.21.ud_ref.refs_5_), channel_id=1, source_target_pairs={{0,8},{8,16},{16,24},{24,28},{28,20},{20,12},{12,4},{4,0},{1,9},{9... | collective-permute-start | bytes 2064392 | tf_op jit(solution)/shard_map/ppermute | solution.py:309
  184.1 58.8 %collective-permute-start.25 = (bf16[384,896]{1,0:T(8,128)(2,1)}, bf16[384,896]{1,0:T(8,128)(2,1)S(1)}, u32[]{:S(2)}, u32[]{:S(2)}) collective-permute-start(bf16[384,896]{1,0:T(8,128)(2,1)} %collective-permute-done.23.gd_ref.refs_2_), channel_id=1, source_target_pairs={{8,0},{16,8},{24,16},{28,24},{20,28},{12,20},{4,12},{0,4},{9,1},{1... | collective-permute-start | bytes 2064392 | tf_op jit(solution)/shard_map/ppermute | solution.py:312
  198.7 63.9 %collective-permute-start.39 = (bf16[896,384]{1,0:T(8,128)(2,1)S(1)}, bf16[896,384]{1,0:T(8,128)(2,1)S(1)}, u32[]{:S(2)}, u32[]{:S(2)}) collective-permute-start(bf16[896,384]{1,0:T(8,128)(2,1)S(1)} %collective-permute-done.38.refs_0_), channel_id=1, source_target_pairs={{0,2},{1,3},{2,0},{3,1},{4,6},{5,7},{6,4},{7,5},{8,10},{9,11},{10,... | collective-permute-start | bytes 2064392 | tf_op jit(solution)/shard_map/ppermute | solution.py:317
  215.4 45.4 %collective-permute-start.20 = (bf16[384,896]{1,0:T(8,128)(2,1)S(1)}, bf16[384,896]{1,0:T(8,128)(2,1)S(1)}, u32[]{:S(2)}, u32[]{:S(2)}) collective-permute-start(bf16[384,896]{1,0:T(8,128)(2,1)S(1)} %collective-permute-done.19.gd_ref.refs_3_), channel_id=1, source_target_pairs={{0,8},{8,16},{16,24},{24,28},{28,20},{20,12},{12,4},{4,0},{1,9},{9... | collective-permute-start | bytes 2064392 | tf_op jit(solution)/shard_map/ppermute | solution.py:309
  228.1 34.1 %collective-permute-start.29 = (bf16[384,896]{1,0:T(8,128)(2,1)S(1)}, bf16[384,896]{1,0:T(8,128)(2,1)S(1)}, u32[]{:S(2)}, u32[]{:S(2)}) collective-permute-start(bf16[384,896]{1,0:T(8,128)(2,1)S(1)} %collective-permute-done.26.ud_ref.refs_4_), channel_id=1, source_target_pairs={{8,0},{16,8},{24,16},{28,24},{20,28},{12,20},{4,12},{0,4},{9,1},{1... | collective-permute-start | bytes 2064392 | tf_op jit(solution)/shard_map/ppermute | solution.py:312
  239.5 29.6 %collective-permute-start.27 = (bf16[384,896]{1,0:T(8,128)(2,1)S(1)}, bf16[384,896]{1,0:T(8,128)(2,1)S(1)}, u32[]{:S(2)}, u32[]{:S(2)}) collective-permute-start(bf16[384,896]{1,0:T(8,128)(2,1)S(1)} %collective-permute-done.22.ud_ref.refs_5_), channel_id=1, source_target_pairs={{0,8},{8,16},{16,24},{24,28},{28,20},{20,12},{12,4},{4,0},{1,9},{9... | collective-permute-start | bytes 2064392 | tf_op jit(solution)/shard_map/ppermute | solution.py:309
  242.9 31.6 %collective-permute-start.28 = (bf16[384,896]{1,0:T(8,128)(2,1)S(1)}, bf16[384,896]{1,0:T(8,128)(2,1)S(1)}, u32[]{:S(2)}, u32[]{:S(2)}) collective-permute-start(bf16[384,896]{1,0:T(8,128)(2,1)S(1)} %collective-permute-done.25.gd_ref.refs_2_), channel_id=1, source_target_pairs={{8,0},{16,8},{24,16},{28,24},{20,28},{12,20},{4,12},{0,4},{9,1},{1... | collective-permute-start | bytes 2064392 | tf_op jit(solution)/shard_map/ppermute | solution.py:312
  262.2 24.9 %collective-permute-start.31 = (bf16[384,896]{1,0:T(8,128)(2,1)S(1)}, bf16[384,896]{1,0:T(8,128)(2,1)S(1)}, u32[]{:S(2)}, u32[]{:S(2)}) collective-permute-start(bf16[384,896]{1,0:T(8,128)(2,1)S(1)} %collective-permute-done.29.ud_ref.refs_4_), channel_id=1, source_target_pairs={{8,0},{16,8},{24,16},{28,24},{20,28},{12,20},{4,12},{0,4},{9,1},{1... | collective-permute-start | bytes 2064392 | tf_op jit(solution)/shard_map/ppermute | solution.py:312
  262.6 37.0 %collective-permute-start.41 = (bf16[896,384]{1,0:T(8,128)(2,1)S(1)}, bf16[896,384]{1,0:T(8,128)(2,1)S(1)}, u32[]{:S(2)}, u32[]{:S(2)}) collective-permute-start(bf16[896,384]{1,0:T(8,128)(2,1)S(1)} %collective-permute-done.38.refs_0_), channel_id=1, source_target_pairs={{0,1},{1,0},{2,3},{3,2},{4,5},{5,4},{6,7},{7,6},{8,9},{9,8},{10,11... | collective-permute-start | bytes 2064392 | tf_op jit(solution)/shard_map/ppermute | solution.py:317
  269.1 56.8 %collective-permute-start.40 = (bf16[896,384]{1,0:T(8,128)(2,1)S(1)}, bf16[896,384]{1,0:T(8,128)(2,1)S(1)}, u32[]{:S(2)}, u32[]{:S(2)}) collective-permute-start(bf16[896,384]{1,0:T(8,128)(2,1)S(1)} %collective-permute-done.39.refs_0_), channel_id=1, source_target_pairs={{0,1},{1,0},{2,3},{3,2},{4,5},{5,4},{6,7},{7,6},{8,9},{9,8},{10,11... | collective-permute-start | bytes 2064392 | tf_op jit(solution)/shard_map/ppermute | solution.py:317
  295.4 27.5 %collective-permute-start.35 = (f32[192,1024]{1,0:T(8,128)}, f32[192,1024]{1,0:T(8,128)}, u32[]{:S(2)}, u32[]{:S(2)}) collective-permute-start(f32[192,1024]{1,0:T(8,128)} %dynamic-slice_bitcast_fusion), channel_id=1, source_target_pairs={{0,1},{1,0},{2,3},{3,2},{4,5},{5,4},{6,7},{7,6},{8,9},{9,8},{10,11... | collective-permute-start | bytes 2359304 | tf_op jit(solution)/shard_map/ppermute | solution.py:432
  299.6 24.7 %collective-permute-start.32 = (f32[192,1024]{1,0:T(8,128)}, f32[192,1024]{1,0:T(8,128)S(1)}, u32[]{:S(2)}, u32[]{:S(2)}) collective-permute-start(f32[192,1024]{1,0:T(8,128)} %dynamic-slice_bitcast_fusion.1), channel_id=1, source_target_pairs={{0,1},{1,0},{2,3},{3,2},{4,5},{5,4},{6,7},{7,6},{8,9},{9,8},{10,11... | collective-permute-start | bytes 2359304 | tf_op jit(solution)/shard_map/ppermute | solution.py:432
  (24 other events, 457.4 us)

commit v4 on v3

--- a/solution.py
+++ b/solution.py
@@ -281,7 +281,7 @@
     place = [ring.index(r) for r in range(rows)]
     ahead = [(ring[p], ring[(p + 1) % rows]) for p in range(rows)]
     back = [(b, a) for a, b in ahead]
-    turn = [(0, 1, 2, 0)[c % 4] for c in range(cols)]
+    turn = [(0, 2, 4, 6)[c % 4] for c in range(cols)]
     me = jnp.array(place, jnp.int32)[lax.axis_index("row")]
     me = lax.rem(me + jnp.array(turn, jnp.int32)[lax.axis_index("col")], rows)
 
@@ -418,6 +418,7 @@
             up_on, gate_back = onward(up_on), backward(gate_back)
             ups[-step % rows], gates[step % rows] = up_on, gate_back
 
+    total, grads = lax.optimization_barrier((total, grads))
     total = add(total, -far)
     grads = column_cuts(grads)
     halves = [sum_over_col(value, cols) for value in jnp.split(total.reshape(count, depth), 2)]

time: 355 us -> 350 us (0.986)
  starting transfers between devices: 68.7 us -> 61.8 us
  Pallas kernels: 141 us -> 146 us
    ppermute x12, starting transfers between devices: 36.1 us -> 13.6 us  [across(): return lax.ppermute(array, 'col', [(c, c ^ bit) for c in range(cols)])]
    ppermute x14, waiting for transfers between devices: 46.2 us -> 24.7 us  [backward(): return lax.ppermute(value, 'row', back)]
    ppermute x1, waiting for transfers between devices: 10.4 us -> 21.4 us  [on_device(): hiddens = {0: lax.ppermute(hidden_t, ('row', 'col'), meet_back)}]
    ppermute x14, starting transfers between devices: 19.7 us -> 30.2 us  [onward(): return lax.ppermute(value, 'row', ahead)]
    ppermute x14, waiting for transfers between devices: 30.1 us -> 39.5 us  [onward(): return lax.ppermute(value, 'row', ahead)]
  transfers between devices with their start and end apart: 42 -> 42, of which waited for: 14 -> 12; matrix products, arithmetic and copies ran while one was open for 6% -> 6% of each run, Pallas kernels for 37% -> 39%
where the time goes in v4:
time: 350 us; the launch traced here: 348 us
  Pallas kernels  146 us (42%)
  waiting for transfers between devices  108 us (31%)
  starting transfers between devices  61.8 us (18%)
  local copies, waits for them, and re-layouts  16.3 us (5%)
  other arithmetic  13.8 us (4%)
    pallas_call x8, Pallas kernels, add_input_grad(): pl.pallas_call(input_grad_kernel, name='input_grad', out_shape=jax.ShapeD...  45 us
    ppermute x14, waiting for transfers between devices, onward(): return lax.ppermute(value, 'row', ahead)  39.5 us
    pallas_call x8, Pallas kernels, products(): pl.pallas_call(functools.partial(product_kernel, parts), name='products',...  34.6 us
    pallas_call x4, Pallas kernels, weight_grads(): pl.pallas_call(functools.partial(weight_grads_kernel, parts), name='weigh...  32.8 us
    ppermute x14, starting transfers between devices, onward(): return lax.ppermute(value, 'row', ahead)  30.2 us
    ppermute x14, waiting for transfers between devices, backward(): return lax.ppermute(value, 'row', back)  24.7 us
    ppermute x1, waiting for transfers between devices, on_device(): hiddens = {0: lax.ppermute(hidden_t, ('row', 'col'), meet_back)}  21.4 us
    pallas_call x2, Pallas kernels, down_grad_cut(): pl.pallas_call(functools.partial(down_grad_kernel, parts), name='down_gra...  15.8 us
  transfers between devices with their start and end apart: 42, of which 12 were waited for; matrix products, arithmetic and copies ran while one was open for 6% of the time, Pallas kernels for 39%

profile of v4, /device:TPU:9, one launch (start us, length us, event | category | flops | bytes accessed | tf_op | source)
XLA Modules:
  0.0 347.9 jit_solution(13790537304372866438)
XLA Ops:
  3.7 4.3 %products.8 = (bf16[384,896]{1,0:T(8,128)(2,1)}, f32[384,896]{1,0:T(8,128)S(1)}) custom-call(s32[3]{0:T(128)S(1)} %get-tuple-element.98.at, bf16[768,1024]{1,0:T(8,128)(2,1)} %x_ref.15, bf16[1024,3584]{1,0:T(8,128)(2,1)} %gw_ref.15, bf16[128,3584]{1,0:T(8,128)(2,1)S(1)} %bitcast.66), custom_call_target="tpu_custom_call" | custom-call | flops 1409286144 | bytes 5963776 | tf_op jit(solution)/shard_map/products/pallas_call | solution.py:63
  10.7 4.4 %products.12 = (bf16[384,896]{1,0:T(8,128)(2,1)}, f32[384,896]{1,0:T(8,128)S(1)}) custom-call(s32[3]{0:T(128)S(1)} %get-tuple-element.98.at, bf16[768,1024]{1,0:T(8,128)(2,1)} %x_ref.15, bf16[1024,3584]{1,0:T(8,128)(2,1)} %uw_ref.15, bf16[128,3584]{1,0:T(8,128)(2,1)S(1)} %bitcast.82), custom_call_target="tpu_custom_call" | custom-call | flops 1409286144 | bytes 5963776 | tf_op jit(solution)/shard_map/products/pallas_call | solution.py:63
  16.4 4.3 %products.9 = (bf16[384,896]{1,0:T(8,128)(2,1)}, f32[384,896]{1,0:T(8,128)S(1)}) custom-call(s32[3]{0:T(128)S(1)} %get-tuple-element.99.at, bf16[768,1024]{1,0:T(8,128)(2,1)} %x_ref.15, bf16[1024,3584]{1,0:T(8,128)(2,1)} %gw_ref.15, bf16[128,3584]{1,0:T(8,128)(2,1)S(1)} %bitcast.67), custom_call_target="tpu_custom_call" | custom-call | flops 1409286144 | bytes 5963776 | tf_op jit(solution)/shard_map/products/pallas_call | solution.py:63
  21.9 4.4 %products.15 = (bf16[384,896]{1,0:T(8,128)(2,1)}, f32[384,896]{1,0:T(8,128)S(1)}) custom-call(s32[3]{0:T(128)S(1)} %get-tuple-element.101.at, bf16[768,1024]{1,0:T(8,128)(2,1)} %x_ref.15, bf16[1024,3584]{1,0:T(8,128)(2,1)} %uw_ref.15, bf16[128,3584]{1,0:T(8,128)(2,1)S(1)} %bitcast.83), custom_call_target="tpu_custom_call" | custom-call | flops 1409286144 | bytes 5963776 | tf_op jit(solution)/shard_map/products/pallas_call | solution.py:63
  54.7 11.4 %hidden_grad.1 = (f32[2,1,384,896]{3,2,1,0:T(8,128)}, bf16[1,384,896]{2,1,0:T(8,128)(2,1)S(1)}, bf16[1,384,896]{2,1,0:T(8,128)(2,1)S(1)}) custom-call(s32[1]{0:T(128)} %bitcast.23.at, bf16[768,2048]{1,0:T(8,128)(2,1)} %g_ref, bf16[1792,2048]{1,0:T(8,128)(2,1)} %w_ref.17, bf16[224,2048]{1,0:T(8,128)(2,1)S(1)} %bitcast.98), custom_call_target="tpu_custom_call" | custom-call | flops 5637144576 | bytes 15990784 | tf_op jit(solution)/shard_map/hidden_grad/pallas_call | solution.py:135
  70.8 8.8 %collective-permute-done.11 = bf16[384,896]{1,0:T(8,128)(2,1)} collective-permute-done((bf16[384,896]{1,0:T(8,128)(2,1)}, bf16[384,896]{1,0:T(8,128)(2,1)}, u32[]{:S(2)}, u32[]{:S(2)}) %collective-permute-start.11) | collective-permute-done | bytes 688160 | tf_op jit(solution)/shard_map/ppermute | solution.py:312
  84.5 7.7 %collective-permute-done.3 = bf16[384,896]{1,0:T(8,128)(2,1)S(1)} collective-permute-done((bf16[384,896]{1,0:T(8,128)(2,1)S(1)}, bf16[384,896]{1,0:T(8,128)(2,1)S(1)}, u32[]{:S(2)}, u32[]{:S(2)}) %collective-permute-start.3) | collective-permute-done | bytes 688160 | tf_op jit(solution)/shard_map/ppermute | solution.py:309
  93.7 14.6 %collective-permute-done.12 = bf16[384,896]{1,0:T(8,128)(2,1)S(1)} collective-permute-done((bf16[384,896]{1,0:T(8,128)(2,1)S(1)}, bf16[384,896]{1,0:T(8,128)(2,1)S(1)}, u32[]{:S(2)}, u32[]{:S(2)}) %collective-permute-start.12) | collective-permute-done | bytes 688160 | tf_op jit(solution)/shard_map/ppermute | solution.py:312
  112.1 9.6 %collective-permute-done.4.gate_on = bf16[384,896]{1,0:T(8,128)(2,1)S(1)} collective-permute-done((bf16[384,896]{1,0:T(8,128)(2,1)S(1)}, bf16[384,896]{1,0:T(8,128)(2,1)S(1)}, u32[]{:S(2)}, u32[]{:S(2)}) %collective-permute-start.4) | collective-permute-done | bytes 688160 | tf_op jit(solution)/shard_map/ppermute | solution.py:309
  122.2 15.6 %collective-permute-done.17.hg_ref = bf16[384,896]{1,0:T(8,128)(2,1)S(1)} collective-permute-done((bf16[384,896]{1,0:T(8,128)(2,1)S(1)}, bf16[384,896]{1,0:T(8,128)(2,1)S(1)}, u32[]{:S(2)}, u32[]{:S(2)}) %collective-permute-start.17) | collective-permute-done | bytes 688160 | tf_op jit(solution)/shard_map/ppermute | solution.py:348
  138.7 6.4 %owner.1 = (bf16[384,896]{1,0:T(8,128)(2,1)S(1)}, bf16[384,896]{1,0:T(8,128)(2,1)}, bf16[896,384]{1,0:T(8,128)(2,1)}) custom-call(f32[384,896]{1,0:T(8,128)} %copy-done.7, bf16[384,896]{1,0:T(8,128)(2,1)S(1)} %collective-permute-done.4.gate_on, bf16[384,896]{1,0:T(8,128)(2,1)S(1)} %collective-permute-done.7.gate_back, f32[384,896]{1,0:T(8,128)} %copy-done.8, ...), custom_call_target="tpu_custom_call" | custom-call | bytes 8257536 | tf_op jit(solution)/shard_map/owner/pallas_call | solution.py:98
  152.9 5.5 %input_grad.8.sum_ref = f32[2,384,1024]{2,1,0:T(8,128)} custom-call(s32[2]{0:T(128)S(1)} %pad_add_fusion.10.at, f32[2,384,1024]{2,1,0:T(8,128)} %broadcast_in_dim.31.sum_ref, bf16[384,896]{1,0:T(8,128)(2,1)S(1)} %get-tuple-element.70.gd_ref.refs_2_, bf16[384,896]{1,0:T(8,128)(2,1)} %get-tuple-element.71.ud_ref.refs_4_, ...), custom_call_target="tpu_custom_call", output_to_operand_aliasing={{}: (1, {})} | custom-call | flops 1409286144 | bytes 6815744 | tf_op jit(solution)/shard_map/input_grad/pallas_call | solution.py:168
  165.9 11.5 %collective-permute-done.18.gd_ref.refs_3_ = bf16[384,896]{1,0:T(8,128)(2,1)} collective-permute-done((bf16[384,896]{1,0:T(8,128)(2,1)S(1)}, bf16[384,896]{1,0:T(8,128)(2,1)}, u32[]{:S(2)}, u32[]{:S(2)}) %collective-permute-start.18) | collective-permute-done | bytes 688160 | tf_op jit(solution)/shard_map/ppermute | solution.py:309
  183.3 5.3 %collective-permute-start.38 = (bf16[896,384]{1,0:T(8,128)(2,1)}, bf16[896,384]{1,0:T(8,128)(2,1)}, u32[]{:S(2)}, u32[]{:S(2)}) collective-permute-start(bf16[896,384]{1,0:T(8,128)(2,1)} %get-tuple-element.91), channel_id=1, source_target_pairs={{0,0},{28,1},{8,2},{20,3},{16,4},{12,5},{24,6},{4,7},{13,8},{17,9}... | collective-permute-start | bytes 2064392 | tf_op jit(solution)/shard_map/ppermute | solution.py:367
  188.8 5.7 %input_grad.9.sum_ref = f32[2,384,1024]{2,1,0:T(8,128)} custom-call(s32[2]{0:T(128)S(1)} %pad_add_fusion.12.at, f32[2,384,1024]{2,1,0:T(8,128)} %input_grad.8.sum_ref, bf16[384,896]{1,0:T(8,128)(2,1)} %collective-permute-done.18.gd_ref.refs_3_, bf16[384,896]{1,0:T(8,128)(2,1)} %collective-permute-done.21.ud_ref.refs_5_, ...), custom_call_target="tpu_custom_call", output_to_operand_aliasing={{}: (1, {})} | custom-call | flops 1409286144 | bytes 6815744 | tf_op jit(solution)/shard_map/input_grad/pallas_call | solution.py:168
  194.5 5.8 %input_grad.10.sum_ref = f32[2,384,1024]{2,1,0:T(8,128)} custom-call(s32[2]{0:T(128)S(1)} %pad_add_fusion.11.at, f32[2,384,1024]{2,1,0:T(8,128)} %input_grad.9.sum_ref, bf16[384,896]{1,0:T(8,128)(2,1)} %collective-permute-done.23.gd_ref.refs_2_, bf16[384,896]{1,0:T(8,128)(2,1)} %collective-permute-done.24.ud_ref.refs_4_, ...), custom_call_target="tpu_custom_call", output_to_operand_aliasing={{}: (1, {})} | custom-call | flops 1409286144 | bytes 6815744 | tf_op jit(solution)/shard_map/input_grad/pallas_call | solution.py:168
  200.3 6.6 %collective-permute-done.19.gd_ref.refs_3_ = bf16[384,896]{1,0:T(8,128)(2,1)} collective-permute-done((bf16[384,896]{1,0:T(8,128)(2,1)}, bf16[384,896]{1,0:T(8,128)(2,1)}, u32[]{:S(2)}, u32[]{:S(2)}) %collective-permute-start.19) | collective-permute-done | bytes 688160 | tf_op jit(solution)/shard_map/ppermute | solution.py:309
  218.9 21.4 %collective-permute-done.38.refs_0_ = bf16[896,384]{1,0:T(8,128)(2,1)} collective-permute-done((bf16[896,384]{1,0:T(8,128)(2,1)}, bf16[896,384]{1,0:T(8,128)(2,1)}, u32[]{:S(2)}, u32[]{:S(2)}) %collective-permute-start.38) | collective-permute-done | bytes 688160 | tf_op jit(solution)/shard_map/ppermute | solution.py:367
  240.3 5.7 %input_grad.11.sum_ref = f32[2,384,1024]{2,1,0:T(8,128)} custom-call(s32[2]{0:T(128)S(1)} %pad_add_fusion.9.at, f32[2,384,1024]{2,1,0:T(8,128)} %input_grad.10.sum_ref, bf16[384,896]{1,0:T(8,128)(2,1)} %collective-permute-done.19.gd_ref.refs_3_, bf16[384,896]{1,0:T(8,128)(2,1)} %collective-permute-done.22.ud_ref.refs_5_, ...), custom_call_target="tpu_custom_call", output_to_operand_aliasing={{}: (1, {})} | custom-call | flops 1409286144 | bytes 6815744 | tf_op jit(solution)/shard_map/input_grad/pallas_call | solution.py:168
  246.0 5.7 %input_grad.12.sum_ref = f32[2,384,1024]{2,1,0:T(8,128)} custom-call(s32[2]{0:T(128)S(1)} %pad_add_fusion.8.at, f32[2,384,1024]{2,1,0:T(8,128)} %input_grad.11.sum_ref, bf16[384,896]{1,0:T(8,128)(2,1)} %collective-permute-done.25.gd_ref.refs_2_, bf16[384,896]{1,0:T(8,128)(2,1)} %collective-permute-done.26.ud_ref.refs_4_, ...), custom_call_target="tpu_custom_call", output_to_operand_aliasing={{}: (1, {})} | custom-call | flops 1409286144 | bytes 6815744 | tf_op jit(solution)/shard_map/input_grad/pallas_call | solution.py:168
  251.7 8.4 %weight_grads.4 = (bf16[1024,3584]{1,0:T(8,128)(2,1)}, bf16[1024,3584]{1,0:T(8,128)(2,1)}) custom-call(s32[3]{0:T(128)S(1)} %pad_add_fusion.7.at, bf16[2,1024,384]{2,1,0:T(8,128)(2,1)} %bitcast.102, bf16[2,1024,384]{2,1,0:T(8,128)(2,1)} %bitcast.103, bf16[384,896]{1,0:T(8,128)(2,1)} %collective-permute-done.25.gd_ref.refs_2_, ...), custom_call_target="tpu_custom_call" | custom-call | flops 2818572288 | bytes 6422528 | tf_op jit(solution)/shard_map/weight_grads/pallas_call | solution.py:213
  260.1 5.7 %collective-permute-start.30 = (bf16[384,896]{1,0:T(8,128)(2,1)}, bf16[384,896]{1,0:T(8,128)(2,1)S(1)}, u32[]{:S(2)}, u32[]{:S(2)}) collective-permute-start(bf16[384,896]{1,0:T(8,128)(2,1)} %collective-permute-done.20.gd_ref.refs_3_), channel_id=1, source_target_pairs={{0,8},{8,16},{16,24},{24,28},{28,20},{20,12},{12,4},{4,0},{1,9},{9... | collective-permute-start | bytes 2064392 | tf_op jit(solution)/shard_map/ppermute | solution.py:309
  265.9 5.7 %input_grad.13.sum_ref = f32[2,384,1024]{2,1,0:T(8,128)} custom-call(s32[2]{0:T(128)S(1)} %pad_add_fusion.2.at, f32[2,384,1024]{2,1,0:T(8,128)} %input_grad.12.sum_ref, bf16[384,896]{1,0:T(8,128)(2,1)} %collective-permute-done.20.gd_ref.refs_3_, bf16[384,896]{1,0:T(8,128)(2,1)} %collective-permute-done.27.ud_ref.refs_5_, ...), custom_call_target="tpu_custom_call", output_to_operand_aliasing={{}: (1, {})} | custom-call | flops 1409286144 | bytes 6815744 | tf_op jit(solution)/shard_map/input_grad/pallas_call | solution.py:168
  271.6 5.7 %input_grad.14.sum_ref = f32[2,384,1024]{2,1,0:T(8,128)} custom-call(s32[2]{0:T(128)S(1)} %pad_add_fusion.1.at, f32[2,384,1024]{2,1,0:T(8,128)} %input_grad.13.sum_ref, bf16[384,896]{1,0:T(8,128)(2,1)} %collective-permute-done.28.gd_ref.refs_2_, bf16[384,896]{1,0:T(8,128)(2,1)} %collective-permute-done.29.ud_ref.refs_4_, ...), custom_call_target="tpu_custom_call", output_to_operand_aliasing={{}: (1, {})} | custom-call | flops 1409286144 | bytes 6815744 | tf_op jit(solution)/shard_map/input_grad/pallas_call | solution.py:168
  277.3 8.4 %weight_grads.5 = (bf16[1024,3584]{1,0:T(8,128)(2,1)}, bf16[1024,3584]{1,0:T(8,128)(2,1)}) custom-call(s32[3]{0:T(128)S(1)} %pad_add_fusion.13.at, bf16[2,1024,384]{2,1,0:T(8,128)(2,1)} %bitcast.104, bf16[2,1024,384]{2,1,0:T(8,128)(2,1)} %bitcast.105, ...), custom_call_target="tpu_custom_call", output_to_operand_aliasing={{0}: (9, {}), {1}: (10, {})} | custom-call | flops 2818572288 | bytes 6422528 | tf_op jit(solution)/shard_map/weight_grads/pallas_call | solution.py:213
  285.6 8.4 %weight_grads.6 = (bf16[1024,3584]{1,0:T(8,128)(2,1)}, bf16[1024,3584]{1,0:T(8,128)(2,1)}) custom-call(s32[3]{0:T(128)S(1)} %get-tuple-element.101.at, bf16[2,1024,384]{2,1,0:T(8,128)(2,1)} %bitcast.106, bf16[2,1024,384]{2,1,0:T(8,128)(2,1)} %bitcast.107, ...), custom_call_target="tpu_custom_call", output_to_operand_aliasing={{0}: (9, {}), {1}: (10, {})} | custom-call | flops 2818572288 | bytes 6422528 | tf_op jit(solution)/shard_map/weight_grads/pallas_call | solution.py:213
  294.0 5.3 %input_grad.15 = f32[2,384,1024]{2,1,0:T(8,128)} custom-call(s32[2]{0:T(128)S(1)} %pad_add_fusion.at, f32[2,384,1024]{2,1,0:T(8,128)} %input_grad.14.sum_ref, bf16[384,896]{1,0:T(8,128)(2,1)S(1)} %collective-permute-done.30.gd_ref.refs_3_, bf16[384,896]{1,0:T(8,128)(2,1)S(1)} %collective-permute-done.31.ud_ref.refs_5_, ...), custom_call_target="tpu_custom_call", output_to_operand_aliasing={{}: (1, {})} | custom-call | flops 1409286144 | bytes 6815744 | tf_op jit(solution)/shard_map/input_grad/pallas_call | solution.py:168
  302.7 4.7 %collective-permute-start.35 = (f32[192,1024]{1,0:T(8,128)}, f32[192,1024]{1,0:T(8,128)}, u32[]{:S(2)}, u32[]{:S(2)}) collective-permute-start(f32[192,1024]{1,0:T(8,128)} %dynamic-slice_bitcast_fusion), channel_id=1, source_target_pairs={{0,1},{1,0},{2,3},{3,2},{4,5},{5,4},{6,7},{7,6},{8,9},{9,8},{10,11... | collective-permute-start | bytes 2359304 | tf_op jit(solution)/shard_map/ppermute | solution.py:433
  309.1 8.0 %down_grad.2.refs_5_ = bf16[1792,2048]{1,0:T(8,128)(2,1)} custom-call(s32[3]{0:T(128)S(1)} %add_add_fusion.1.at, bf16[896,384]{1,0:T(8,128)(2,1)} %collective-permute-done.38.refs_0_, bf16[896,384]{1,0:T(8,128)(2,1)} %collective-permute-done.41.refs_1_, bf16[2,384,2048]{2,1,0:T(8,128)(2,1)} %bitcast.110, bf16[2,384,2048]{2,1,0:T(8,128)(2,1)} %bitcast.111, ...), custom_call_target="tpu_custom_call" | custom-call | flops 2818572288 | bytes 6815744 | tf_op jit(solution)/shard_map/down_grad/pallas_call | solution.py:254
  321.4 7.8 %down_grad.3 = bf16[1792,2048]{1,0:T(8,128)(2,1)} custom-call(s32[3]{0:T(128)S(1)} %add_add_fusion.at, bf16[896,384]{1,0:T(8,128)(2,1)} %collective-permute-done.39.refs_0_, bf16[896,384]{1,0:T(8,128)(2,1)S(1)} %collective-permute-done.40.refs_1_, bf16[2,384,2048]{2,1,0:T(8,128)(2,1)} %bitcast.112, ...), custom_call_target="tpu_custom_call", output_to_operand_aliasing={{}: (6, {})} | custom-call | flops 2818572288 | bytes 6815744 | tf_op jit(solution)/shard_map/down_grad/pallas_call | solution.py:254
  330.9 6.7 %collective-permute-done.33 = bf16[192,1024]{1,0:T(8,128)(2,1)S(1)} collective-permute-done((bf16[192,1024]{1,0:T(8,128)(2,1)S(1)}, bf16[192,1024]{1,0:T(8,128)(2,1)S(1)}, u32[]{:S(2)}, u32[]{:S(2)}) %collective-permute-start.33) | collective-permute-done | bytes 393248 | tf_op jit(solution)/shard_map/ppermute | solution.py:433
  338.7 7.7 %weight_grads.7 = (bf16[1024,3584]{1,0:T(8,128)(2,1)}, bf16[1024,3584]{1,0:T(8,128)(2,1)}) custom-call(s32[3]{0:T(128)S(1)} %pad_add_fusion.14.at, bf16[2,1024,384]{2,1,0:T(8,128)(2,1)} %bitcast.108, bf16[2,1024,384]{2,1,0:T(8,128)(2,1)} %bitcast.109, ...), custom_call_target="tpu_custom_call", output_to_operand_aliasing={{0}: (9, {}), {1}: (10, {})} | custom-call | flops 2818572288 | bytes 6422528 | tf_op jit(solution)/shard_map/weight_grads/pallas_call | solution.py:213
  (174 shorter events, 98.9 us)
Async XLA Ops:
  9.1 37.1 %collective-permute-start = (bf16[384,896]{1,0:T(8,128)(2,1)}, bf16[384,896]{1,0:T(8,128)(2,1)S(1)}, u32[]{:S(2)}, u32[]{:S(2)}) collective-permute-start(bf16[384,896]{1,0:T(8,128)(2,1)} %get-tuple-element.52), channel_id=1, source_target_pairs={{0,8},{8,16},{16,24},{24,28},{28,20},{20,12},{12,4},{4,0},{1,9},{9... | collective-permute-start | bytes 2064392 | tf_op jit(solution)/shard_map/ppermute | solution.py:309
  16.2 30.1 %collective-permute-start.1 = (bf16[384,896]{1,0:T(8,128)(2,1)}, bf16[384,896]{1,0:T(8,128)(2,1)S(1)}, u32[]{:S(2)}, u32[]{:S(2)}) collective-permute-start(bf16[384,896]{1,0:T(8,128)(2,1)} %get-tuple-element.53), channel_id=1, source_target_pairs={{8,0},{16,8},{24,16},{28,24},{20,28},{12,20},{4,12},{0,4},{9,1},{1... | collective-permute-start | bytes 2064392 | tf_op jit(solution)/shard_map/ppermute | solution.py:312
  21.8 26.9 %collective-permute-start.5 = (bf16[384,896]{1,0:T(8,128)(2,1)}, bf16[384,896]{1,0:T(8,128)(2,1)}, u32[]{:S(2)}, u32[]{:S(2)}) collective-permute-start(bf16[384,896]{1,0:T(8,128)(2,1)} %get-tuple-element.57), channel_id=1, source_target_pairs={{8,0},{16,8},{24,16},{28,24},{20,28},{12,20},{4,12},{0,4},{9,1},{1... | collective-permute-start | bytes 2064392 | tf_op jit(solution)/shard_map/ppermute | solution.py:312
  27.3 22.8 %collective-permute-start.8 = (bf16[384,896]{1,0:T(8,128)(2,1)}, bf16[384,896]{1,0:T(8,128)(2,1)}, u32[]{:S(2)}, u32[]{:S(2)}) collective-permute-start(bf16[384,896]{1,0:T(8,128)(2,1)} %get-tuple-element.61), channel_id=1, source_target_pairs={{0,8},{8,16},{16,24},{24,28},{28,20},{20,12},{12,4},{4,0},{1,9},{9... | collective-permute-start | bytes 2064392 | tf_op jit(solution)/shard_map/ppermute | solution.py:309
  47.3 21.7 %collective-permute-start.2 = (bf16[384,896]{1,0:T(8,128)(2,1)}, bf16[384,896]{1,0:T(8,128)(2,1)S(1)}, u32[]{:S(2)}, u32[]{:S(2)}) collective-permute-start(bf16[384,896]{1,0:T(8,128)(2,1)} %add_convert_fusion.9), channel_id=1, source_target_pairs={{0,8},{8,16},{16,24},{24,28},{28,20},{20,12},{12,4},{4,0},{1,9},{9... | collective-permute-start | bytes 2064392 | tf_op jit(solution)/shard_map/ppermute | solution.py:309
  49.9 19.4 %collective-permute-start.6 = (bf16[384,896]{1,0:T(8,128)(2,1)S(1)}, bf16[384,896]{1,0:T(8,128)(2,1)S(1)}, u32[]{:S(2)}, u32[]{:S(2)}) collective-permute-start(bf16[384,896]{1,0:T(8,128)(2,1)S(1)} %add_convert_fusion.6), channel_id=1, source_target_pairs={{8,0},{16,8},{24,16},{28,24},{20,28},{12,20},{4,12},{0,4},{9,1},{1... | collective-permute-start | bytes 2064392 | tf_op jit(solution)/shard_map/ppermute | solution.py:312
  52.2 30.8 %collective-permute-start.9 = (bf16[384,896]{1,0:T(8,128)(2,1)}, bf16[384,896]{1,0:T(8,128)(2,1)S(1)}, u32[]{:S(2)}, u32[]{:S(2)}) collective-permute-start(bf16[384,896]{1,0:T(8,128)(2,1)} %add_convert_fusion.4), channel_id=1, source_target_pairs={{0,8},{8,16},{16,24},{24,28},{28,20},{20,12},{12,4},{4,0},{1,9},{9... | collective-permute-start | bytes 2064392 | tf_op jit(solution)/shard_map/ppermute | solution.py:309
  54.5 25.2 %collective-permute-start.11 = (bf16[384,896]{1,0:T(8,128)(2,1)}, bf16[384,896]{1,0:T(8,128)(2,1)}, u32[]{:S(2)}, u32[]{:S(2)}) collective-permute-start(bf16[384,896]{1,0:T(8,128)(2,1)} %add_convert_fusion.2), channel_id=1, source_target_pairs={{8,0},{16,8},{24,16},{28,24},{20,28},{12,20},{4,12},{0,4},{9,1},{1... | collective-permute-start | bytes 2064392 | tf_op jit(solution)/shard_map/ppermute | solution.py:312
  69.3 22.9 %collective-permute-start.3 = (bf16[384,896]{1,0:T(8,128)(2,1)S(1)}, bf16[384,896]{1,0:T(8,128)(2,1)S(1)}, u32[]{:S(2)}, u32[]{:S(2)}) collective-permute-start(bf16[384,896]{1,0:T(8,128)(2,1)S(1)} %add_convert_fusion.8), channel_id=1, source_target_pairs={{0,8},{8,16},{16,24},{24,28},{28,20},{20,12},{12,4},{4,0},{1,9},{9... | collective-permute-start | bytes 2064392 | tf_op jit(solution)/shard_map/ppermute | solution.py:309
  79.6 32.4 %collective-permute-start.7 = (bf16[384,896]{1,0:T(8,128)(2,1)S(1)}, bf16[384,896]{1,0:T(8,128)(2,1)S(1)}, u32[]{:S(2)}, u32[]{:S(2)}) collective-permute-start(bf16[384,896]{1,0:T(8,128)(2,1)S(1)} %add_convert_fusion.5), channel_id=1, source_target_pairs={{8,0},{16,8},{24,16},{28,24},{20,28},{12,20},{4,12},{0,4},{9,1},{1... | collective-permute-start | bytes 2064392 | tf_op jit(solution)/shard_map/ppermute | solution.py:312
  81.0 27.3 %collective-permute-start.12 = (bf16[384,896]{1,0:T(8,128)(2,1)S(1)}, bf16[384,896]{1,0:T(8,128)(2,1)S(1)}, u32[]{:S(2)}, u32[]{:S(2)}) collective-permute-start(bf16[384,896]{1,0:T(8,128)(2,1)S(1)} %add_convert_fusion.1), channel_id=1, source_target_pairs={{8,0},{16,8},{24,16},{28,24},{20,28},{12,20},{4,12},{0,4},{9,1},{1... | collective-permute-start | bytes 2064392 | tf_op jit(solution)/shard_map/ppermute | solution.py:312
  81.8 26.9 %collective-permute-start.16 = (bf16[1,384,896]{2,1,0:T(8,128)(2,1)S(1)}, bf16[1,384,896]{2,1,0:T(8,128)(2,1)S(1)}, u32[]{:S(2)}, u32[]{:S(2)}) collective-permute-start(bf16[1,384,896]{2,1,0:T(8,128)(2,1)S(1)} %fusion.3), channel_id=1, source_target_pairs={{0,2},{1,3},{2,0},{3,1},{4,6},{5,7},{6,4},{7,5},{8,10},{9,11},{10,... | collective-permute-start | bytes 2064392 | tf_op jit(solution)/shard_map/ppermute | solution.py:317
  83.2 28.9 %collective-permute-start.10 = (bf16[384,896]{1,0:T(8,128)(2,1)S(1)}, bf16[384,896]{1,0:T(8,128)(2,1)S(1)}, u32[]{:S(2)}, u32[]{:S(2)}) collective-permute-start(bf16[384,896]{1,0:T(8,128)(2,1)S(1)} %add_convert_fusion.3), channel_id=1, source_target_pairs={{0,8},{8,16},{16,24},{24,28},{28,20},{20,12},{12,4},{4,0},{1,9},{9... | collective-permute-start | bytes 2064392 | tf_op jit(solution)/shard_map/ppermute | solution.py:309
  92.3 29.3 %collective-permute-start.4 = (bf16[384,896]{1,0:T(8,128)(2,1)S(1)}, bf16[384,896]{1,0:T(8,128)(2,1)S(1)}, u32[]{:S(2)}, u32[]{:S(2)}) collective-permute-start(bf16[384,896]{1,0:T(8,128)(2,1)S(1)} %add_convert_fusion.7), channel_id=1, source_target_pairs={{0,8},{8,16},{16,24},{24,28},{28,20},{20,12},{12,4},{4,0},{1,9},{9... | collective-permute-start | bytes 2064392 | tf_op jit(solution)/shard_map/ppermute | solution.py:309
  108.8 29.0 %collective-permute-start.17 = (bf16[384,896]{1,0:T(8,128)(2,1)S(1)}, bf16[384,896]{1,0:T(8,128)(2,1)S(1)}, u32[]{:S(2)}, u32[]{:S(2)}) collective-permute-start(bf16[384,896]{1,0:T(8,128)(2,1)S(1)} %fusion.4), channel_id=1, source_target_pairs={{0,0},{1,28},{2,8},{3,20},{4,16},{5,12},{6,24},{7,4},{8,13},{9,17}... | collective-permute-start | bytes 2064392 | tf_op jit(solution)/shard_map/ppermute | solution.py:348
  145.0 17.6 %collective-permute-start.21 = (bf16[384,896]{1,0:T(8,128)(2,1)}, bf16[384,896]{1,0:T(8,128)(2,1)}, u32[]{:S(2)}, u32[]{:S(2)}) collective-permute-start(bf16[384,896]{1,0:T(8,128)(2,1)} %get-tuple-element.71.ud_ref.refs_4_), channel_id=1, source_target_pairs={{0,8},{8,16},{16,24},{24,28},{28,20},{20,12},{12,4},{4,0},{1,9},{9... | collective-permute-start | bytes 2064392 | tf_op jit(solution)/shard_map/ppermute | solution.py:309
  147.8 29.6 %collective-permute-start.18 = (bf16[384,896]{1,0:T(8,128)(2,1)S(1)}, bf16[384,896]{1,0:T(8,128)(2,1)}, u32[]{:S(2)}, u32[]{:S(2)}) collective-permute-start(bf16[384,896]{1,0:T(8,128)(2,1)S(1)} %get-tuple-element.70.gd_ref.refs_2_), channel_id=1, source_target_pairs={{0,8},{8,16},{16,24},{24,28},{28,20},{20,12},{12,4},{4,0},{1,9},{9... | collective-permute-start | bytes 2064392 | tf_op jit(solution)/shard_map/ppermute | solution.py:309
  150.3 30.2 %collective-permute-start.24 = (bf16[384,896]{1,0:T(8,128)(2,1)}, bf16[384,896]{1,0:T(8,128)(2,1)}, u32[]{:S(2)}, u32[]{:S(2)}) collective-permute-start(bf16[384,896]{1,0:T(8,128)(2,1)} %get-tuple-element.71.ud_ref.refs_4_), channel_id=1, source_target_pairs={{8,0},{16,8},{24,16},{28,24},{20,28},{12,20},{4,12},{0,4},{9,1},{1... | collective-permute-start | bytes 2064392 | tf_op jit(solution)/shard_map/ppermute | solution.py:312
  150.3 32.1 %collective-permute-start.23 = (bf16[384,896]{1,0:T(8,128)(2,1)S(1)}, bf16[384,896]{1,0:T(8,128)(2,1)}, u32[]{:S(2)}, u32[]{:S(2)}) collective-permute-start(bf16[384,896]{1,0:T(8,128)(2,1)S(1)} %get-tuple-element.70.gd_ref.refs_2_), channel_id=1, source_target_pairs={{8,0},{16,8},{24,16},{28,24},{20,28},{12,20},{4,12},{0,4},{9,1},{1... | collective-permute-start | bytes 2064392 | tf_op jit(solution)/shard_map/ppermute | solution.py:312
  162.6 37.6 %collective-permute-start.22 = (bf16[384,896]{1,0:T(8,128)(2,1)}, bf16[384,896]{1,0:T(8,128)(2,1)}, u32[]{:S(2)}, u32[]{:S(2)}) collective-permute-start(bf16[384,896]{1,0:T(8,128)(2,1)} %collective-permute-done.21.ud_ref.refs_5_), channel_id=1, source_target_pairs={{0,8},{8,16},{16,24},{24,28},{28,20},{20,12},{12,4},{4,0},{1,9},{9... | collective-permute-start | bytes 2064392 | tf_op jit(solution)/shard_map/ppermute | solution.py:309
  177.4 29.5 %collective-permute-start.19 = (bf16[384,896]{1,0:T(8,128)(2,1)}, bf16[384,896]{1,0:T(8,128)(2,1)}, u32[]{:S(2)}, u32[]{:S(2)}) collective-permute-start(bf16[384,896]{1,0:T(8,128)(2,1)} %collective-permute-done.18.gd_ref.refs_3_), channel_id=1, source_target_pairs={{0,8},{8,16},{16,24},{24,28},{28,20},{20,12},{12,4},{4,0},{1,9},{9... | collective-permute-start | bytes 2064392 | tf_op jit(solution)/shard_map/ppermute | solution.py:309
  180.6 29.6 %collective-permute-start.26 = (bf16[384,896]{1,0:T(8,128)(2,1)}, bf16[384,896]{1,0:T(8,128)(2,1)}, u32[]{:S(2)}, u32[]{:S(2)}) collective-permute-start(bf16[384,896]{1,0:T(8,128)(2,1)} %collective-permute-done.24.ud_ref.refs_4_), channel_id=1, source_target_pairs={{8,0},{16,8},{24,16},{28,24},{20,28},{12,20},{4,12},{0,4},{9,1},{1... | collective-permute-start | bytes 2064392 | tf_op jit(solution)/shard_map/ppermute | solution.py:312
  182.5 30.9 %collective-permute-start.25 = (bf16[384,896]{1,0:T(8,128)(2,1)}, bf16[384,896]{1,0:T(8,128)(2,1)}, u32[]{:S(2)}, u32[]{:S(2)}) collective-permute-start(bf16[384,896]{1,0:T(8,128)(2,1)} %collective-permute-done.23.gd_ref.refs_2_), channel_id=1, source_target_pairs={{8,0},{16,8},{24,16},{28,24},{20,28},{12,20},{4,12},{0,4},{9,1},{1... | collective-permute-start | bytes 2064392 | tf_op jit(solution)/shard_map/ppermute | solution.py:312
  183.3 57.0 %collective-permute-start.38 = (bf16[896,384]{1,0:T(8,128)(2,1)}, bf16[896,384]{1,0:T(8,128)(2,1)}, u32[]{:S(2)}, u32[]{:S(2)}) collective-permute-start(bf16[896,384]{1,0:T(8,128)(2,1)} %get-tuple-element.91), channel_id=1, source_target_pairs={{0,0},{28,1},{8,2},{20,3},{16,4},{12,5},{24,6},{4,7},{13,8},{17,9}... | collective-permute-start | bytes 2064392 | tf_op jit(solution)/shard_map/ppermute | solution.py:367
  200.3 59.8 %collective-permute-start.27 = (bf16[384,896]{1,0:T(8,128)(2,1)}, bf16[384,896]{1,0:T(8,128)(2,1)}, u32[]{:S(2)}, u32[]{:S(2)}) collective-permute-start(bf16[384,896]{1,0:T(8,128)(2,1)} %collective-permute-done.22.ud_ref.refs_5_), channel_id=1, source_target_pairs={{0,8},{8,16},{16,24},{24,28},{28,20},{20,12},{12,4},{4,0},{1,9},{9... | collective-permute-start | bytes 2064392 | tf_op jit(solution)/shard_map/ppermute | solution.py:309
  206.9 53.2 %collective-permute-start.20 = (bf16[384,896]{1,0:T(8,128)(2,1)}, bf16[384,896]{1,0:T(8,128)(2,1)}, u32[]{:S(2)}, u32[]{:S(2)}) collective-permute-start(bf16[384,896]{1,0:T(8,128)(2,1)} %collective-permute-done.19.gd_ref.refs_3_), channel_id=1, source_target_pairs={{0,8},{8,16},{16,24},{24,28},{28,20},{20,12},{12,4},{4,0},{1,9},{9... | collective-permute-start | bytes 2064392 | tf_op jit(solution)/shard_map/ppermute | solution.py:309
  210.2 55.7 %collective-permute-start.29 = (bf16[384,896]{1,0:T(8,128)(2,1)}, bf16[384,896]{1,0:T(8,128)(2,1)}, u32[]{:S(2)}, u32[]{:S(2)}) collective-permute-start(bf16[384,896]{1,0:T(8,128)(2,1)} %collective-permute-done.26.ud_ref.refs_4_), channel_id=1, source_target_pairs={{8,0},{16,8},{24,16},{28,24},{20,28},{12,20},{4,12},{0,4},{9,1},{1... | collective-permute-start | bytes 2064392 | tf_op jit(solution)/shard_map/ppermute | solution.py:312
  213.4 58.2 %collective-permute-start.28 = (bf16[384,896]{1,0:T(8,128)(2,1)}, bf16[384,896]{1,0:T(8,128)(2,1)}, u32[]{:S(2)}, u32[]{:S(2)}) collective-permute-start(bf16[384,896]{1,0:T(8,128)(2,1)} %collective-permute-done.25.gd_ref.refs_2_), channel_id=1, source_target_pairs={{8,0},{16,8},{24,16},{28,24},{20,28},{12,20},{4,12},{0,4},{9,1},{1... | collective-permute-start | bytes 2064392 | tf_op jit(solution)/shard_map/ppermute | solution.py:312
  240.3 68.5 %collective-permute-start.39 = (bf16[896,384]{1,0:T(8,128)(2,1)}, bf16[896,384]{1,0:T(8,128)(2,1)}, u32[]{:S(2)}, u32[]{:S(2)}) collective-permute-start(bf16[896,384]{1,0:T(8,128)(2,1)} %collective-permute-done.38.refs_0_), channel_id=1, source_target_pairs={{0,2},{1,3},{2,0},{3,1},{4,6},{5,7},{6,4},{7,5},{8,10},{9,11},{10,... | collective-permute-start | bytes 2064392 | tf_op jit(solution)/shard_map/ppermute | solution.py:317
  260.0 49.1 %collective-permute-start.41 = (bf16[896,384]{1,0:T(8,128)(2,1)}, bf16[896,384]{1,0:T(8,128)(2,1)}, u32[]{:S(2)}, u32[]{:S(2)}) collective-permute-start(bf16[896,384]{1,0:T(8,128)(2,1)} %collective-permute-done.38.refs_0_), channel_id=1, source_target_pairs={{0,1},{1,0},{2,3},{3,2},{4,5},{5,4},{6,7},{7,6},{8,9},{9,8},{10,11... | collective-permute-start | bytes 2064392 | tf_op jit(solution)/shard_map/ppermute | solution.py:317
  260.1 33.9 %collective-permute-start.30 = (bf16[384,896]{1,0:T(8,128)(2,1)}, bf16[384,896]{1,0:T(8,128)(2,1)S(1)}, u32[]{:S(2)}, u32[]{:S(2)}) collective-permute-start(bf16[384,896]{1,0:T(8,128)(2,1)} %collective-permute-done.20.gd_ref.refs_3_), channel_id=1, source_target_pairs={{0,8},{8,16},{16,24},{24,28},{28,20},{20,12},{12,4},{4,0},{1,9},{9... | collective-permute-start | bytes 2064392 | tf_op jit(solution)/shard_map/ppermute | solution.py:309
  265.8 28.2 %collective-permute-start.31 = (bf16[384,896]{1,0:T(8,128)(2,1)}, bf16[384,896]{1,0:T(8,128)(2,1)S(1)}, u32[]{:S(2)}, u32[]{:S(2)}) collective-permute-start(bf16[384,896]{1,0:T(8,128)(2,1)} %collective-permute-done.29.ud_ref.refs_4_), channel_id=1, source_target_pairs={{8,0},{16,8},{24,16},{28,24},{20,28},{12,20},{4,12},{0,4},{9,1},{1... | collective-permute-start | bytes 2064392 | tf_op jit(solution)/shard_map/ppermute | solution.py:312
  (32 other events, 525.0 us)

commit v5 on v4

--- a/solution.py
+++ b/solution.py
@@ -281,7 +281,7 @@
     place = [ring.index(r) for r in range(rows)]
     ahead = [(ring[p], ring[(p + 1) % rows]) for p in range(rows)]
     back = [(b, a) for a, b in ahead]
-    turn = [(0, 2, 4, 6)[c % 4] for c in range(cols)]
+    turn = [(0, 6, 4, 2)[c % 4] for c in range(cols)]
     me = jnp.array(place, jnp.int32)[lax.axis_index("row")]
     me = lax.rem(me + jnp.array(turn, jnp.int32)[lax.axis_index("col")], rows)
 

time: 350 us -> 351 us (level)
  waiting for transfers between devices: 108 us -> 80.7 us
  starting transfers between devices: 61.8 us -> 88.6 us
    ppermute x1, waiting for transfers between devices: 21.4 us -> 0.01 us  [on_device(): hiddens = {0: lax.ppermute(hidden_t, ('row', 'col'), meet_back)}]
    ppermute x12, starting transfers between devices: 13.6 us -> 34.5 us  [across(): return lax.ppermute(array, 'col', [(c, c ^ bit) for c in range(cols)])]
    ppermute x1, waiting for transfers between devices: 15.6 us -> 0.01 us  [hidden_grad_of(): lax.ppermute(held.reshape(tokens, columns).astype(BF16), ('row', 'col'),...]
    ppermute x14, waiting for transfers between devices: 39.5 us -> 49.6 us  [onward(): return lax.ppermute(value, 'row', ahead)]
    ppermute x14, starting transfers between devices: 30.2 us -> 34.3 us  [onward(): return lax.ppermute(value, 'row', ahead)]
  transfers between devices with their start and end apart: 42 -> 42, of which waited for: 12 -> 10; matrix products, arithmetic and copies ran while one was open for 6% -> 6% of each run, Pallas kernels for 39% -> 39%
where the time goes in v5:
time: 351 us; the launch traced here: 350 us
  Pallas kernels  146 us (42%)
  starting transfers between devices  88.6 us (25%)
  waiting for transfers between devices  80.7 us (23%)
  local copies, waits for them, and re-layouts  17.8 us (5%)
  other arithmetic  13.8 us (4%)
    ppermute x14, waiting for transfers between devices, onward(): return lax.ppermute(value, 'row', ahead)  49.6 us
    pallas_call x8, Pallas kernels, add_input_grad(): pl.pallas_call(input_grad_kernel, name='input_grad', out_shape=jax.ShapeD...  45 us
    pallas_call x8, Pallas kernels, products(): pl.pallas_call(functools.partial(product_kernel, parts), name='products',...  34.6 us
    ppermute x12, starting transfers between devices, across(): return lax.ppermute(array, 'col', [(c, c ^ bit) for c in range(cols)])  34.5 us
    ppermute x14, starting transfers between devices, onward(): return lax.ppermute(value, 'row', ahead)  34.3 us
    pallas_call x4, Pallas kernels, weight_grads(): pl.pallas_call(functools.partial(weight_grads_kernel, parts), name='weigh...  32.8 us
    ppermute x14, waiting for transfers between devices, backward(): return lax.ppermute(value, 'row', back)  24.3 us
    pallas_call x2, Pallas kernels, down_grad_cut(): pl.pallas_call(functools.partial(down_grad_kernel, parts), name='down_gra...  15.8 us
  transfers between devices with their start and end apart: 42, of which 10 were waited for; matrix products, arithmetic and copies ran while one was open for 6% of the time, Pallas kernels for 39%

profile of v5, /device:TPU:9, one launch (start us, length us, event | category | flops | bytes accessed | tf_op | source)
XLA Modules:
  0.0 349.5 jit_solution(16307947631154486933)
XLA Ops:
  5.6 4.3 %products.8 = (bf16[384,896]{1,0:T(8,128)(2,1)}, f32[384,896]{1,0:T(8,128)S(1)}) custom-call(s32[3]{0:T(128)S(1)} %get-tuple-element.98.at, bf16[768,1024]{1,0:T(8,128)(2,1)} %x_ref.15, bf16[1024,3584]{1,0:T(8,128)(2,1)} %gw_ref.15, bf16[128,3584]{1,0:T(8,128)(2,1)S(1)} %bitcast.65), custom_call_target="tpu_custom_call" | custom-call | flops 1409286144 | bytes 5963776 | tf_op jit(solution)/shard_map/products/pallas_call | solution.py:63
  12.6 4.4 %products.12 = (bf16[384,896]{1,0:T(8,128)(2,1)}, f32[384,896]{1,0:T(8,128)S(1)}) custom-call(s32[3]{0:T(128)S(1)} %get-tuple-element.98.at, bf16[768,1024]{1,0:T(8,128)(2,1)} %x_ref.15, bf16[1024,3584]{1,0:T(8,128)(2,1)} %uw_ref.15, bf16[128,3584]{1,0:T(8,128)(2,1)S(1)} %bitcast.81), custom_call_target="tpu_custom_call" | custom-call | flops 1409286144 | bytes 5963776 | tf_op jit(solution)/shard_map/products/pallas_call | solution.py:63
  18.2 4.3 %products.9 = (bf16[384,896]{1,0:T(8,128)(2,1)}, f32[384,896]{1,0:T(8,128)S(1)}) custom-call(s32[3]{0:T(128)S(1)} %get-tuple-element.99.at, bf16[768,1024]{1,0:T(8,128)(2,1)} %x_ref.15, bf16[1024,3584]{1,0:T(8,128)(2,1)} %gw_ref.15, bf16[128,3584]{1,0:T(8,128)(2,1)S(1)} %bitcast.66), custom_call_target="tpu_custom_call" | custom-call | flops 1409286144 | bytes 5963776 | tf_op jit(solution)/shard_map/products/pallas_call | solution.py:63
  23.7 4.4 %products.15 = (bf16[384,896]{1,0:T(8,128)(2,1)}, f32[384,896]{1,0:T(8,128)S(1)}) custom-call(s32[3]{0:T(128)S(1)} %get-tuple-element.101.at, bf16[768,1024]{1,0:T(8,128)(2,1)} %x_ref.15, bf16[1024,3584]{1,0:T(8,128)(2,1)} %uw_ref.15, bf16[128,3584]{1,0:T(8,128)(2,1)S(1)} %bitcast.82), custom_call_target="tpu_custom_call" | custom-call | flops 1409286144 | bytes 5963776 | tf_op jit(solution)/shard_map/products/pallas_call | solution.py:63
  56.6 11.5 %hidden_grad.1 = (f32[2,1,384,896]{3,2,1,0:T(8,128)}, bf16[1,384,896]{2,1,0:T(8,128)(2,1)S(1)}, bf16[1,384,896]{2,1,0:T(8,128)(2,1)S(1)}) custom-call(s32[1]{0:T(128)} %bitcast.22.at, bf16[768,2048]{1,0:T(8,128)(2,1)} %g_ref, bf16[1792,2048]{1,0:T(8,128)(2,1)} %w_ref.17, bf16[224,2048]{1,0:T(8,128)(2,1)S(1)} %bitcast.97), custom_call_target="tpu_custom_call" | custom-call | flops 5637144576 | bytes 15990784 | tf_op jit(solution)/shard_map/hidden_grad/pallas_call | solution.py:135
  72.7 8.8 %collective-permute-done.11 = bf16[384,896]{1,0:T(8,128)(2,1)} collective-permute-done((bf16[384,896]{1,0:T(8,128)(2,1)}, bf16[384,896]{1,0:T(8,128)(2,1)}, u32[]{:S(2)}, u32[]{:S(2)}) %collective-permute-start.11) | collective-permute-done | bytes 688160 | tf_op jit(solution)/shard_map/ppermute | solution.py:312
  86.4 7.7 %collective-permute-done.3 = bf16[384,896]{1,0:T(8,128)(2,1)S(1)} collective-permute-done((bf16[384,896]{1,0:T(8,128)(2,1)S(1)}, bf16[384,896]{1,0:T(8,128)(2,1)S(1)}, u32[]{:S(2)}, u32[]{:S(2)}) %collective-permute-start.3) | collective-permute-done | bytes 688160 | tf_op jit(solution)/shard_map/ppermute | solution.py:309
  95.6 14.6 %collective-permute-done.12 = bf16[384,896]{1,0:T(8,128)(2,1)S(1)} collective-permute-done((bf16[384,896]{1,0:T(8,128)(2,1)S(1)}, bf16[384,896]{1,0:T(8,128)(2,1)S(1)}, u32[]{:S(2)}, u32[]{:S(2)}) %collective-permute-start.12) | collective-permute-done | bytes 688160 | tf_op jit(solution)/shard_map/ppermute | solution.py:312
  113.9 9.7 %collective-permute-done.4.gate_on = bf16[384,896]{1,0:T(8,128)(2,1)S(1)} collective-permute-done((bf16[384,896]{1,0:T(8,128)(2,1)S(1)}, bf16[384,896]{1,0:T(8,128)(2,1)S(1)}, u32[]{:S(2)}, u32[]{:S(2)}) %collective-permute-start.4) | collective-permute-done | bytes 688160 | tf_op jit(solution)/shard_map/ppermute | solution.py:309
  125.1 6.4 %owner.1 = (bf16[384,896]{1,0:T(8,128)(2,1)S(1)}, bf16[384,896]{1,0:T(8,128)(2,1)}, bf16[896,384]{1,0:T(8,128)(2,1)}) custom-call(f32[384,896]{1,0:T(8,128)} %copy-done.7, bf16[384,896]{1,0:T(8,128)(2,1)S(1)} %collective-permute-done.4.gate_on, bf16[384,896]{1,0:T(8,128)(2,1)S(1)} %collective-permute-done.7.gate_back, f32[384,896]{1,0:T(8,128)} %copy-done.8, ...), custom_call_target="tpu_custom_call" | custom-call | bytes 8257536 | tf_op jit(solution)/shard_map/owner/pallas_call | solution.py:98
  131.5 17.6 %collective-permute-start.21 = (bf16[384,896]{1,0:T(8,128)(2,1)}, bf16[384,896]{1,0:T(8,128)(2,1)}, u32[]{:S(2)}, u32[]{:S(2)}) collective-permute-start(bf16[384,896]{1,0:T(8,128)(2,1)} %get-tuple-element.71.ud_ref.refs_4_), channel_id=1, source_target_pairs={{0,8},{8,16},{16,24},{24,28},{28,20},{20,12},{12,4},{4,0},{1,9},{9... | collective-permute-start | bytes 2064392 | tf_op jit(solution)/shard_map/ppermute | solution.py:309
  156.6 5.5 %input_grad.8.sum_ref = f32[2,384,1024]{2,1,0:T(8,128)} custom-call(s32[2]{0:T(128)S(1)} %pad_add_fusion.10.at, f32[2,384,1024]{2,1,0:T(8,128)} %broadcast_in_dim.31.sum_ref, bf16[384,896]{1,0:T(8,128)(2,1)S(1)} %get-tuple-element.70.gd_ref.refs_2_, bf16[384,896]{1,0:T(8,128)(2,1)} %get-tuple-element.71.ud_ref.refs_4_, ...), custom_call_target="tpu_custom_call", output_to_operand_aliasing={{}: (1, {})} | custom-call | flops 1409286144 | bytes 6815744 | tf_op jit(solution)/shard_map/input_grad/pallas_call | solution.py:168
  162.1 7.1 %collective-permute-done.21.ud_ref.refs_5_ = bf16[384,896]{1,0:T(8,128)(2,1)} collective-permute-done((bf16[384,896]{1,0:T(8,128)(2,1)}, bf16[384,896]{1,0:T(8,128)(2,1)}, u32[]{:S(2)}, u32[]{:S(2)}) %collective-permute-start.21) | collective-permute-done | bytes 688160 | tf_op jit(solution)/shard_map/ppermute | solution.py:309
  169.2 14.7 %collective-permute-done.18.gd_ref.refs_3_ = bf16[384,896]{1,0:T(8,128)(2,1)} collective-permute-done((bf16[384,896]{1,0:T(8,128)(2,1)S(1)}, bf16[384,896]{1,0:T(8,128)(2,1)}, u32[]{:S(2)}, u32[]{:S(2)}) %collective-permute-start.18) | collective-permute-done | bytes 688160 | tf_op jit(solution)/shard_map/ppermute | solution.py:309
  187.0 4.5 %collective-permute-start.38 = (bf16[896,384]{1,0:T(8,128)(2,1)}, bf16[896,384]{1,0:T(8,128)(2,1)}, u32[]{:S(2)}, u32[]{:S(2)}) collective-permute-start(bf16[896,384]{1,0:T(8,128)(2,1)} %get-tuple-element.91), channel_id=1, source_target_pairs={{0,0},{28,1},{8,2},{20,3},{16,4},{12,5},{24,6},{4,7},{17,8},{13,9}... | collective-permute-start | bytes 2064392 | tf_op jit(solution)/shard_map/ppermute | solution.py:367
  191.7 5.7 %input_grad.9.sum_ref = f32[2,384,1024]{2,1,0:T(8,128)} custom-call(s32[2]{0:T(128)S(1)} %pad_add_fusion.12.at, f32[2,384,1024]{2,1,0:T(8,128)} %input_grad.8.sum_ref, bf16[384,896]{1,0:T(8,128)(2,1)} %collective-permute-done.18.gd_ref.refs_3_, bf16[384,896]{1,0:T(8,128)(2,1)} %collective-permute-done.21.ud_ref.refs_5_, ...), custom_call_target="tpu_custom_call", output_to_operand_aliasing={{}: (1, {})} | custom-call | flops 1409286144 | bytes 6815744 | tf_op jit(solution)/shard_map/input_grad/pallas_call | solution.py:168
  197.3 5.7 %input_grad.10.sum_ref = f32[2,384,1024]{2,1,0:T(8,128)} custom-call(s32[2]{0:T(128)S(1)} %pad_add_fusion.11.at, f32[2,384,1024]{2,1,0:T(8,128)} %input_grad.9.sum_ref, bf16[384,896]{1,0:T(8,128)(2,1)} %collective-permute-done.23.gd_ref.refs_2_, bf16[384,896]{1,0:T(8,128)(2,1)} %collective-permute-done.24.ud_ref.refs_4_, ...), custom_call_target="tpu_custom_call", output_to_operand_aliasing={{}: (1, {})} | custom-call | flops 1409286144 | bytes 6815744 | tf_op jit(solution)/shard_map/input_grad/pallas_call | solution.py:168
  203.0 10.4 %collective-permute-done.19.gd_ref.refs_3_ = bf16[384,896]{1,0:T(8,128)(2,1)} collective-permute-done((bf16[384,896]{1,0:T(8,128)(2,1)}, bf16[384,896]{1,0:T(8,128)(2,1)}, u32[]{:S(2)}, u32[]{:S(2)}) %collective-permute-start.19) | collective-permute-done | bytes 688160 | tf_op jit(solution)/shard_map/ppermute | solution.py:309
  223.2 15.6 %collective-permute-start.39 = (bf16[896,384]{1,0:T(8,128)(2,1)}, bf16[896,384]{1,0:T(8,128)(2,1)}, u32[]{:S(2)}, u32[]{:S(2)}) collective-permute-start(bf16[896,384]{1,0:T(8,128)(2,1)} %collective-permute-done.38.refs_0_), channel_id=1, source_target_pairs={{0,2},{1,3},{2,0},{3,1},{4,6},{5,7},{6,4},{7,5},{8,10},{9,11},{10,... | collective-permute-start | bytes 2064392 | tf_op jit(solution)/shard_map/ppermute | solution.py:317
  238.8 5.7 %input_grad.11.sum_ref = f32[2,384,1024]{2,1,0:T(8,128)} custom-call(s32[2]{0:T(128)S(1)} %pad_add_fusion.9.at, f32[2,384,1024]{2,1,0:T(8,128)} %input_grad.10.sum_ref, bf16[384,896]{1,0:T(8,128)(2,1)} %collective-permute-done.19.gd_ref.refs_3_, bf16[384,896]{1,0:T(8,128)(2,1)} %collective-permute-done.22.ud_ref.refs_5_, ...), custom_call_target="tpu_custom_call", output_to_operand_aliasing={{}: (1, {})} | custom-call | flops 1409286144 | bytes 6815744 | tf_op jit(solution)/shard_map/input_grad/pallas_call | solution.py:168
  244.5 5.7 %input_grad.12.sum_ref = f32[2,384,1024]{2,1,0:T(8,128)} custom-call(s32[2]{0:T(128)S(1)} %pad_add_fusion.8.at, f32[2,384,1024]{2,1,0:T(8,128)} %input_grad.11.sum_ref, bf16[384,896]{1,0:T(8,128)(2,1)} %collective-permute-done.25.gd_ref.refs_2_, bf16[384,896]{1,0:T(8,128)(2,1)} %collective-permute-done.26.ud_ref.refs_4_, ...), custom_call_target="tpu_custom_call", output_to_operand_aliasing={{}: (1, {})} | custom-call | flops 1409286144 | bytes 6815744 | tf_op jit(solution)/shard_map/input_grad/pallas_call | solution.py:168
  250.2 8.4 %weight_grads.4 = (bf16[1024,3584]{1,0:T(8,128)(2,1)}, bf16[1024,3584]{1,0:T(8,128)(2,1)}) custom-call(s32[3]{0:T(128)S(1)} %pad_add_fusion.7.at, bf16[2,1024,384]{2,1,0:T(8,128)(2,1)} %bitcast.101, bf16[2,1024,384]{2,1,0:T(8,128)(2,1)} %bitcast.102, bf16[384,896]{1,0:T(8,128)(2,1)} %collective-permute-done.25.gd_ref.refs_2_, ...), custom_call_target="tpu_custom_call" | custom-call | flops 2818572288 | bytes 6422528 | tf_op jit(solution)/shard_map/weight_grads/pallas_call | solution.py:213
  258.6 6.1 %collective-permute-start.41 = (bf16[896,384]{1,0:T(8,128)(2,1)}, bf16[896,384]{1,0:T(8,128)(2,1)}, u32[]{:S(2)}, u32[]{:S(2)}) collective-permute-start(bf16[896,384]{1,0:T(8,128)(2,1)} %collective-permute-done.38.refs_0_), channel_id=1, source_target_pairs={{0,1},{1,0},{2,3},{3,2},{4,5},{5,4},{6,7},{7,6},{8,9},{9,8},{10,11... | collective-permute-start | bytes 2064392 | tf_op jit(solution)/shard_map/ppermute | solution.py:317
  267.7 5.8 %input_grad.13.sum_ref = f32[2,384,1024]{2,1,0:T(8,128)} custom-call(s32[2]{0:T(128)S(1)} %pad_add_fusion.2.at, f32[2,384,1024]{2,1,0:T(8,128)} %input_grad.12.sum_ref, bf16[384,896]{1,0:T(8,128)(2,1)} %collective-permute-done.20.gd_ref.refs_3_, bf16[384,896]{1,0:T(8,128)(2,1)} %collective-permute-done.27.ud_ref.refs_5_, ...), custom_call_target="tpu_custom_call", output_to_operand_aliasing={{}: (1, {})} | custom-call | flops 1409286144 | bytes 6815744 | tf_op jit(solution)/shard_map/input_grad/pallas_call | solution.py:168
  274.0 5.7 %input_grad.14.sum_ref = f32[2,384,1024]{2,1,0:T(8,128)} custom-call(s32[2]{0:T(128)S(1)} %pad_add_fusion.1.at, f32[2,384,1024]{2,1,0:T(8,128)} %input_grad.13.sum_ref, bf16[384,896]{1,0:T(8,128)(2,1)} %collective-permute-done.28.gd_ref.refs_2_, bf16[384,896]{1,0:T(8,128)(2,1)} %collective-permute-done.29.ud_ref.refs_4_, ...), custom_call_target="tpu_custom_call", output_to_operand_aliasing={{}: (1, {})} | custom-call | flops 1409286144 | bytes 6815744 | tf_op jit(solution)/shard_map/input_grad/pallas_call | solution.py:168
  279.7 8.4 %weight_grads.5 = (bf16[1024,3584]{1,0:T(8,128)(2,1)}, bf16[1024,3584]{1,0:T(8,128)(2,1)}) custom-call(s32[3]{0:T(128)S(1)} %pad_add_fusion.13.at, bf16[2,1024,384]{2,1,0:T(8,128)(2,1)} %bitcast.103, bf16[2,1024,384]{2,1,0:T(8,128)(2,1)} %bitcast.104, ...), custom_call_target="tpu_custom_call", output_to_operand_aliasing={{0}: (9, {}), {1}: (10, {})} | custom-call | flops 2818572288 | bytes 6422528 | tf_op jit(solution)/shard_map/weight_grads/pallas_call | solution.py:213
  288.0 8.4 %weight_grads.6 = (bf16[1024,3584]{1,0:T(8,128)(2,1)}, bf16[1024,3584]{1,0:T(8,128)(2,1)}) custom-call(s32[3]{0:T(128)S(1)} %get-tuple-element.101.at, bf16[2,1024,384]{2,1,0:T(8,128)(2,1)} %bitcast.105, bf16[2,1024,384]{2,1,0:T(8,128)(2,1)} %bitcast.106, ...), custom_call_target="tpu_custom_call", output_to_operand_aliasing={{0}: (9, {}), {1}: (10, {})} | custom-call | flops 2818572288 | bytes 6422528 | tf_op jit(solution)/shard_map/weight_grads/pallas_call | solution.py:213
  296.4 5.3 %input_grad.15 = f32[2,384,1024]{2,1,0:T(8,128)} custom-call(s32[2]{0:T(128)S(1)} %pad_add_fusion.at, f32[2,384,1024]{2,1,0:T(8,128)} %input_grad.14.sum_ref, bf16[384,896]{1,0:T(8,128)(2,1)S(1)} %collective-permute-done.30.gd_ref.refs_3_, bf16[384,896]{1,0:T(8,128)(2,1)S(1)} %collective-permute-done.31.ud_ref.refs_5_, ...), custom_call_target="tpu_custom_call", output_to_operand_aliasing={{}: (1, {})} | custom-call | flops 1409286144 | bytes 6815744 | tf_op jit(solution)/shard_map/input_grad/pallas_call | solution.py:168
  310.8 8.0 %down_grad.2.refs_5_ = bf16[1792,2048]{1,0:T(8,128)(2,1)} custom-call(s32[3]{0:T(128)S(1)} %add_add_fusion.1.at, bf16[896,384]{1,0:T(8,128)(2,1)} %collective-permute-done.38.refs_0_, bf16[896,384]{1,0:T(8,128)(2,1)} %collective-permute-done.41.refs_1_, bf16[2,384,2048]{2,1,0:T(8,128)(2,1)} %bitcast.109, bf16[2,384,2048]{2,1,0:T(8,128)(2,1)} %bitcast.110, ...), custom_call_target="tpu_custom_call" | custom-call | flops 2818572288 | bytes 6815744 | tf_op jit(solution)/shard_map/down_grad/pallas_call | solution.py:254
  323.0 7.8 %down_grad.3 = bf16[1792,2048]{1,0:T(8,128)(2,1)} custom-call(s32[3]{0:T(128)S(1)} %add_add_fusion.at, bf16[896,384]{1,0:T(8,128)(2,1)} %collective-permute-done.39.refs_0_, bf16[896,384]{1,0:T(8,128)(2,1)S(1)} %collective-permute-done.40.refs_1_, bf16[2,384,2048]{2,1,0:T(8,128)(2,1)} %bitcast.111, ...), custom_call_target="tpu_custom_call", output_to_operand_aliasing={{}: (6, {})} | custom-call | flops 2818572288 | bytes 6815744 | tf_op jit(solution)/shard_map/down_grad/pallas_call | solution.py:254
  332.5 6.7 %collective-permute-done.33 = bf16[192,1024]{1,0:T(8,128)(2,1)S(1)} collective-permute-done((bf16[192,1024]{1,0:T(8,128)(2,1)S(1)}, bf16[192,1024]{1,0:T(8,128)(2,1)S(1)}, u32[]{:S(2)}, u32[]{:S(2)}) %collective-permute-start.33) | collective-permute-done | bytes 393248 | tf_op jit(solution)/shard_map/ppermute | solution.py:433
  340.4 7.7 %weight_grads.7 = (bf16[1024,3584]{1,0:T(8,128)(2,1)}, bf16[1024,3584]{1,0:T(8,128)(2,1)}) custom-call(s32[3]{0:T(128)S(1)} %pad_add_fusion.14.at, bf16[2,1024,384]{2,1,0:T(8,128)(2,1)} %bitcast.107, bf16[2,1024,384]{2,1,0:T(8,128)(2,1)} %bitcast.108, ...), custom_call_target="tpu_custom_call", output_to_operand_aliasing={{0}: (9, {}), {1}: (10, {})} | custom-call | flops 2818572288 | bytes 6422528 | tf_op jit(solution)/shard_map/weight_grads/pallas_call | solution.py:213
  (175 shorter events, 94.6 us)
Async XLA Ops:
  11.0 37.1 %collective-permute-start = (bf16[384,896]{1,0:T(8,128)(2,1)}, bf16[384,896]{1,0:T(8,128)(2,1)S(1)}, u32[]{:S(2)}, u32[]{:S(2)}) collective-permute-start(bf16[384,896]{1,0:T(8,128)(2,1)} %get-tuple-element.52), channel_id=1, source_target_pairs={{0,8},{8,16},{16,24},{24,28},{28,20},{20,12},{12,4},{4,0},{1,9},{9... | collective-permute-start | bytes 2064392 | tf_op jit(solution)/shard_map/ppermute | solution.py:309
  18.1 30.1 %collective-permute-start.1 = (bf16[384,896]{1,0:T(8,128)(2,1)}, bf16[384,896]{1,0:T(8,128)(2,1)S(1)}, u32[]{:S(2)}, u32[]{:S(2)}) collective-permute-start(bf16[384,896]{1,0:T(8,128)(2,1)} %get-tuple-element.53), channel_id=1, source_target_pairs={{8,0},{16,8},{24,16},{28,24},{20,28},{12,20},{4,12},{0,4},{9,1},{1... | collective-permute-start | bytes 2064392 | tf_op jit(solution)/shard_map/ppermute | solution.py:312
  23.7 26.9 %collective-permute-start.5 = (bf16[384,896]{1,0:T(8,128)(2,1)}, bf16[384,896]{1,0:T(8,128)(2,1)}, u32[]{:S(2)}, u32[]{:S(2)}) collective-permute-start(bf16[384,896]{1,0:T(8,128)(2,1)} %get-tuple-element.57), channel_id=1, source_target_pairs={{8,0},{16,8},{24,16},{28,24},{20,28},{12,20},{4,12},{0,4},{9,1},{1... | collective-permute-start | bytes 2064392 | tf_op jit(solution)/shard_map/ppermute | solution.py:312
  29.2 22.8 %collective-permute-start.8 = (bf16[384,896]{1,0:T(8,128)(2,1)}, bf16[384,896]{1,0:T(8,128)(2,1)}, u32[]{:S(2)}, u32[]{:S(2)}) collective-permute-start(bf16[384,896]{1,0:T(8,128)(2,1)} %get-tuple-element.61), channel_id=1, source_target_pairs={{0,8},{8,16},{16,24},{24,28},{28,20},{20,12},{12,4},{4,0},{1,9},{9... | collective-permute-start | bytes 2064392 | tf_op jit(solution)/shard_map/ppermute | solution.py:309
  49.2 21.7 %collective-permute-start.2 = (bf16[384,896]{1,0:T(8,128)(2,1)}, bf16[384,896]{1,0:T(8,128)(2,1)S(1)}, u32[]{:S(2)}, u32[]{:S(2)}) collective-permute-start(bf16[384,896]{1,0:T(8,128)(2,1)} %add_convert_fusion.9), channel_id=1, source_target_pairs={{0,8},{8,16},{16,24},{24,28},{28,20},{20,12},{12,4},{4,0},{1,9},{9... | collective-permute-start | bytes 2064392 | tf_op jit(solution)/shard_map/ppermute | solution.py:309
  51.7 19.4 %collective-permute-start.6 = (bf16[384,896]{1,0:T(8,128)(2,1)S(1)}, bf16[384,896]{1,0:T(8,128)(2,1)S(1)}, u32[]{:S(2)}, u32[]{:S(2)}) collective-permute-start(bf16[384,896]{1,0:T(8,128)(2,1)S(1)} %add_convert_fusion.6), channel_id=1, source_target_pairs={{8,0},{16,8},{24,16},{28,24},{20,28},{12,20},{4,12},{0,4},{9,1},{1... | collective-permute-start | bytes 2064392 | tf_op jit(solution)/shard_map/ppermute | solution.py:312
  54.0 30.8 %collective-permute-start.9 = (bf16[384,896]{1,0:T(8,128)(2,1)}, bf16[384,896]{1,0:T(8,128)(2,1)S(1)}, u32[]{:S(2)}, u32[]{:S(2)}) collective-permute-start(bf16[384,896]{1,0:T(8,128)(2,1)} %add_convert_fusion.4), channel_id=1, source_target_pairs={{0,8},{8,16},{16,24},{24,28},{28,20},{20,12},{12,4},{4,0},{1,9},{9... | collective-permute-start | bytes 2064392 | tf_op jit(solution)/shard_map/ppermute | solution.py:309
  56.4 25.2 %collective-permute-start.11 = (bf16[384,896]{1,0:T(8,128)(2,1)}, bf16[384,896]{1,0:T(8,128)(2,1)}, u32[]{:S(2)}, u32[]{:S(2)}) collective-permute-start(bf16[384,896]{1,0:T(8,128)(2,1)} %add_convert_fusion.2), channel_id=1, source_target_pairs={{8,0},{16,8},{24,16},{28,24},{20,28},{12,20},{4,12},{0,4},{9,1},{1... | collective-permute-start | bytes 2064392 | tf_op jit(solution)/shard_map/ppermute | solution.py:312
  71.2 22.9 %collective-permute-start.3 = (bf16[384,896]{1,0:T(8,128)(2,1)S(1)}, bf16[384,896]{1,0:T(8,128)(2,1)S(1)}, u32[]{:S(2)}, u32[]{:S(2)}) collective-permute-start(bf16[384,896]{1,0:T(8,128)(2,1)S(1)} %add_convert_fusion.8), channel_id=1, source_target_pairs={{0,8},{8,16},{16,24},{24,28},{28,20},{20,12},{12,4},{4,0},{1,9},{9... | collective-permute-start | bytes 2064392 | tf_op jit(solution)/shard_map/ppermute | solution.py:309
  81.5 32.4 %collective-permute-start.7 = (bf16[384,896]{1,0:T(8,128)(2,1)S(1)}, bf16[384,896]{1,0:T(8,128)(2,1)S(1)}, u32[]{:S(2)}, u32[]{:S(2)}) collective-permute-start(bf16[384,896]{1,0:T(8,128)(2,1)S(1)} %add_convert_fusion.5), channel_id=1, source_target_pairs={{8,0},{16,8},{24,16},{28,24},{20,28},{12,20},{4,12},{0,4},{9,1},{1... | collective-permute-start | bytes 2064392 | tf_op jit(solution)/shard_map/ppermute | solution.py:312
  82.9 27.3 %collective-permute-start.12 = (bf16[384,896]{1,0:T(8,128)(2,1)S(1)}, bf16[384,896]{1,0:T(8,128)(2,1)S(1)}, u32[]{:S(2)}, u32[]{:S(2)}) collective-permute-start(bf16[384,896]{1,0:T(8,128)(2,1)S(1)} %add_convert_fusion.1), channel_id=1, source_target_pairs={{8,0},{16,8},{24,16},{28,24},{20,28},{12,20},{4,12},{0,4},{9,1},{1... | collective-permute-start | bytes 2064392 | tf_op jit(solution)/shard_map/ppermute | solution.py:312
  83.7 26.9 %collective-permute-start.16 = (bf16[1,384,896]{2,1,0:T(8,128)(2,1)S(1)}, bf16[1,384,896]{2,1,0:T(8,128)(2,1)S(1)}, u32[]{:S(2)}, u32[]{:S(2)}) collective-permute-start(bf16[1,384,896]{2,1,0:T(8,128)(2,1)S(1)} %fusion.3), channel_id=1, source_target_pairs={{0,2},{1,3},{2,0},{3,1},{4,6},{5,7},{6,4},{7,5},{8,10},{9,11},{10,... | collective-permute-start | bytes 2064392 | tf_op jit(solution)/shard_map/ppermute | solution.py:317
  85.0 28.8 %collective-permute-start.10 = (bf16[384,896]{1,0:T(8,128)(2,1)S(1)}, bf16[384,896]{1,0:T(8,128)(2,1)S(1)}, u32[]{:S(2)}, u32[]{:S(2)}) collective-permute-start(bf16[384,896]{1,0:T(8,128)(2,1)S(1)} %add_convert_fusion.3), channel_id=1, source_target_pairs={{0,8},{8,16},{16,24},{24,28},{28,20},{20,12},{12,4},{4,0},{1,9},{9... | collective-permute-start | bytes 2064392 | tf_op jit(solution)/shard_map/ppermute | solution.py:309
  94.2 29.3 %collective-permute-start.4 = (bf16[384,896]{1,0:T(8,128)(2,1)S(1)}, bf16[384,896]{1,0:T(8,128)(2,1)S(1)}, u32[]{:S(2)}, u32[]{:S(2)}) collective-permute-start(bf16[384,896]{1,0:T(8,128)(2,1)S(1)} %add_convert_fusion.7), channel_id=1, source_target_pairs={{0,8},{8,16},{16,24},{24,28},{28,20},{20,12},{12,4},{4,0},{1,9},{9... | collective-permute-start | bytes 2064392 | tf_op jit(solution)/shard_map/ppermute | solution.py:309
  131.5 37.7 %collective-permute-start.21 = (bf16[384,896]{1,0:T(8,128)(2,1)}, bf16[384,896]{1,0:T(8,128)(2,1)}, u32[]{:S(2)}, u32[]{:S(2)}) collective-permute-start(bf16[384,896]{1,0:T(8,128)(2,1)} %get-tuple-element.71.ud_ref.refs_4_), channel_id=1, source_target_pairs={{0,8},{8,16},{16,24},{24,28},{28,20},{20,12},{12,4},{4,0},{1,9},{9... | collective-permute-start | bytes 2064392 | tf_op jit(solution)/shard_map/ppermute | solution.py:309
  149.1 34.8 %collective-permute-start.18 = (bf16[384,896]{1,0:T(8,128)(2,1)S(1)}, bf16[384,896]{1,0:T(8,128)(2,1)}, u32[]{:S(2)}, u32[]{:S(2)}) collective-permute-start(bf16[384,896]{1,0:T(8,128)(2,1)S(1)} %get-tuple-element.70.gd_ref.refs_2_), channel_id=1, source_target_pairs={{0,8},{8,16},{16,24},{24,28},{28,20},{20,12},{12,4},{4,0},{1,9},{9... | collective-permute-start | bytes 2064392 | tf_op jit(solution)/shard_map/ppermute | solution.py:309
  153.4 30.5 %collective-permute-start.24 = (bf16[384,896]{1,0:T(8,128)(2,1)}, bf16[384,896]{1,0:T(8,128)(2,1)}, u32[]{:S(2)}, u32[]{:S(2)}) collective-permute-start(bf16[384,896]{1,0:T(8,128)(2,1)} %get-tuple-element.71.ud_ref.refs_4_), channel_id=1, source_target_pairs={{8,0},{16,8},{24,16},{28,24},{20,28},{12,20},{4,12},{0,4},{9,1},{1... | collective-permute-start | bytes 2064392 | tf_op jit(solution)/shard_map/ppermute | solution.py:312
  153.4 32.1 %collective-permute-start.23 = (bf16[384,896]{1,0:T(8,128)(2,1)S(1)}, bf16[384,896]{1,0:T(8,128)(2,1)}, u32[]{:S(2)}, u32[]{:S(2)}) collective-permute-start(bf16[384,896]{1,0:T(8,128)(2,1)S(1)} %get-tuple-element.70.gd_ref.refs_2_), channel_id=1, source_target_pairs={{8,0},{16,8},{24,16},{28,24},{20,28},{12,20},{4,12},{0,4},{9,1},{1... | collective-permute-start | bytes 2064392 | tf_op jit(solution)/shard_map/ppermute | solution.py:312
  169.2 33.9 %collective-permute-start.22 = (bf16[384,896]{1,0:T(8,128)(2,1)}, bf16[384,896]{1,0:T(8,128)(2,1)}, u32[]{:S(2)}, u32[]{:S(2)}) collective-permute-start(bf16[384,896]{1,0:T(8,128)(2,1)} %collective-permute-done.21.ud_ref.refs_5_), channel_id=1, source_target_pairs={{0,8},{8,16},{16,24},{24,28},{28,20},{20,12},{12,4},{4,0},{1,9},{9... | collective-permute-start | bytes 2064392 | tf_op jit(solution)/shard_map/ppermute | solution.py:309
  183.9 29.5 %collective-permute-start.19 = (bf16[384,896]{1,0:T(8,128)(2,1)}, bf16[384,896]{1,0:T(8,128)(2,1)}, u32[]{:S(2)}, u32[]{:S(2)}) collective-permute-start(bf16[384,896]{1,0:T(8,128)(2,1)} %collective-permute-done.18.gd_ref.refs_3_), channel_id=1, source_target_pairs={{0,8},{8,16},{16,24},{24,28},{28,20},{20,12},{12,4},{4,0},{1,9},{9... | collective-permute-start | bytes 2064392 | tf_op jit(solution)/shard_map/ppermute | solution.py:309
  183.9 29.5 %collective-permute-start.26 = (bf16[384,896]{1,0:T(8,128)(2,1)}, bf16[384,896]{1,0:T(8,128)(2,1)}, u32[]{:S(2)}, u32[]{:S(2)}) collective-permute-start(bf16[384,896]{1,0:T(8,128)(2,1)} %collective-permute-done.24.ud_ref.refs_4_), channel_id=1, source_target_pairs={{8,0},{16,8},{24,16},{28,24},{20,28},{12,20},{4,12},{0,4},{9,1},{1... | collective-permute-start | bytes 2064392 | tf_op jit(solution)/shard_map/ppermute | solution.py:312
  185.5 31.9 %collective-permute-start.25 = (bf16[384,896]{1,0:T(8,128)(2,1)}, bf16[384,896]{1,0:T(8,128)(2,1)}, u32[]{:S(2)}, u32[]{:S(2)}) collective-permute-start(bf16[384,896]{1,0:T(8,128)(2,1)} %collective-permute-done.23.gd_ref.refs_2_), channel_id=1, source_target_pairs={{8,0},{16,8},{24,16},{28,24},{20,28},{12,20},{4,12},{0,4},{9,1},{1... | collective-permute-start | bytes 2064392 | tf_op jit(solution)/shard_map/ppermute | solution.py:312
  187.0 36.2 %collective-permute-start.38 = (bf16[896,384]{1,0:T(8,128)(2,1)}, bf16[896,384]{1,0:T(8,128)(2,1)}, u32[]{:S(2)}, u32[]{:S(2)}) collective-permute-start(bf16[896,384]{1,0:T(8,128)(2,1)} %get-tuple-element.91), channel_id=1, source_target_pairs={{0,0},{28,1},{8,2},{20,3},{16,4},{12,5},{24,6},{4,7},{17,8},{13,9}... | collective-permute-start | bytes 2064392 | tf_op jit(solution)/shard_map/ppermute | solution.py:367
  203.0 61.7 %collective-permute-start.27 = (bf16[384,896]{1,0:T(8,128)(2,1)}, bf16[384,896]{1,0:T(8,128)(2,1)}, u32[]{:S(2)}, u32[]{:S(2)}) collective-permute-start(bf16[384,896]{1,0:T(8,128)(2,1)} %collective-permute-done.22.ud_ref.refs_5_), channel_id=1, source_target_pairs={{0,8},{8,16},{16,24},{24,28},{28,20},{20,12},{12,4},{4,0},{1,9},{9... | collective-permute-start | bytes 2064392 | tf_op jit(solution)/shard_map/ppermute | solution.py:309
  213.4 45.2 %collective-permute-start.20 = (bf16[384,896]{1,0:T(8,128)(2,1)}, bf16[384,896]{1,0:T(8,128)(2,1)}, u32[]{:S(2)}, u32[]{:S(2)}) collective-permute-start(bf16[384,896]{1,0:T(8,128)(2,1)} %collective-permute-done.19.gd_ref.refs_3_), channel_id=1, source_target_pairs={{0,8},{8,16},{16,24},{24,28},{28,20},{20,12},{12,4},{4,0},{1,9},{9... | collective-permute-start | bytes 2064392 | tf_op jit(solution)/shard_map/ppermute | solution.py:309
  213.4 54.3 %collective-permute-start.29 = (bf16[384,896]{1,0:T(8,128)(2,1)}, bf16[384,896]{1,0:T(8,128)(2,1)}, u32[]{:S(2)}, u32[]{:S(2)}) collective-permute-start(bf16[384,896]{1,0:T(8,128)(2,1)} %collective-permute-done.26.ud_ref.refs_4_), channel_id=1, source_target_pairs={{8,0},{16,8},{24,16},{28,24},{20,28},{12,20},{4,12},{0,4},{9,1},{1... | collective-permute-start | bytes 2064392 | tf_op jit(solution)/shard_map/ppermute | solution.py:312
  217.4 56.6 %collective-permute-start.28 = (bf16[384,896]{1,0:T(8,128)(2,1)}, bf16[384,896]{1,0:T(8,128)(2,1)}, u32[]{:S(2)}, u32[]{:S(2)}) collective-permute-start(bf16[384,896]{1,0:T(8,128)(2,1)} %collective-permute-done.25.gd_ref.refs_2_), channel_id=1, source_target_pairs={{8,0},{16,8},{24,16},{28,24},{20,28},{12,20},{4,12},{0,4},{9,1},{1... | collective-permute-start | bytes 2064392 | tf_op jit(solution)/shard_map/ppermute | solution.py:312
  223.2 87.1 %collective-permute-start.39 = (bf16[896,384]{1,0:T(8,128)(2,1)}, bf16[896,384]{1,0:T(8,128)(2,1)}, u32[]{:S(2)}, u32[]{:S(2)}) collective-permute-start(bf16[896,384]{1,0:T(8,128)(2,1)} %collective-permute-done.38.refs_0_), channel_id=1, source_target_pairs={{0,2},{1,3},{2,0},{3,1},{4,6},{5,7},{6,4},{7,5},{8,10},{9,11},{10,... | collective-permute-start | bytes 2064392 | tf_op jit(solution)/shard_map/ppermute | solution.py:317
  258.6 52.2 %collective-permute-start.41 = (bf16[896,384]{1,0:T(8,128)(2,1)}, bf16[896,384]{1,0:T(8,128)(2,1)}, u32[]{:S(2)}, u32[]{:S(2)}) collective-permute-start(bf16[896,384]{1,0:T(8,128)(2,1)} %collective-permute-done.38.refs_0_), channel_id=1, source_target_pairs={{0,1},{1,0},{2,3},{3,2},{4,5},{5,4},{6,7},{7,6},{8,9},{9,8},{10,11... | collective-permute-start | bytes 2064392 | tf_op jit(solution)/shard_map/ppermute | solution.py:317
  264.7 31.7 %collective-permute-start.30 = (bf16[384,896]{1,0:T(8,128)(2,1)}, bf16[384,896]{1,0:T(8,128)(2,1)S(1)}, u32[]{:S(2)}, u32[]{:S(2)}) collective-permute-start(bf16[384,896]{1,0:T(8,128)(2,1)} %collective-permute-done.20.gd_ref.refs_3_), channel_id=1, source_target_pairs={{0,8},{8,16},{16,24},{24,28},{28,20},{20,12},{12,4},{4,0},{1,9},{9... | collective-permute-start | bytes 2064392 | tf_op jit(solution)/shard_map/ppermute | solution.py:309
  267.7 28.7 %collective-permute-start.31 = (bf16[384,896]{1,0:T(8,128)(2,1)}, bf16[384,896]{1,0:T(8,128)(2,1)S(1)}, u32[]{:S(2)}, u32[]{:S(2)}) collective-permute-start(bf16[384,896]{1,0:T(8,128)(2,1)} %collective-permute-done.29.ud_ref.refs_4_), channel_id=1, source_target_pairs={{8,0},{16,8},{24,16},{28,24},{20,28},{12,20},{4,12},{0,4},{9,1},{1... | collective-permute-start | bytes 2064392 | tf_op jit(solution)/shard_map/ppermute | solution.py:312
  321.9 17.3 %collective-permute-start.33 = (bf16[192,1024]{1,0:T(8,128)(2,1)S(1)}, bf16[192,1024]{1,0:T(8,128)(2,1)S(1)}, u32[]{:S(2)}, u32[]{:S(2)}) collective-permute-start(bf16[192,1024]{1,0:T(8,128)(2,1)S(1)} %fusion.2), channel_id=1, source_target_pairs={{0,2},{1,3},{2,0},{3,1},{4,6},{5,7},{6,4},{7,5},{8,10},{9,11},{10,... | collective-permute-start | bytes 1179656 | tf_op jit(solution)/shard_map/ppermute | solution.py:433
  (32 other events, 503.3 us)
